TPU v7x, 256 devices: a whole 4x4x8 slice. The times are simulated.
256 devices in a mesh: section: 2 (over y_hi), fsdp: 64 (over y_lo, x, z), mp: 2 (over core).
Axes of the slice: x: 4, y: 4 (y_hi: 2, y_lo: 2; y = y_hi * 2 + y_lo), z: 8, core: 2. Of those that a mesh axis runs over, the one named last changes fastest.
Arguments:
- section_rows: bfloat16 [2, 8192, 4096], P('section', 'fsdp', 'mp'), may hold values from -6 to 6
- norm_gains: bfloat16 [2, 4096], P('section', 'mp'), may hold values from 0.5 to 1.5
- proj_weights: bfloat16 [2, 4096, 2, 2048], P('section', 'fsdp', None, 'mp'), may hold values from -1 to 1
- section_cotan: bfloat16 [2, 8192, 4096], P('section', 'fsdp', 'mp'), may hold values from -6 to 6
- enc_lengths: int32 [64, 2], P('fsdp'), may hold values from 1 to 64, 96 in all within a row
- dec_segments: int32 [64, 128], P('fsdp'), may hold values from 0 to 1, never falling along the last dimension, each value on 1 to 127 neighbouring positions
Outputs:
- section_grads: float32 [2, 8192, 4096], P('section', 'fsdp', 'mp')
Inputs may be any that keep to these rules, and one draw needn't show every extreme that they name: `enc_lengths`: each row of an fsdp index sums to 96. `dec_segments`: never falls along a row; each slot owns 1 to 127 rows.
All inputs are finite; a program needn't handle non-finite values.
Results may differ from a plain program's by a relative error of at most 0.024.
Values may be sent and summed in bfloat16 or wider, within the bound.
No kernel may reach another device: no remote copies, remote signals or barrier semaphores. Data moves between devices by JAX's collectives and lax.ppermute only.
A program may use at most 64 MiB of HBM per device.

v0:
```python
import jax
import jax.numpy as jnp
from jax import lax
from jax.sharding import PartitionSpec as P

HD = 64
ELEN = 64


EPS = 1e-06


def from_behind(block, axis, distance):
    devices = range(lax.axis_size(axis))
    route = [(i - distance, i) for i in devices if i - distance in devices]
    return lax.ppermute(block, axis, route)


def attend(query, output_grad, keys, values, segment, lengths):
    row_count = query.shape[0]
    block_rows = min(row_count, 512)
    block_count = row_count // block_rows
    head_count = query.shape[1] // HD
    key_index = jnp.arange(row_count)
    key_seq = key_index // ELEN
    slot_ids = jnp.arange(lengths.shape[0])
    key_len = jnp.sum(jnp.where(key_seq[:, None] == slot_ids[None, :], lengths[None, :], 0), 1)
    key_valid = key_index % ELEN < key_len
    key_heads = keys.reshape(row_count, head_count, HD)
    value_heads = values.reshape(row_count, head_count, HD)
    query_blocks = query.reshape(block_count, block_rows, head_count, HD)
    grad_blocks = output_grad.reshape(block_count, block_rows, head_count, HD)
    segment_blocks = segment.reshape(block_count, block_rows)

    def advance(running, pieces):
        query_part, grad_part, segment_part = pieces
        allowed = (segment_part[:, None] == key_seq[None, :]) & key_valid[None, :]
        scores = jnp.einsum(
            "qhd,khd->hqk", query_part, key_heads, preferred_element_type=jnp.float32
        )
        scores = jnp.where(allowed[None], scores, -1e30)
        row_peak = jnp.max(scores, -1, keepdims=True)
        exponent = jnp.exp(scores - row_peak)
        softmax_rows = exponent / jnp.sum(exponent, -1, keepdims=True)
        soft_low = softmax_rows.astype(jnp.bfloat16)
        attended = jnp.einsum(
            "hqk,khd->qhd", soft_low, value_heads, preferred_element_type=jnp.float32
        ).astype(jnp.bfloat16)
        row_delta = jnp.sum(grad_part.astype(jnp.float32) * attended.astype(jnp.float32), -1)
        prob_grad = jnp.einsum(
            "qhd,khd->hqk", grad_part, value_heads, preferred_element_type=jnp.float32
        )
        score_grad = (softmax_rows * (prob_grad - jnp.transpose(row_delta)[:, :, None])).astype(
            jnp.bfloat16
        )
        query_grad = jnp.einsum(
            "hqk,khd->qhd", score_grad, key_heads, preferred_element_type=jnp.float32
        ).astype(jnp.bfloat16)
        key_sum = running[0] + jnp.einsum(
            "hqk,qhd->khd", score_grad, query_part, preferred_element_type=jnp.float32
        )
        value_sum = running[1] + jnp.einsum(
            "hqk,qhd->khd", soft_low, grad_part, preferred_element_type=jnp.float32
        )
        return ((key_sum, value_sum), query_grad)

    empty_grad = jnp.zeros((row_count, head_count, HD), jnp.float32)
    (key_sum, value_sum), query_grads = lax.scan(
        advance, (empty_grad, empty_grad), (query_blocks, grad_blocks, segment_blocks)
    )
    flat = (row_count, head_count * HD)
    key_grad = key_sum.astype(jnp.bfloat16).reshape(flat)
    value_grad = value_sum.astype(jnp.bfloat16).reshape(flat)
    return (query_grads.reshape(flat), jnp.stack((key_grad, value_grad), 1))


def on_device(section_rows, norm_gains, proj_weights, section_cotan, enc_lengths, dec_segments):
    half_width = section_rows.shape[2]
    full_rows, full_cotan, full_gain = (
        lax.all_gather(section_rows[0], "mp", axis=1, tiled=True),
        lax.all_gather(section_cotan[0], "mp", axis=1, tiled=True),
        lax.all_gather(norm_gains, "mp", axis=1, tiled=True),
    )
    at_encoder = lax.axis_index("section") == 0
    gain_row = full_gain[0].astype(jnp.float32)
    wide_rows = full_rows.astype(jnp.float32)
    inverse = lax.rsqrt(jnp.mean(wide_rows * wide_rows, -1, keepdims=True) + EPS)
    normed = (wide_rows * inverse * gain_row).astype(jnp.bfloat16)
    weight_tensors = lax.all_gather(proj_weights[0], "fsdp", axis=0, tiled=True)
    second_left = jnp.where(at_encoder, normed, full_cotan)
    first_proj = jnp.dot(normed, weight_tensors[:, 0], preferred_element_type=jnp.float32).astype(
        jnp.bfloat16
    )
    second_projection = jnp.dot(
        second_left, weight_tensors[:, 1], preferred_element_type=jnp.float32
    ).astype(jnp.bfloat16)
    packed = jnp.stack((first_proj, second_projection), 1)
    memory = from_behind(packed, "section", 1)

    def decoder_side(operand_list):
        query, output_grad, keys, values, segment, lengths = operand_list
        return attend(query, output_grad, keys, values, segment, lengths)

    def encoder_side(operand_list):
        query = operand_list[0]
        return (jnp.zeros_like(query), jnp.zeros((query.shape[0], 2, query.shape[1]), jnp.bfloat16))

    query_grad, encoder_memory_grad = lax.cond(
        at_encoder,
        encoder_side,
        decoder_side,
        (
            first_proj,
            second_projection,
            memory[:, 0],
            memory[:, 1],
            dec_segments[0],
            enc_lengths[0],
        ),
    )
    returned = from_behind(encoder_memory_grad, "section", -1)

    def encoder_back(operand_list):
        return jnp.einsum(
            "vob,kob->vk", operand_list[0], weight_tensors, preferred_element_type=jnp.float32
        )

    def decoder_back(operand_list):
        return jnp.dot(operand_list[1], weight_tensors[:, 0].T, preferred_element_type=jnp.float32)

    partial_grad = lax.cond(at_encoder, encoder_back, decoder_back, (returned, query_grad))
    own_start = lax.axis_index("mp") * half_width
    own_cotan = section_cotan[0].astype(jnp.float32)
    summed = lax.psum(partial_grad, "mp")
    upstream = summed + jnp.where(at_encoder, full_cotan.astype(jnp.float32), 0.0)
    gain_grad = gain_row * upstream
    row_dot = jnp.mean(wide_rows * gain_grad, -1, keepdims=True)
    whole_grad = inverse * gain_grad - wide_rows * inverse**3 * row_dot
    own_grad = lax.dynamic_slice_in_dim(whole_grad, own_start, half_width, 1)
    result = own_grad + jnp.where(at_encoder, 0.0, own_cotan)
    return result[None]


def solution(mesh):
    return jax.shard_map(
        on_device,
        mesh=mesh,
        in_specs=(
            P("section", "fsdp", "mp"),
            P("section", "mp"),
            P("section", "fsdp", None, "mp"),
            P("section", "fsdp", "mp"),
            P("fsdp", None),
            P("fsdp", None),
        ),
        out_specs=P("section", "fsdp", "mp"),
        check_vma=False,
    )
```

profile of v0, /device:TPU:1, one launch (start us, length us, event | category | flops | bytes accessed | tf_op | source)
XLA Modules:
  0.0 476.9 jit_solution(9354550927795335171)
XLA Ops:
  6.5 0.7 all-gather.7.cloned.1.call-update
  7.3 0.0 all-gather.9.cloned.1.call-start
  7.3 1.7 copy.39
  9.0 0.0 all-gather.9.cloned.1.call-update
  9.0 0.0 all-gather.11.cloned.1.call-start
  9.1 0.7 all-gather.11.cloned.1.call-update
  9.8 0.0 all-reduce.2.cloned.1.call-start
  9.8 4.9 %all_gather.13 = bf16[1,4096]{1,0:T(2,128)(2,1)S(1)} all-gather(bf16[1,2048]{1,0:T(2,128)(2,1)} %param.11), channel_id=1, replica_groups=mesh['section'=2,'fsdp'=64,'mp'=2] {'mp'}, dimensions={1}, use_global_device_ids=true | all-gather | bytes 12288 | tf_op jit(solution)/shard_map/all_gather | solution.py:82
  14.8 13.3 %all-gather.7.cloned.1.call-done = bf16[1,128,4096]{2,1,0:T(8,128)(2,1)} async-done(((bf16[1,128,2048]{2,1,0:T(8,128)(2,1)}), bf16[1,128,4096]{2,1,0:T(8,128)(2,1)}) %all-gather.7.cloned.1.call-update) | async-done | bytes 1048592 | tf_op jit(solution)/shard_map/all_gather | solution.py:80
  28.1 1.5 multiply_reduce_fusion.1
  29.6 292.1 %all-gather.9.cloned.1.call-done = bf16[1,4096,2,1024]{3,1,2,0:T(8,128)(2,1)} async-done(((bf16[1,64,2,1024]{3,1,2,0:T(8,128)(2,1)}), bf16[1,4096,2,1024]{3,1,2,0:T(8,128)(2,1)}) %all-gather.9.cloned.1.call-update) | async-done | bytes 16777232 | tf_op jit(solution)/shard_map/all_gather | solution.py:89
  321.7 5.1 %fusion.21 = bf16[128,1024]{1,0:T(8,128)(2,1)S(1)} fusion(bf16[4096,2,1024]{2,0,1:T(8,128)(2,1)} %bitcast.73, bf16[1,128,4096]{2,1,0:T(8,128)(2,1)} %all-gather.7.cloned.1.call-done, f32[4096]{0:T(1024)S(1)} %bitcast.91, f32[128]{0:T(128)S(1)} %get-tuple-element.110), kind=kOutput, calls=%fused_computation.41 | convolution fusion | flops 1075970048 | bytes 9716224 | tf_op jit(solution)/shard_map/dot_general | solution.py:91
  326.8 0.0 copy-start.4
  326.8 50.4 %all-gather.11.cloned.1.call-done = bf16[1,128,4096]{2,1,0:T(8,128)(2,1)} async-done(((bf16[1,128,2048]{2,1,0:T(8,128)(2,1)}), bf16[1,128,4096]{2,1,0:T(8,128)(2,1)}) %all-gather.11.cloned.1.call-update) | async-done | bytes 1048592 | tf_op jit(solution)/shard_map/all_gather | solution.py:81
  377.3 5.0 %fusion.22 = bf16[128,1024]{1,0:T(8,128)(2,1)S(1)} fusion(bf16[4096,2,1024]{2,0,1:T(8,128)(2,1)} %bitcast.74, bf16[1,128,4096]{2,1,0:T(8,128)(2,1)} %all-gather.11.cloned.1.call-done, pred[]{:T(512)S(6)} %eq.44, bf16[1,128,4096]{2,1,0:T(8,128)(2,1)S(1)} %copy-done, f32[4096]{0:T(1024)S(1)} %bitcast.92, f32[128]{0:T(128)S(1)} %get-tuple-element.110), kind=kOutput, calls=%fused_computation.42 | convolution fusion | flops 1076494336 | bytes 10764801 | tf_op jit(solution)/shard_map/dot_general | solution.py:94
  382.3 0.1 pad_maximum_fusion.1
  382.3 4.4 collective-permute-start
  386.8 11.1 %collective-permute-done = bf16[128,2,1024]{2,0,1:T(8,128)(2,1)S(1)} collective-permute-done((bf16[128,2,1024]{2,0,1:T(8,128)(2,1)S(1)}, bf16[128,2,1024]{2,0,1:T(8,128)(2,1)S(1)}, u32[]{:S(2)}, u32[]{:S(2)}) %collective-permute-start) | collective-permute-done | bytes 524320 | tf_op jit(solution)/shard_map/ppermute | solution.py:16
  397.8 0.1 conditional.2
  397.9 0.1 broadcast.138
  398.0 0.2 copy.44
  398.2 1.3 collective-permute-start.1
  399.5 20.7 %collective-permute-done.1 = bf16[128,2,1024]{2,0,1:T(8,128)(2,1)S(1)} collective-permute-done((bf16[128,2,1024]{2,0,1:T(8,128)(2,1)S(1)}, bf16[128,2,1024]{2,0,1:T(8,128)(2,1)S(1)}, u32[]{:S(2)}, u32[]{:S(2)}) %collective-permute-start.1) | collective-permute-done | bytes 524320 | tf_op jit(solution)/shard_map/ppermute | solution.py:16
  420.2 12.4 %conditional.3 = (f32[128,4096]{1,0:T(8,128)S(1)}) conditional(s32[]{:T(128)} %convert_element_type.68, (bf16[4096,2,1024]{2,0,1:T(8,128)(2,1)}, bf16[128,1024]{0,1:T(8,128)(2,1)S(1)}) %tuple.46, (bf16[128,2,1024]{2,0,1:T(8,128)(2,1)S(1)}, bf16[4096,2,1024]{2,0,1:T(8,128)(2,1)}) %tuple.47), branch_computations={%region_7.8_spmd, %region_8.9_spmd} | conditional | flops 2147483648 | bytes 21495844 | solution.py:131
  420.2 0.8 copy-done.3
  421.0 11.6 %convolution_bitcast_fusion = f32[128,4096]{1,0:T(8,128)S(1)} fusion(bf16[128,2,1024]{2,0,1:T(8,128)(2,1)} %copy-done.3, bf16[4096,2,1024]{2,0,1:T(8,128)(2,1)} %get-tuple-element.70), kind=kOutput, calls=%fused_computation.32 | convolution fusion | flops 2147483648 | bytes 19398656 | tf_op jit(solution)/shard_map/cond/branch_1_fun/vob,kob->vk/dot_general | solution.py:124
  432.6 1.3 copy-done.2
  433.9 0.0 all-reduce.2.cloned.1.call-update
  433.9 0.2 bitcast_convert_fusion
  434.1 32.5 %all-reduce.2.cloned.1.call-done = f32[128,4096]{1,0:T(8,128)} async-done(((f32[128,4096]{1,0:T(8,128)}), f32[128,4096]{1,0:T(8,128)}) %all-reduce.2.cloned.1.call-update) | async-done | bytes 2097168 | tf_op jit(solution)/shard_map/psum | solution.py:134
  466.6 2.5 multiply_reduce_fusion
  469.1 1.3 fusion.25
  (14 shorter events, 0.1 us)
Async XLA Ops:
  6.5 21.6 %all-gather.7.cloned.1.call-start = ((), (), s32[]{:S(2)}) async-start(), calls=%async_computation.1 | async-start | bytes 1572864 | tf_op jit(solution)/shard_map/all_gather | solution.py:80
  7.3 314.5 %all-gather.9.cloned.1.call-start = ((), (), s32[]{:S(2)}) async-start(), calls=%async_computation.2 | async-start | bytes 17039360 | tf_op jit(solution)/shard_map/all_gather | solution.py:89
  9.0 368.2 %all-gather.11.cloned.1.call-start = ((), (), s32[]{:S(2)}) async-start(), calls=%async_computation.3 | async-start | bytes 1572864 | tf_op jit(solution)/shard_map/all_gather | solution.py:81
  9.8 456.8 %all-reduce.2.cloned.1.call-start = ((), (), s32[]{:S(2)}) async-start(), calls=%async_computation | async-start | bytes 4194304 | tf_op jit(solution)/shard_map/psum | solution.py:134
  321.7 55.5 %copy-start = (bf16[1,128,4096]{2,1,0:T(8,128)(2,1)S(1)}, bf16[1,128,4096]{2,1,0:T(8,128)(2,1)}, u32[]{:S(2)}) copy-start(bf16[1,128,4096]{2,1,0:T(8,128)(2,1)} %all-gather.7.cloned.1.call-done) | copy-start | bytes 3145732
  326.8 71.0 %copy-start.4 = (s32[1,128]{1,0:T(1,128)S(1)}, s32[1,128]{1,0:T(1,128)}, u32[]{:S(2)}) copy-start(s32[1,128]{1,0:T(1,128)} %param.15) | copy-start | bytes 1540
  326.8 71.0 %copy-start.5 = (s32[1,2]{1,0:T(1,128)S(1)}, s32[1,2]{1,0:T(1,128)}, u32[]{:S(2)}) copy-start(s32[1,2]{1,0:T(1,128)} %param.14) | copy-start | bytes 28
  382.3 15.5 %collective-permute-start = (bf16[128,2,1024]{2,0,1:T(8,128)(2,1)S(1)}, bf16[128,2,1024]{2,0,1:T(8,128)(2,1)S(1)}, u32[]{:S(2)}, u32[]{:S(2)}) collective-permute-start(bf16[128,2,1024]{2,0,1:T(8,128)(2,1)S(1)} %pad_maximum_fusion.1), channel_id=1, source_target_pairs={{0,128},{1,129},{2,130},{3,131},{4,132},{5,133},{6,134},{7,135},{8... | collective-permute-start | bytes 1572872 | tf_op jit(solution)/shard_map/ppermute | solution.py:16
  398.2 22.0 %collective-permute-start.1 = (bf16[128,2,1024]{2,0,1:T(8,128)(2,1)S(1)}, bf16[128,2,1024]{2,0,1:T(8,128)(2,1)S(1)}, u32[]{:S(2)}, u32[]{:S(2)}) collective-permute-start(bf16[128,2,1024]{2,0,1:T(8,128)(2,1)S(1)} %copy.44), channel_id=1, source_target_pairs={{128,0},{129,1},{130,2},{131,3},{132,4},{133,5},{134,6},{135,7},{1... | collective-permute-start | bytes 1572872 | tf_op jit(solution)/shard_map/ppermute | solution.py:16
  420.2 0.8 copy-start.3
  432.6 1.3 copy-start.2
  466.6 2.5 copy-start.1
Sparse Core Ops, SparseCore 0:
  9.2 18.8 all-gather.6
  29.9 291.7 all-gather.8
  323.5 53.6 all-gather.10
  434.0 32.5 all-reduce.1
where the time goes:
time: 477 us
  waiting for transfers between devices  422 us (88%)
  matrix products  21.7 us (5%)
  between operations  13.3 us (3%)
  starting transfers between devices  5.82 us (1%)
  other arithmetic  5.59 us (1%)
  blocking collectives  4.94 us (1%)
    all_gather x1, waiting for transfers between devices, on_device(): weight_tensors = lax.all_gather(proj_weights[0], 'fsdp', axis=0, tiled=True)  292 us
    all_gather x1, waiting for transfers between devices, on_device(): lax.all_gather(section_cotan[0], 'mp', axis=1, tiled=True)  50.4 us
    psum x1, waiting for transfers between devices, on_device(): summed = lax.psum(partial_grad, 'mp')  32.5 us
    ppermute x2, waiting for transfers between devices, from_behind(): return lax.ppermute(block, axis, route)  31.8 us
    all_gather x1, waiting for transfers between devices, on_device(): lax.all_gather(section_rows[0], 'mp', axis=1, tiled=True)  13.3 us
    dot_general x1, matrix products, encoder_back(): jnp.einsum('vob,kob->vk', operand_list[0], weight_tensors, preferred_elem...  11.6 us
  transfers between devices with their start and end apart: 6, of which 6 were waited for; matrix products, arithmetic and copies ran while one was open for 2% of the time, Pallas kernels for 0%

commit v1 on v0

v1 whole, which is shorter than its diff:
```python
import jax
import jax.numpy as jnp
import numpy as np
from jax import lax
from jax.experimental import pallas as pl
from jax.experimental.pallas import tpu as pltpu
from jax.sharding import Mesh, PartitionSpec as P

HD = 64
ELEN = 64
EPS = 1e-06
BF = jnp.bfloat16
F32 = jnp.float32


def shift(block, axis, distance):
    size = lax.axis_size(axis)
    return lax.ppermute(block, axis, [(i, (i + distance) % size) for i in range(size)])


def dot(left, right, contract):
    return lax.dot_general(left, right, (contract, ((), ())), preferred_element_type=F32)


def attention_kernel(lengths_ref, side_ref, keep_ref, recv_ref, segment_ref, stay_ref, send_ref):
    at_encoder = side_ref[0] == 0
    rows = segment_ref.shape[1]
    key_index = lax.broadcasted_iota(jnp.int32, (rows, rows), 1)
    lane = lax.broadcasted_iota(jnp.int32, (rows, 2 * HD), 1)
    slot = key_index // ELEN
    place = key_index % ELEN
    for block in range(segment_ref.shape[0]):
        pick = pl.ds(block * rows, rows)
        kept = [keep_ref[part, pick, :] for part in range(2)]
        received = [recv_ref[part, pick, :] for part in range(2)]
        query, output_grad = [jnp.where(at_encoder, r, k) for k, r in zip(kept, received)]
        keys, values = [jnp.where(at_encoder, k, r) for k, r in zip(kept, received)]
        key_len = jnp.where(slot == 0, lengths_ref[block, 0], lengths_ref[block, 1])
        allowed = (segment_ref[block] == slot) & (place < key_len)
        sums = None
        for head in range(2):
            mine = lane // HD == head
            query_head = jnp.where(mine, query, 0)
            grad_head = jnp.where(mine, output_grad, 0)
            scores = dot(query_head, keys, ((1,), (1,)))
            scores = jnp.where(allowed, scores, -1e30)
            exponent = jnp.exp(scores - jnp.max(scores, -1, keepdims=True))
            softmax_rows = exponent / jnp.sum(exponent, -1, keepdims=True)
            soft_low = softmax_rows.astype(BF)
            attended = dot(soft_low, values, ((1,), (0,))).astype(BF)
            row_delta = jnp.sum(grad_head.astype(F32) * attended.astype(F32), -1, keepdims=True)
            prob_grad = dot(grad_head, values, ((1,), (1,)))
            score_grad = (softmax_rows * (prob_grad - row_delta)).astype(BF)
            query_grad = dot(score_grad, keys, ((1,), (0,)))
            key_grad = dot(score_grad, query, ((0,), (0,)))
            value_grad = dot(soft_low, output_grad, ((0,), (0,)))
            grads = (query_grad, key_grad, value_grad)
            sums = grads if head == 0 else [jnp.where(mine, g, s) for g, s in zip(grads, sums)]
        query_grad, key_grad, value_grad = [g.astype(BF) for g in sums]
        empty = jnp.zeros_like(query_grad)
        stay_ref[0, pick, :] = jnp.where(at_encoder, key_grad, query_grad)
        stay_ref[1, pick, :] = jnp.where(at_encoder, value_grad, empty)
        send_ref[0, pick, :] = jnp.where(at_encoder, query_grad, key_grad)
        send_ref[1, pick, :] = jnp.where(at_encoder, empty, value_grad)


def attention(lengths, side, keep, recv, segment):
    shape = jax.ShapeDtypeStruct(keep.shape, BF)
    whole = pl.BlockSpec(memory_space=pltpu.VMEM)
    scalars = pl.BlockSpec(memory_space=pltpu.SMEM)
    return pl.pallas_call(
        attention_kernel,
        out_shape=(shape, shape),
        in_specs=[scalars, scalars, whole, whole, whole],
        out_specs=(whole, whole),
        compiler_params=pltpu.CompilerParams(vmem_limit_bytes=32 * 1024 * 1024),
    )(lengths, side, keep, recv, segment)


def gather_weights(weights, own_y, own_z, own_c):
    rows, parts, columns = weights.shape
    x_size, y_size, z_size = (lax.axis_size(a) for a in ("x", "y", "z"))
    slices = weights.reshape(rows, parts, x_size, columns // x_size).transpose(2, 1, 0, 3)
    chunk = lax.all_to_all(slices, "x", 0, 0, tiled=True)
    chunk = chunk.transpose(1, 0, 2, 3)
    full = jnp.zeros((parts, y_size, x_size, z_size, rows, columns // x_size), BF)

    def put(full, piece, part, from_y, from_z):
        half = jnp.where(from_y == own_c, 0, 1)
        return lax.dynamic_update_slice(
            full, piece[:, None, :, None], (part, half, 0, from_z % z_size, 0, 0)
        )

    def place(full, piece, part, from_z):
        full = put(full, piece, part, own_y, from_z)
        return put(full, shift(piece, "y", 1), part, 1 - own_y, from_z)

    full = place(full, chunk, 0, own_z)
    up = down = chunk
    for step in range(1, z_size // 2):
        up = shift(up, "z", 1)
        down = shift(down, "z", -1)
        full = place(full, up, 0, own_z - step)
        full = place(full, down, 0, own_z + step)
    up = shift(up[:1], "z", 1)
    down = shift(down[1:], "z", -1)
    full = place(full, up, 0, own_z + z_size // 2)
    full = place(full, down, 1, own_z + z_size // 2)
    return full.reshape(parts, y_size, x_size * z_size * rows, columns // x_size)


def decoder_shift(block, axis, distance):
    size = lax.axis_size(axis)
    route = [(size + i, size + (i + distance) % size) for i in range(size)]
    return lax.ppermute(block, ("section", axis), route)


def on_device(section_rows, norm_gains, proj_weights, section_cotan, enc_lengths, dec_segments):
    side = lax.axis_index("section")
    own_x, own_y, own_z, own_c = (lax.axis_index(a) for a in ("x", "y", "z", "mp"))
    x_size = lax.axis_size("x")
    at_encoder = side == 0
    rows, cotan, weights = section_rows[0], section_cotan[0], proj_weights[0]
    row_count, half_width = rows.shape
    width = 2 * half_width
    gain = norm_gains[0].astype(F32)
    wide_rows = rows.astype(F32)

    full = gather_weights(weights, own_y, own_z, own_c)

    square = jnp.sum(wide_rows * wide_rows, -1, keepdims=True)
    inverse = lax.rsqrt((square + shift(square, "mp", 1)) / width + EPS)
    normed = (wide_rows * inverse * gain).astype(BF)
    first_left = jnp.concatenate([normed] + [shift(normed, "x", -r) for r in range(1, x_size)], 0)
    far_cotan = [decoder_shift(cotan, "x", -r) for r in range(1, x_size)]
    cotan_rows = jnp.concatenate([cotan] + far_cotan, 0)
    second_left = jnp.where(at_encoder, first_left, cotan_rows)
    first_other = shift(first_left, "mp", 1)
    second_other = jnp.where(at_encoder, first_other, decoder_shift(cotan_rows, "mp", 1))

    small = jnp.concatenate([dec_segments[0], enc_lengths[0]])
    small = lax.all_gather(small, "x")
    small = jnp.concatenate([small, small], 0)
    small = lax.dynamic_slice_in_dim(small, own_x, x_size, 0)
    segment, lengths = small[:, :row_count], small[:, row_count:]

    def project(left, other, part):
        return (
            dot(left, full[part, 0], ((1,), (0,))) + dot(other, full[part, 1], ((1,), (0,)))
        ).astype(BF)

    packed = jnp.stack(
        (project(first_left, first_other, 0), project(second_left, second_other, 1)), 0
    )
    half = packed.shape[2] // 2
    keep = lax.dynamic_slice_in_dim(packed, side * half, half, 2)
    send = lax.dynamic_slice_in_dim(packed, (1 - side) * half, half, 2)
    recv = shift(send, "section", 1)
    stay, back = attention(lengths, side[None], keep, recv, segment[:, :, None])
    back = shift(back, "section", 1)
    grads = jnp.concatenate(
        (jnp.where(at_encoder, stay, back), jnp.where(at_encoder, back, stay)), 2
    )
    other_grads = shift(grads, "mp", 1)
    other_full = shift(full[:, 1], "mp", 1)

    def upstream_part(block):
        pick = slice(block * row_count, (block + 1) * row_count)
        total = 0.0
        for part in range(2):
            total += dot(grads[part, pick], full[part, 0], ((1,), (1,)))
            total += dot(other_grads[part, pick], other_full[part], ((1,), (1,)))
        return total

    upstream = upstream_part(0)
    for block in (2, 1, 3):
        upstream += shift(upstream_part(block).astype(BF), "x", block).astype(F32)

    wide_cotan = cotan.astype(F32)
    upstream += jnp.where(at_encoder, wide_cotan, 0.0)
    gain_grad = gain * upstream
    row_dot = jnp.sum(wide_rows * gain_grad, -1, keepdims=True)
    row_dot = (row_dot + shift(row_dot, "mp", 1)) / width
    result = inverse * gain_grad - wide_rows * inverse**3 * row_dot
    return (result + jnp.where(at_encoder, 0.0, wide_cotan))[None]


def solution(mesh):
    names = ("section", "y", "x", "z", "mp")
    split = Mesh(mesh.devices.reshape(2, 2, 4, 8, 2), names)
    fsdp = ("y", "x", "z")
    return jax.shard_map(
        on_device,
        mesh=split,
        in_specs=(
            P("section", fsdp, "mp"),
            P("section", "mp"),
            P("section", fsdp, None, "mp"),
            P("section", fsdp, "mp"),
            P(fsdp, None),
            P(fsdp, None),
        ),
        out_specs=P("section", fsdp, "mp"),
        check_vma=False,
    )
```

time: 477 us -> 180 us (0.38)
  waiting for transfers between devices: 422 us -> 80.5 us
  starting transfers between devices: 5.82 us -> 59.3 us
  between operations: 13.3 us -> 1.2 us
  matrix products: 21.7 us -> 12.2 us
  Pallas kernels: 0 us -> 5.52 us
    all_gather x3 -> x0, waiting for transfers between devices: 356 us -> none  [the longest x1 292 us: on_device(): weight_tensors = lax.all_gather(proj_weights[0], 'fsdp', axis=0, tiled=True)]
    ppermute x2 -> x34, starting transfers between devices: 5.7 us -> 54.4 us  [the longest x30 51.6 us: shift(): lax.ppermute(block, axis, [(i, (i + distance) % size) for i in range(size)])]
    ppermute x2 -> x34, waiting for transfers between devices: 31.8 us -> 80.5 us  [the longest x30 80.5 us: shift(): lax.ppermute(block, axis, [(i, (i + distance) % size) for i in range(size)])]
    psum x1 -> x0, waiting for transfers between devices: 32.5 us -> none  [on_device(): summed = lax.psum(partial_grad, 'mp')]
    dot_general x3 -> x20, matrix products: 21.7 us -> 12.2 us  [dot(): lax.dot_general(left, right, (contract, ((), ())), preferred_element_type...]
    unnamed x0 -> x1, blocking collectives: none -> 7.32 us
    pallas_call x0 -> x1, Pallas kernels: none -> 5.52 us  [attention(): pl.pallas_call(attention_kernel, out_shape=(shape, shape), in_specs=[scal...]
    all_gather x1 -> x0, blocking collectives: 4.94 us -> none  [on_device(): lax.all_gather(norm_gains, 'mp', axis=1, tiled=True)]
  transfers between devices with their start and end apart: 6 -> 35, of which waited for: 6 -> 16; matrix products, arithmetic and copies ran while one was open for 2% -> 12% of each run, Pallas kernels for 0% -> 3%
where the time goes in v1:
time: 180 us; the launch traced here: 179 us
  waiting for transfers between devices  80.5 us (45%)
  starting transfers between devices  59.3 us (33%)
  matrix products  12.2 us (7%)
  blocking collectives  7.32 us (4%)
  other arithmetic  6.75 us (4%)
  local copies, waits for them, and re-layouts  6.55 us (4%)
  Pallas kernels  5.52 us (3%)
    ppermute x30, waiting for transfers between devices, shift(): lax.ppermute(block, axis, [(i, (i + distance) % size) for i in range(size)])  80.5 us
    ppermute x30, starting transfers between devices, shift(): lax.ppermute(block, axis, [(i, (i + distance) % size) for i in range(size)])  51.6 us
    dot_general x20, matrix products, dot(): lax.dot_general(left, right, (contract, ((), ())), preferred_element_type...  12.2 us
    unnamed x1, blocking collectives  7.32 us
    pallas_call x1, Pallas kernels, attention(): pl.pallas_call(attention_kernel, out_shape=(shape, shape), in_specs=[scal...  5.52 us
    all_to_all x1, starting transfers between devices, gather_weights(): chunk = lax.all_to_all(slices, 'x', 0, 0, tiled=True)  4.84 us
  transfers between devices with their start and end apart: 35, of which 16 were waited for; matrix products, arithmetic and copies ran while one was open for 12% of the time, Pallas kernels for 3%

profile of v1, /device:TPU:1, one launch (start us, length us, event | category | flops | bytes accessed | tf_op | source)
XLA Modules:
  0.0 179.3 jit_solution(8275068364563221408)
XLA Ops:
  4.0 4.8 %all-to-all-start = ((bf16[4,2,64,256]{3,2,1,0:T(8,128)(2,1)}), bf16[4,2,64,256]{3,2,1,0:T(8,128)(2,1)S(1)}, u32[]{:S(2)}, u32[]{:S(2)}) async-start(bf16[4,2,64,256]{3,2,1,0:T(8,128)(2,1)} %copy.60), calls=%async_computation | async-start | bytes 524288 | tf_op jit(solution)/shard_map/all_to_all | solution.py:84
  10.1 1.9 %collective-permute-start = (f32[128,1]{0,1:T(1,128)S(1)}, f32[128,1]{0,1:T(1,128)S(1)}, u32[]{:S(2)}, u32[]{:S(2)}) collective-permute-start(f32[128,1]{0,1:T(1,128)S(1)} %bitcast.222), channel_id=1, source_target_pairs={{0,1},{1,0},{2,3},{3,2},{4,5},{5,4},{6,7},{7,6},{8,9},{9,8},{10,11... | collective-permute-start | bytes 1544 | tf_op jit(solution)/shard_map/ppermute | solution.py:18
  15.4 7.3 %all-reduce = s32[520]{0:T(1024)S(1)} all-reduce(s32[520]{0:T(1024)S(1)} %add_dynamic-update-slice_fusion), channel_id=2, replica_groups=mesh['section'=2,'y'=2,'x'=4,'z'=8,'mp'=2] {'x'}, use_global_device_ids=true, to_apply=%add | all-reduce | flops 520 | bytes 4160
  23.4 1.6 collective-permute-start.5
  26.8 1.7 collective-permute-done.4
  29.4 3.7 %collective-permute-done.5 = bf16[2,4,64,256]{3,2,1,0:T(8,128)(2,1)S(1)} collective-permute-done((bf16[2,4,64,256]{3,2,1,0:T(8,128)(2,1)S(1)}, bf16[2,4,64,256]{3,2,1,0:T(8,128)(2,1)S(1)}, u32[]{:S(2)}, u32[]{:S(2)}) %collective-permute-start.5) | collective-permute-done | bytes 262176 | tf_op jit(solution)/shard_map/ppermute | solution.py:18
  34.7 1.4 collective-permute-start.7
  37.0 3.2 %collective-permute-done.7 = bf16[2,4,64,256]{3,2,1,0:T(8,128)(2,1)S(1)} collective-permute-done((bf16[2,4,64,256]{3,2,1,0:T(8,128)(2,1)S(1)}, bf16[2,4,64,256]{3,2,1,0:T(8,128)(2,1)S(1)}, u32[]{:S(2)}, u32[]{:S(2)}) %collective-permute-start.7) | collective-permute-done | bytes 262176 | tf_op jit(solution)/shard_map/ppermute | solution.py:18
  40.5 4.6 %collective-permute-done.2 = bf16[128,2048]{1,0:T(8,128)(2,1)S(1)} collective-permute-done((bf16[128,2048]{1,0:T(8,128)(2,1)S(1)}, bf16[128,2048]{1,0:T(8,128)(2,1)S(1)}, u32[]{:S(2)}, u32[]{:S(2)}) %collective-permute-start.2) | collective-permute-done | bytes 524320 | tf_op jit(solution)/shard_map/ppermute | solution.py:18
  46.2 13.5 %collective-permute-done.3 = bf16[128,2048]{1,0:T(8,128)(2,1)S(1)} collective-permute-done((bf16[128,2048]{1,0:T(8,128)(2,1)S(1)}, bf16[128,2048]{1,0:T(8,128)(2,1)S(1)}, u32[]{:S(2)}, u32[]{:S(2)}) %collective-permute-start.3) | collective-permute-done | bytes 524320 | tf_op jit(solution)/shard_map/ppermute | solution.py:18
  61.7 2.7 %collective-permute-start.15 = (bf16[2,4,64,256]{3,2,1,0:T(8,128)(2,1)S(1)}, bf16[2,4,64,256]{3,2,1,0:T(8,128)(2,1)S(1)}, u32[]{:S(2)}, u32[]{:S(2)}) collective-permute-start(bf16[2,4,64,256]{3,2,1,0:T(8,128)(2,1)S(1)} %collective-permute-done.11), channel_id=1, source_target_pairs={{0,14},{2,0},{4,2},{6,4},{8,6},{10,8},{12,10},{14,12},{1,15},{3,1}... | collective-permute-start | bytes 786440 | tf_op jit(solution)/shard_map/ppermute | solution.py:18
  64.4 6.0 %collective-permute-done.13 = bf16[2,4,64,256]{3,2,1,0:T(8,128)(2,1)S(1)} collective-permute-done((bf16[2,4,64,256]{3,2,1,0:T(8,128)(2,1)S(1)}, bf16[2,4,64,256]{3,2,1,0:T(8,128)(2,1)S(1)}, u32[]{:S(2)}, u32[]{:S(2)}) %collective-permute-start.13) | collective-permute-done | bytes 262176 | tf_op jit(solution)/shard_map/ppermute | solution.py:18
  71.9 2.7 %collective-permute-start.19 = (bf16[1,4,64,256]{3,2,1,0:T(8,128)(2,1)S(1)}, bf16[1,4,64,256]{3,2,1,0:T(8,128)(2,1)S(1)}, u32[]{:S(2)}, u32[]{:S(2)}) collective-permute-start(bf16[1,4,64,256]{3,2,1,0:T(8,128)(2,1)S(1)} %slice.124), channel_id=1, source_target_pairs={{0,14},{2,0},{4,2},{6,4},{8,6},{10,8},{12,10},{14,12},{1,15},{3,1}... | collective-permute-start | bytes 393224 | tf_op jit(solution)/shard_map/ppermute | solution.py:18
  74.7 2.4 %collective-permute-done.12 = bf16[2,4,64,256]{3,2,1,0:T(8,128)(2,1)S(1)} collective-permute-done((bf16[2,4,64,256]{3,2,1,0:T(8,128)(2,1)S(1)}, bf16[2,4,64,256]{3,2,1,0:T(8,128)(2,1)S(1)}, u32[]{:S(2)}, u32[]{:S(2)}) %collective-permute-start.12) | collective-permute-done | bytes 262176 | tf_op jit(solution)/shard_map/ppermute | solution.py:18
  78.7 1.3 collective-permute-start.18
  80.0 2.8 %collective-permute-done.14 = bf16[2,4,64,256]{3,2,1,0:T(8,128)(2,1)S(1)} collective-permute-done((bf16[2,4,64,256]{3,2,1,0:T(8,128)(2,1)S(1)}, bf16[2,4,64,256]{3,2,1,0:T(8,128)(2,1)S(1)}, u32[]{:S(2)}, u32[]{:S(2)}) %collective-permute-start.14) | collective-permute-done | bytes 262176 | tf_op jit(solution)/shard_map/ppermute | solution.py:18
  84.1 4.3 %collective-permute-done.16 = bf16[2,4,64,256]{3,2,1,0:T(8,128)(2,1)S(1)} collective-permute-done((bf16[2,4,64,256]{3,2,1,0:T(8,128)(2,1)S(1)}, bf16[2,4,64,256]{3,2,1,0:T(8,128)(2,1)S(1)}, u32[]{:S(2)}, u32[]{:S(2)}) %collective-permute-start.16) | collective-permute-done | bytes 262176 | tf_op jit(solution)/shard_map/ppermute | solution.py:18
  88.4 2.8 %collective-permute-done.18 = bf16[1,4,64,256]{3,2,1,0:T(8,128)(2,1)S(1)} collective-permute-done((bf16[1,4,64,256]{3,2,1,0:T(8,128)(2,1)S(1)}, bf16[1,4,64,256]{3,2,1,0:T(8,128)(2,1)S(1)}, u32[]{:S(2)}, u32[]{:S(2)}) %collective-permute-start.18) | collective-permute-done | bytes 131104 | tf_op jit(solution)/shard_map/ppermute | solution.py:18
  91.2 2.8 %collective-permute-done.20 = bf16[1,4,64,256]{3,2,1,0:T(8,128)(2,1)S(1)} collective-permute-done((bf16[1,4,64,256]{3,2,1,0:T(8,128)(2,1)S(1)}, bf16[1,4,64,256]{3,2,1,0:T(8,128)(2,1)S(1)}, u32[]{:S(2)}, u32[]{:S(2)}) %collective-permute-start.20) | collective-permute-done | bytes 131104 | tf_op jit(solution)/shard_map/ppermute | solution.py:18
  94.0 1.6 slice_bitcast_fusion
  95.6 3.0 %collective-permute-start.29 = (bf16[2,2048,256]{2,1,0:T(8,128)(2,1)}, bf16[2,2048,256]{2,1,0:T(8,128)(2,1)S(1)}, u32[]{:S(2)}, u32[]{:S(2)}) collective-permute-start(bf16[2,2048,256]{2,1,0:T(8,128)(2,1)} %slice_bitcast_fusion), channel_id=1, source_target_pairs={{0,1},{1,0},{2,3},{3,2},{4,5},{5,4},{6,7},{7,6},{8,9},{9,8},{10,11... | collective-permute-start | bytes 6291464 | tf_op jit(solution)/shard_map/ppermute | solution.py:18
  103.0 18.1 %collective-permute-start.26 = (bf16[2,512,128]{2,1,0:T(8,128)(2,1)}, bf16[2,512,128]{2,1,0:T(8,128)(2,1)S(1)}, u32[]{:S(2)}, u32[]{:S(2)}) collective-permute-start(bf16[2,512,128]{2,1,0:T(8,128)(2,1)} %get-tuple-element.13), channel_id=1, source_target_pairs={{0,128},{128,0},{1,129},{129,1},{2,130},{130,2},{3,131},{131,3},{4... | collective-permute-start | bytes 786440 | tf_op jit(solution)/shard_map/ppermute | solution.py:18
  121.3 6.7 %collective-permute-done.26.recv_ref = bf16[2,512,128]{2,1,0:T(8,128)(2,1)S(1)} collective-permute-done((bf16[2,512,128]{2,1,0:T(8,128)(2,1)}, bf16[2,512,128]{2,1,0:T(8,128)(2,1)S(1)}, u32[]{:S(2)}, u32[]{:S(2)}) %collective-permute-start.26) | collective-permute-done | bytes 262176 | tf_op jit(solution)/shard_map/ppermute | solution.py:18
  128.0 5.5 %shard_map.64 = (bf16[2,512,128]{2,1,0:T(8,128)(2,1)S(1)}, bf16[2,512,128]{2,1,0:T(8,128)(2,1)S(1)}) custom-call(s32[4,2]{1,0:T(4,128)S(1)} %slice.122.lengths_ref, s32[1]{0:T(128)} %bitcast.7.side_ref, bf16[2,512,128]{2,1,0:T(8,128)(2,1)S(1)} %get-tuple-element.14.keep_ref, bf16[2,512,128]{2,1,0:T(8,128)(2,1)S(1)} %collective-permute-done.26.recv_ref, ...), custom_call_target="tpu_custom_call" | custom-call | tf_op jit(solution)/shard_map/pallas_call | solution.py:71
  133.6 2.9 %collective-permute-start.27 = (bf16[2,512,128]{2,1,0:T(8,128)(2,1)S(1)}, bf16[2,512,128]{2,1,0:T(8,128)(2,1)S(1)}, u32[]{:S(2)}, u32[]{:S(2)}) collective-permute-start(bf16[2,512,128]{2,1,0:T(8,128)(2,1)S(1)} %get-tuple-element.8), channel_id=1, source_target_pairs={{0,128},{128,0},{1,129},{129,1},{2,130},{130,2},{3,131},{131,3},{4... | collective-permute-start | bytes 786440 | tf_op jit(solution)/shard_map/ppermute | solution.py:18
  136.4 6.0 %collective-permute-done.27 = bf16[2,512,128]{2,1,0:T(8,128)(2,1)S(1)} collective-permute-done((bf16[2,512,128]{2,1,0:T(8,128)(2,1)S(1)}, bf16[2,512,128]{2,1,0:T(8,128)(2,1)S(1)}, u32[]{:S(2)}, u32[]{:S(2)}) %collective-permute-start.27) | collective-permute-done | bytes 262176 | tf_op jit(solution)/shard_map/ppermute | solution.py:18
  142.5 1.8 collective-permute-start.28
  144.3 1.7 fusion.37
  151.0 2.3 %collective-permute-start.31 = (bf16[128,2048]{1,0:T(8,128)(2,1)S(1)}, bf16[128,2048]{1,0:T(8,128)(2,1)S(1)}, u32[]{:S(2)}, u32[]{:S(2)}) collective-permute-start(bf16[128,2048]{1,0:T(8,128)(2,1)S(1)} %fusion.6), channel_id=1, source_target_pairs={{0,16},{16,32},{32,48},{48,0},{1,17},{17,33},{33,49},{49,1},{2,18}... | collective-permute-start | bytes 1572872 | tf_op jit(solution)/shard_map/ppermute | solution.py:18
  156.3 7.8 %collective-permute-done.30 = bf16[128,2048]{1,0:T(8,128)(2,1)S(1)} collective-permute-done((bf16[128,2048]{1,0:T(8,128)(2,1)S(1)}, bf16[128,2048]{1,0:T(8,128)(2,1)S(1)}, u32[]{:S(2)}, u32[]{:S(2)}) %collective-permute-start.30) | collective-permute-done | bytes 524320 | tf_op jit(solution)/shard_map/ppermute | solution.py:18
  164.1 11.5 %collective-permute-done.31 = bf16[128,2048]{1,0:T(8,128)(2,1)S(1)} collective-permute-done((bf16[128,2048]{1,0:T(8,128)(2,1)S(1)}, bf16[128,2048]{1,0:T(8,128)(2,1)S(1)}, u32[]{:S(2)}, u32[]{:S(2)}) %collective-permute-start.31) | collective-permute-done | bytes 524320 | tf_op jit(solution)/shard_map/ppermute | solution.py:18
  177.8 1.5 fusion.26
  (124 shorter events, 36.3 us)
Async XLA Ops:
  0.0 34.4 %collective-permute-start.22 = (bf16[128,2048]{1,0:T(8,128)(2,1)}, bf16[128,2048]{1,0:T(8,128)(2,1)S(1)}, u32[]{:S(2)}, u32[]{:S(2)}) collective-permute-start(bf16[128,2048]{1,0:T(8,128)(2,1)} %bitcast.209), channel_id=1, source_target_pairs={{128,176},{144,128},{160,144},{176,160},{129,177},{145,129},{161,1... | collective-permute-start | bytes 1572872 | tf_op jit(solution)/shard_map/ppermute | solution.py:115
  0.7 34.0 %collective-permute-start.23 = (bf16[128,2048]{1,0:T(8,128)(2,1)}, bf16[128,2048]{1,0:T(8,128)(2,1)S(1)}, u32[]{:S(2)}, u32[]{:S(2)}) collective-permute-start(bf16[128,2048]{1,0:T(8,128)(2,1)} %bitcast.210), channel_id=1, source_target_pairs={{128,160},{144,176},{160,128},{176,144},{129,161},{145,177},{161,1... | collective-permute-start | bytes 1572872 | tf_op jit(solution)/shard_map/ppermute | solution.py:115
  1.4 34.7 %collective-permute-start.24 = (bf16[128,2048]{1,0:T(8,128)(2,1)}, bf16[128,2048]{1,0:T(8,128)(2,1)S(1)}, u32[]{:S(2)}, u32[]{:S(2)}) collective-permute-start(bf16[128,2048]{1,0:T(8,128)(2,1)} %bitcast.211), channel_id=1, source_target_pairs={{128,144},{144,160},{160,176},{176,128},{129,145},{145,161},{161,1... | collective-permute-start | bytes 1572872 | tf_op jit(solution)/shard_map/ppermute | solution.py:115
  4.0 18.8 %all-to-all-start = ((bf16[4,2,64,256]{3,2,1,0:T(8,128)(2,1)}), bf16[4,2,64,256]{3,2,1,0:T(8,128)(2,1)S(1)}, u32[]{:S(2)}, u32[]{:S(2)}) async-start(bf16[4,2,64,256]{3,2,1,0:T(8,128)(2,1)} %copy.60), calls=%async_computation | async-start | bytes 524288 | tf_op jit(solution)/shard_map/all_to_all | solution.py:84
  10.1 12.7 %collective-permute-start = (f32[128,1]{0,1:T(1,128)S(1)}, f32[128,1]{0,1:T(1,128)S(1)}, u32[]{:S(2)}, u32[]{:S(2)}) collective-permute-start(f32[128,1]{0,1:T(1,128)S(1)} %bitcast.222), channel_id=1, source_target_pairs={{0,1},{1,0},{2,3},{3,2},{4,5},{5,4},{6,7},{7,6},{8,9},{9,8},{10,11... | collective-permute-start | bytes 1544 | tf_op jit(solution)/shard_map/ppermute | solution.py:18
  22.8 5.7 %collective-permute-start.4 = (bf16[2,4,64,256]{3,2,1,0:T(8,128)(2,1)S(1)}, bf16[2,4,64,256]{3,2,1,0:T(8,128)(2,1)S(1)}, u32[]{:S(2)}, u32[]{:S(2)}) collective-permute-start(bf16[2,4,64,256]{3,2,1,0:T(8,128)(2,1)S(1)} %bitcast.215), channel_id=1, source_target_pairs={{0,64},{64,0},{1,65},{65,1},{2,66},{66,2},{3,67},{67,3},{4,68},{68... | collective-permute-start | bytes 786440 | tf_op jit(solution)/shard_map/ppermute | solution.py:18
  23.4 9.7 %collective-permute-start.5 = (bf16[2,4,64,256]{3,2,1,0:T(8,128)(2,1)S(1)}, bf16[2,4,64,256]{3,2,1,0:T(8,128)(2,1)S(1)}, u32[]{:S(2)}, u32[]{:S(2)}) collective-permute-start(bf16[2,4,64,256]{3,2,1,0:T(8,128)(2,1)S(1)} %bitcast.216), channel_id=1, source_target_pairs={{0,2},{2,4},{4,6},{6,8},{8,10},{10,12},{12,14},{14,0},{1,3},{3,5},... | collective-permute-start | bytes 786440 | tf_op jit(solution)/shard_map/ppermute | solution.py:18
  28.5 11.7 %collective-permute-start.1 = (bf16[128,2048]{1,0:T(8,128)(2,1)S(1)}, bf16[128,2048]{1,0:T(8,128)(2,1)S(1)}, u32[]{:S(2)}, u32[]{:S(2)}) collective-permute-start(bf16[128,2048]{1,0:T(8,128)(2,1)S(1)} %fusion.29), channel_id=1, source_target_pairs={{0,48},{16,0},{32,16},{48,32},{1,49},{17,1},{33,17},{49,33},{2,50}... | collective-permute-start | bytes 1572872 | tf_op jit(solution)/shard_map/ppermute | solution.py:18
  33.1 11.9 %collective-permute-start.2 = (bf16[128,2048]{1,0:T(8,128)(2,1)S(1)}, bf16[128,2048]{1,0:T(8,128)(2,1)S(1)}, u32[]{:S(2)}, u32[]{:S(2)}) collective-permute-start(bf16[128,2048]{1,0:T(8,128)(2,1)S(1)} %fusion.29), channel_id=1, source_target_pairs={{0,32},{16,48},{32,0},{48,16},{1,33},{17,49},{33,1},{49,17},{2,34}... | collective-permute-start | bytes 1572872 | tf_op jit(solution)/shard_map/ppermute | solution.py:18
  34.4 25.3 %collective-permute-start.3 = (bf16[128,2048]{1,0:T(8,128)(2,1)S(1)}, bf16[128,2048]{1,0:T(8,128)(2,1)S(1)}, u32[]{:S(2)}, u32[]{:S(2)}) collective-permute-start(bf16[128,2048]{1,0:T(8,128)(2,1)S(1)} %fusion.29), channel_id=1, source_target_pairs={{0,16},{16,32},{32,48},{48,0},{1,17},{17,33},{33,49},{49,1},{2,18}... | collective-permute-start | bytes 1572872 | tf_op jit(solution)/shard_map/ppermute | solution.py:18
  36.1 24.6 %collective-permute-start.6 = (bf16[2,4,64,256]{3,2,1,0:T(8,128)(2,1)S(1)}, bf16[2,4,64,256]{3,2,1,0:T(8,128)(2,1)S(1)}, u32[]{:S(2)}, u32[]{:S(2)}) collective-permute-start(bf16[2,4,64,256]{3,2,1,0:T(8,128)(2,1)S(1)} %collective-permute-done.5), channel_id=1, source_target_pairs={{0,64},{64,0},{1,65},{65,1},{2,66},{66,2},{3,67},{67,3},{4,68},{68... | collective-permute-start | bytes 786440 | tf_op jit(solution)/shard_map/ppermute | solution.py:18
  40.3 21.1 %collective-permute-start.9 = (bf16[2,4,64,256]{3,2,1,0:T(8,128)(2,1)S(1)}, bf16[2,4,64,256]{3,2,1,0:T(8,128)(2,1)S(1)}, u32[]{:S(2)}, u32[]{:S(2)}) collective-permute-start(bf16[2,4,64,256]{3,2,1,0:T(8,128)(2,1)S(1)} %collective-permute-done.5), channel_id=1, source_target_pairs={{0,2},{2,4},{4,6},{6,8},{8,10},{10,12},{12,14},{14,0},{1,3},{3,5},... | collective-permute-start | bytes 786440 | tf_op jit(solution)/shard_map/ppermute | solution.py:18
  40.3 21.3 %collective-permute-start.8 = (bf16[2,4,64,256]{3,2,1,0:T(8,128)(2,1)S(1)}, bf16[2,4,64,256]{3,2,1,0:T(8,128)(2,1)S(1)}, u32[]{:S(2)}, u32[]{:S(2)}) collective-permute-start(bf16[2,4,64,256]{3,2,1,0:T(8,128)(2,1)S(1)} %collective-permute-done.7), channel_id=1, source_target_pairs={{0,64},{64,0},{1,65},{65,1},{2,66},{66,2},{3,67},{67,3},{4,68},{68... | collective-permute-start | bytes 786440 | tf_op jit(solution)/shard_map/ppermute | solution.py:18
  45.0 16.7 %collective-permute-start.11 = (bf16[2,4,64,256]{3,2,1,0:T(8,128)(2,1)S(1)}, bf16[2,4,64,256]{3,2,1,0:T(8,128)(2,1)S(1)}, u32[]{:S(2)}, u32[]{:S(2)}) collective-permute-start(bf16[2,4,64,256]{3,2,1,0:T(8,128)(2,1)S(1)} %collective-permute-done.7), channel_id=1, source_target_pairs={{0,14},{2,0},{4,2},{6,4},{8,6},{10,8},{12,10},{14,12},{1,15},{3,1}... | collective-permute-start | bytes 786440 | tf_op jit(solution)/shard_map/ppermute | solution.py:18
  59.7 39.7 %collective-permute-start.25 = (bf16[512,2048]{1,0:T(8,128)(2,1)S(1)}, bf16[512,2048]{1,0:T(8,128)(2,1)S(1)}, u32[]{:S(2)}, u32[]{:S(2)}) collective-permute-start(bf16[512,2048]{1,0:T(8,128)(2,1)S(1)} %pad_maximum_fusion.1), channel_id=1, source_target_pairs={{128,129},{129,128},{130,131},{131,130},{132,133},{133,132},{134,1... | collective-permute-start | bytes 6291464 | tf_op jit(solution)/shard_map/ppermute | solution.py:115
  60.7 37.9 %collective-permute-start.21 = (bf16[512,2048]{1,0:T(8,128)(2,1)S(1)}, bf16[512,2048]{1,0:T(8,128)(2,1)S(1)}, u32[]{:S(2)}, u32[]{:S(2)}) collective-permute-start(bf16[512,2048]{1,0:T(8,128)(2,1)S(1)} %pad_maximum_fusion), channel_id=1, source_target_pairs={{0,1},{1,0},{2,3},{3,2},{4,5},{5,4},{6,7},{7,6},{8,9},{9,8},{10,11... | collective-permute-start | bytes 6291464 | tf_op jit(solution)/shard_map/ppermute | solution.py:18
  61.3 10.5 %collective-permute-start.10 = (bf16[2,4,64,256]{3,2,1,0:T(8,128)(2,1)S(1)}, bf16[2,4,64,256]{3,2,1,0:T(8,128)(2,1)S(1)}, u32[]{:S(2)}, u32[]{:S(2)}) collective-permute-start(bf16[2,4,64,256]{3,2,1,0:T(8,128)(2,1)S(1)} %collective-permute-done.9), channel_id=1, source_target_pairs={{0,64},{64,0},{1,65},{65,1},{2,66},{66,2},{3,67},{67,3},{4,68},{68... | collective-permute-start | bytes 786440 | tf_op jit(solution)/shard_map/ppermute | solution.py:18
  61.6 8.8 %collective-permute-start.13 = (bf16[2,4,64,256]{3,2,1,0:T(8,128)(2,1)S(1)}, bf16[2,4,64,256]{3,2,1,0:T(8,128)(2,1)S(1)}, u32[]{:S(2)}, u32[]{:S(2)}) collective-permute-start(bf16[2,4,64,256]{3,2,1,0:T(8,128)(2,1)S(1)} %collective-permute-done.9), channel_id=1, source_target_pairs={{0,2},{2,4},{4,6},{6,8},{8,10},{10,12},{12,14},{14,0},{1,3},{3,5},... | collective-permute-start | bytes 786440 | tf_op jit(solution)/shard_map/ppermute | solution.py:18
  61.7 10.0 %collective-permute-start.15 = (bf16[2,4,64,256]{3,2,1,0:T(8,128)(2,1)S(1)}, bf16[2,4,64,256]{3,2,1,0:T(8,128)(2,1)S(1)}, u32[]{:S(2)}, u32[]{:S(2)}) collective-permute-start(bf16[2,4,64,256]{3,2,1,0:T(8,128)(2,1)S(1)} %collective-permute-done.11), channel_id=1, source_target_pairs={{0,14},{2,0},{4,2},{6,4},{8,6},{10,8},{12,10},{14,12},{1,15},{3,1}... | collective-permute-start | bytes 786440 | tf_op jit(solution)/shard_map/ppermute | solution.py:18
  70.4 6.6 %collective-permute-start.12 = (bf16[2,4,64,256]{3,2,1,0:T(8,128)(2,1)S(1)}, bf16[2,4,64,256]{3,2,1,0:T(8,128)(2,1)S(1)}, u32[]{:S(2)}, u32[]{:S(2)}) collective-permute-start(bf16[2,4,64,256]{3,2,1,0:T(8,128)(2,1)S(1)} %collective-permute-done.11), channel_id=1, source_target_pairs={{0,64},{64,0},{1,65},{65,1},{2,66},{66,2},{3,67},{67,3},{4,68},{68... | collective-permute-start | bytes 786440 | tf_op jit(solution)/shard_map/ppermute | solution.py:18
  71.8 6.6 %collective-permute-start.17 = (bf16[1,4,64,256]{3,2,1,0:T(8,128)(2,1)S(1)}, bf16[1,4,64,256]{3,2,1,0:T(8,128)(2,1)S(1)}, u32[]{:S(2)}, u32[]{:S(2)}) collective-permute-start(bf16[1,4,64,256]{3,2,1,0:T(8,128)(2,1)S(1)} %slice.123), channel_id=1, source_target_pairs={{0,2},{2,4},{4,6},{6,8},{8,10},{10,12},{12,14},{14,0},{1,3},{3,5},... | collective-permute-start | bytes 393224 | tf_op jit(solution)/shard_map/ppermute | solution.py:18
  71.9 6.8 %collective-permute-start.19 = (bf16[1,4,64,256]{3,2,1,0:T(8,128)(2,1)S(1)}, bf16[1,4,64,256]{3,2,1,0:T(8,128)(2,1)S(1)}, u32[]{:S(2)}, u32[]{:S(2)}) collective-permute-start(bf16[1,4,64,256]{3,2,1,0:T(8,128)(2,1)S(1)} %slice.124), channel_id=1, source_target_pairs={{0,14},{2,0},{4,2},{6,4},{8,6},{10,8},{12,10},{14,12},{1,15},{3,1}... | collective-permute-start | bytes 393224 | tf_op jit(solution)/shard_map/ppermute | solution.py:18
  77.0 5.7 %collective-permute-start.14 = (bf16[2,4,64,256]{3,2,1,0:T(8,128)(2,1)S(1)}, bf16[2,4,64,256]{3,2,1,0:T(8,128)(2,1)S(1)}, u32[]{:S(2)}, u32[]{:S(2)}) collective-permute-start(bf16[2,4,64,256]{3,2,1,0:T(8,128)(2,1)S(1)} %collective-permute-done.13), channel_id=1, source_target_pairs={{0,64},{64,0},{1,65},{65,1},{2,66},{66,2},{3,67},{67,3},{4,68},{68... | collective-permute-start | bytes 786440 | tf_op jit(solution)/shard_map/ppermute | solution.py:18
  78.4 9.9 %collective-permute-start.16 = (bf16[2,4,64,256]{3,2,1,0:T(8,128)(2,1)S(1)}, bf16[2,4,64,256]{3,2,1,0:T(8,128)(2,1)S(1)}, u32[]{:S(2)}, u32[]{:S(2)}) collective-permute-start(bf16[2,4,64,256]{3,2,1,0:T(8,128)(2,1)S(1)} %collective-permute-done.15), channel_id=1, source_target_pairs={{0,64},{64,0},{1,65},{65,1},{2,66},{66,2},{3,67},{67,3},{4,68},{68... | collective-permute-start | bytes 786440 | tf_op jit(solution)/shard_map/ppermute | solution.py:18
  78.7 12.5 %collective-permute-start.18 = (bf16[1,4,64,256]{3,2,1,0:T(8,128)(2,1)S(1)}, bf16[1,4,64,256]{3,2,1,0:T(8,128)(2,1)S(1)}, u32[]{:S(2)}, u32[]{:S(2)}) collective-permute-start(bf16[1,4,64,256]{3,2,1,0:T(8,128)(2,1)S(1)} %collective-permute-done.17), channel_id=1, source_target_pairs={{0,64},{64,0},{1,65},{65,1},{2,66},{66,2},{3,67},{67,3},{4,68},{68... | collective-permute-start | bytes 393224 | tf_op jit(solution)/shard_map/ppermute | solution.py:18
  82.7 11.2 %collective-permute-start.20 = (bf16[1,4,64,256]{3,2,1,0:T(8,128)(2,1)S(1)}, bf16[1,4,64,256]{3,2,1,0:T(8,128)(2,1)S(1)}, u32[]{:S(2)}, u32[]{:S(2)}) collective-permute-start(bf16[1,4,64,256]{3,2,1,0:T(8,128)(2,1)S(1)} %collective-permute-done.19), channel_id=1, source_target_pairs={{0,64},{64,0},{1,65},{65,1},{2,66},{66,2},{3,67},{67,3},{4,68},{68... | collective-permute-start | bytes 393224 | tf_op jit(solution)/shard_map/ppermute | solution.py:18
  95.6 51.8 %collective-permute-start.29 = (bf16[2,2048,256]{2,1,0:T(8,128)(2,1)}, bf16[2,2048,256]{2,1,0:T(8,128)(2,1)S(1)}, u32[]{:S(2)}, u32[]{:S(2)}) collective-permute-start(bf16[2,2048,256]{2,1,0:T(8,128)(2,1)} %slice_bitcast_fusion), channel_id=1, source_target_pairs={{0,1},{1,0},{2,3},{3,2},{4,5},{5,4},{6,7},{7,6},{8,9},{9,8},{10,11... | collective-permute-start | bytes 6291464 | tf_op jit(solution)/shard_map/ppermute | solution.py:18
  103.0 25.0 %collective-permute-start.26 = (bf16[2,512,128]{2,1,0:T(8,128)(2,1)}, bf16[2,512,128]{2,1,0:T(8,128)(2,1)S(1)}, u32[]{:S(2)}, u32[]{:S(2)}) collective-permute-start(bf16[2,512,128]{2,1,0:T(8,128)(2,1)} %get-tuple-element.13), channel_id=1, source_target_pairs={{0,128},{128,0},{1,129},{129,1},{2,130},{130,2},{3,131},{131,3},{4... | collective-permute-start | bytes 786440 | tf_op jit(solution)/shard_map/ppermute | solution.py:18
  133.6 8.9 %collective-permute-start.27 = (bf16[2,512,128]{2,1,0:T(8,128)(2,1)S(1)}, bf16[2,512,128]{2,1,0:T(8,128)(2,1)S(1)}, u32[]{:S(2)}, u32[]{:S(2)}) collective-permute-start(bf16[2,512,128]{2,1,0:T(8,128)(2,1)S(1)} %get-tuple-element.8), channel_id=1, source_target_pairs={{0,128},{128,0},{1,129},{129,1},{2,130},{130,2},{3,131},{131,3},{4... | collective-permute-start | bytes 786440 | tf_op jit(solution)/shard_map/ppermute | solution.py:18
  148.9 15.2 %collective-permute-start.30 = (bf16[128,2048]{1,0:T(8,128)(2,1)S(1)}, bf16[128,2048]{1,0:T(8,128)(2,1)S(1)}, u32[]{:S(2)}, u32[]{:S(2)}) collective-permute-start(bf16[128,2048]{1,0:T(8,128)(2,1)S(1)} %fusion.5), channel_id=1, source_target_pairs={{0,32},{16,48},{32,0},{48,16},{1,33},{17,49},{33,1},{49,17},{2,34}... | collective-permute-start | bytes 1572872 | tf_op jit(solution)/shard_map/ppermute | solution.py:18
  151.0 24.6 %collective-permute-start.31 = (bf16[128,2048]{1,0:T(8,128)(2,1)S(1)}, bf16[128,2048]{1,0:T(8,128)(2,1)S(1)}, u32[]{:S(2)}, u32[]{:S(2)}) collective-permute-start(bf16[128,2048]{1,0:T(8,128)(2,1)S(1)} %fusion.6), channel_id=1, source_target_pairs={{0,16},{16,32},{32,48},{48,0},{1,17},{17,33},{33,49},{49,1},{2,18}... | collective-permute-start | bytes 1572872 | tf_op jit(solution)/shard_map/ppermute | solution.py:18
  154.8 20.8 %collective-permute-start.32 = (bf16[128,2048]{1,0:T(8,128)(2,1)S(1)}, bf16[128,2048]{1,0:T(8,128)(2,1)S(1)}, u32[]{:S(2)}, u32[]{:S(2)}) collective-permute-start(bf16[128,2048]{1,0:T(8,128)(2,1)S(1)} %fusion.7), channel_id=1, source_target_pairs={{0,48},{16,0},{32,16},{48,32},{1,49},{17,1},{33,17},{49,33},{2,50}... | collective-permute-start | bytes 1572872 | tf_op jit(solution)/shard_map/ppermute | solution.py:18
  (13 other events, 175.7 us)

commit v2 on v1

v2 whole, which is shorter than its diff:
```python
import functools

import jax
import jax.numpy as jnp
import numpy as np
from jax import lax
from jax.experimental import pallas as pl
from jax.experimental.pallas import tpu as pltpu
from jax.sharding import Mesh, PartitionSpec as P

HD = 64
ELEN = 64
EPS = 1e-06
BF = jnp.bfloat16
F32 = jnp.float32
MIB = 1024 * 1024
META = 16
PIECES = 9


def shift(block, axis, distance):
    size = lax.axis_size(axis)
    return lax.ppermute(block, axis, [(i, (i + distance) % size) for i in range(size)])


def dot(left, right, contract):
    return lax.dot_general(left, right, (contract, ((), ())), preferred_element_type=F32)


def attention_kernel(place_ref, meta_ref, *refs):
    keep_refs, recv_refs, (stay_ref, send_ref) = refs[:2], refs[2:4], refs[4:]
    at_encoder = place_ref[0] == 0
    rows = 2 * ELEN
    query_index = lax.broadcasted_iota(jnp.int32, (rows, rows), 0).astype(F32)
    key_place = lax.broadcasted_iota(jnp.int32, (rows, rows), 1)
    key_slot = (key_place >= ELEN).astype(F32)
    key_index = key_place.astype(F32)
    lane = lax.broadcasted_iota(jnp.int32, (rows, 2 * HD), 1)
    for block in range(meta_ref.shape[0]):
        pick = pl.ds(block * rows, rows)
        kept = [ref[pick, :] for ref in keep_refs]
        received = [ref[pick, :] for ref in recv_refs]
        query, output_grad = [jnp.where(at_encoder, r, k) for k, r in zip(kept, received)]
        keys, values = [jnp.where(at_encoder, k, r) for k, r in zip(kept, received)]
        meta = meta_ref[block].astype(F32)
        own_slot = (query_index >= meta[:1, 0:1]).astype(F32)
        key_end = jnp.where(key_slot > 0, meta[:1, 2:3] + ELEN, meta[:1, 1:2])
        allowed = (own_slot == key_slot) & (key_index < key_end)
        sums = None
        for head in range(2):
            mine = lane // HD == head
            query_head = jnp.where(mine, query, 0)
            grad_head = jnp.where(mine, output_grad, 0)
            scores = dot(query_head, keys, ((1,), (1,)))
            scores = jnp.where(allowed, scores, -1e30)
            exponent = jnp.exp(scores - jnp.max(scores, -1, keepdims=True))
            softmax_rows = exponent / jnp.sum(exponent, -1, keepdims=True)
            soft_low = softmax_rows.astype(BF)
            attended = dot(soft_low, values, ((1,), (0,))).astype(BF)
            row_delta = jnp.sum(grad_head.astype(F32) * attended.astype(F32), -1, keepdims=True)
            prob_grad = dot(grad_head, values, ((1,), (1,)))
            score_grad = (softmax_rows * (prob_grad - row_delta)).astype(BF)
            query_grad = dot(score_grad, keys, ((1,), (0,)))
            key_grad = dot(score_grad, query, ((0,), (0,)))
            value_grad = dot(soft_low, output_grad, ((0,), (0,)))
            grads = (query_grad, key_grad, value_grad)
            sums = grads if head == 0 else [jnp.where(mine, g, s) for g, s in zip(grads, sums)]
        query_grad, key_grad, value_grad = [g.astype(BF) for g in sums]
        empty = jnp.zeros_like(query_grad)
        stay_ref[0, pick, :] = jnp.where(at_encoder, key_grad, query_grad)
        stay_ref[1, pick, :] = jnp.where(at_encoder, value_grad, empty)
        send_ref[0, pick, :] = jnp.where(at_encoder, query_grad, key_grad)
        send_ref[1, pick, :] = jnp.where(at_encoder, empty, value_grad)


def attention(place, meta, keep, recv):
    shape = jax.ShapeDtypeStruct((2,) + keep[0].shape, BF)
    whole = pl.BlockSpec(memory_space=pltpu.VMEM)
    return pl.pallas_call(
        attention_kernel,
        out_shape=(shape, shape),
        in_specs=[pl.BlockSpec(memory_space=pltpu.SMEM)] + [whole] * 5,
        out_specs=(whole, whole),
        compiler_params=pltpu.CompilerParams(vmem_limit_bytes=8 * MIB),
    )(place, meta, *keep, *recv)


def swap_halves(even, odd, lane):
    low = lane < HD
    return (
        jnp.where(low, even, pltpu.roll(odd, HD, 1)),
        jnp.where(low, pltpu.roll(even, HD, 1), odd),
    )


def prepare_kernel(
    place_ref,
    lengths_ref,
    segments_ref,
    rows_ref,
    cotan_ref,
    gain_ref,
    square_ref,
    earlier_ref,
    inverse_ref,
    out_ref,
):
    at_encoder = place_ref[0] == 0
    row_count, half_width = rows_ref.shape
    inverse = lax.rsqrt(square_ref[...] / (2 * half_width) + EPS)
    inverse_ref[...] = inverse
    first_count = row_count - jnp.sum(segments_ref[...].astype(F32), -1, keepdims=True)
    at = lax.broadcasted_iota(jnp.int32, (META, half_width), 1)
    lengths = [lengths_ref[0, slot].astype(F32) for slot in range(2)]
    meta = jnp.where(at == 1, lengths[0], jnp.where(at == 2, lengths[1], 0.0))
    out_ref[pl.ds(2 * row_count, META), :] = jnp.where(at == 0, first_count, meta).astype(BF)
    tile = 2 * HD
    lane = lax.broadcasted_iota(jnp.int32, (row_count, tile), 1)
    step = half_width // 4
    for j in range(step // tile):
        for couple in range(2):
            normed, second = [], []
            for x in (2 * couple, 2 * couple + 1):
                pick = pl.ds(x * step + j * tile, tile)
                wide = rows_ref[:, pick].astype(F32) * inverse * gain_ref[:, pick].astype(F32)
                normed.append(wide)
                second.append(jnp.where(at_encoder, wide, cotan_ref[:, pick].astype(F32)))
            for part, pair in enumerate((normed, second)):
                for odd, moved in enumerate(swap_halves(*pair, lane)):
                    start = (2 * j + odd) * 4 * HD + couple * tile
                    out_ref[pl.ds(part * row_count, row_count), pl.ds(start, tile)] = moved.astype(BF)


def prepare(place, lengths, segments, rows, cotan, gain, square, earlier):
    whole = pl.BlockSpec(memory_space=pltpu.VMEM)
    scalars = pl.BlockSpec(memory_space=pltpu.SMEM)
    return pl.pallas_call(
        prepare_kernel,
        out_shape=(
            jax.ShapeDtypeStruct(square.shape, F32),
            jax.ShapeDtypeStruct((2 * rows.shape[0] + META, rows.shape[1]), BF),
        ),
        in_specs=[scalars, scalars] + [whole] * 5 + [pl.BlockSpec(memory_space=pl.ANY)],
        out_specs=(whole, whole),
        compiler_params=pltpu.CompilerParams(vmem_limit_bytes=5 * MIB),
    )(place, lengths, segments, rows, cotan, gain, square, earlier)


def join(refs, pick):
    return jnp.concatenate([ref[:, pick].astype(F32) for ref in refs], 0)


def finish_kernel(place_ref, rows_ref, cotan_ref, gain_ref, *refs):
    parts, (grad_ref, dot_ref) = refs[:-2], refs[-2:]
    keep_cotan = jnp.where(place_ref[0] == 0, 1.0, 0.0)
    row_count, half_width = rows_ref.shape
    tile = 2 * HD
    lane = lax.broadcasted_iota(jnp.int32, (row_count, tile), 1)
    step = half_width // 4
    total = jnp.zeros((row_count, tile), F32)
    for j in range(step // tile):
        for couple in range(2):
            pair = []
            for odd in range(2):
                pick = pl.ds((2 * j + odd) * 4 * HD + couple * tile, tile)
                pair.append(parts[0][:, pick] + join(parts[1:3], pick) + join(parts[3:5], pick))
            for odd, upstream in enumerate(swap_halves(*pair, lane)):
                pick = pl.ds((2 * couple + odd) * step + j * tile, tile)
                upstream = upstream + keep_cotan * cotan_ref[:, pick].astype(F32)
                gain_grad = gain_ref[:, pick].astype(F32) * upstream
                grad_ref[:, pick] = gain_grad
                total = total + rows_ref[:, pick].astype(F32) * gain_grad
    dot_ref[...] = jnp.sum(total, -1, keepdims=True)


def finish(place, rows, cotan, gain, parts):
    whole = pl.BlockSpec(memory_space=pltpu.VMEM)
    return pl.pallas_call(
        finish_kernel,
        out_shape=(
            jax.ShapeDtypeStruct(rows.shape, F32),
            jax.ShapeDtypeStruct((rows.shape[0], 1), F32),
        ),
        in_specs=[pl.BlockSpec(memory_space=pltpu.SMEM)] + [whole] * (3 + len(parts)),
        out_specs=(whole, whole),
        compiler_params=pltpu.CompilerParams(vmem_limit_bytes=8 * MIB),
    )(place, rows, cotan, gain, *parts)


def weight_copies(own_z, piece_refs, weight_ref, sems):
    z_size = weight_ref.shape[1]
    distances = [0]
    for step in range(1, z_size // 2):
        distances += [-step, step]
    pairs = [
        (ref, weight_ref.at[:, lax.rem(own_z + distance + z_size, z_size)])
        for ref, distance in zip(piece_refs, distances)
    ]
    far = lax.rem(own_z + z_size // 2, z_size)
    half = piece_refs[-1].shape[1]
    for at in range(2):
        pairs.append((piece_refs[at - 2], weight_ref.at[:, far, pl.ds(at * half, half)]))
    return [
        pltpu.make_async_copy(source, there, sems.at[at]) for at, (source, there) in enumerate(pairs)
    ]


def project_kernel(part, place_ref, gathered_ref, *refs):
    piece_refs = refs[:PIECES]
    own_ref, other_ref, meta_ref, weight_ref, left_ref, left_sems, sems = refs[PIECES:]
    blocks = gathered_ref.shape[0]
    rows = left_ref.shape[0] // blocks
    copies = []
    for at in range(blocks):
        source = gathered_ref.at[lax.rem(place_ref[2] + at, blocks)]
        there = left_ref.at[pl.ds(at * rows, rows)]
        copies.append((source.at[pl.ds(part * rows, rows)], there, left_sems.at[0, at]))
        meta = source.at[pl.ds(2 * rows, META), pl.ds(0, 2 * HD)]
        copies.append((meta, meta_ref.at[at], left_sems.at[1, at]))
    copies = [pltpu.make_async_copy(*copy) for copy in copies]
    copies += weight_copies(place_ref[1], piece_refs, weight_ref, sems)
    for copy in copies:
        copy.start()
    for copy in copies:
        copy.wait()
    half = own_ref.shape[2]
    z_size, depth, width = weight_ref.shape[1:]
    for columns, out_ref in enumerate((own_ref, other_ref)):
        weights = weight_ref[columns].reshape(z_size * depth, width)
        product = dot(left_ref[...], weights, ((1,), (0,)))
        for at in range(2):
            out_ref[at] = product[:, at * half : (at + 1) * half].astype(out_ref.dtype)


def project(part, place, gathered, pieces):
    blocks, rows, width = gathered.shape
    rows = (rows - META) // 2
    _, depth, columns = pieces[0].shape
    shape = (2, blocks * rows, columns // 2)
    whole = pl.BlockSpec(memory_space=pltpu.VMEM)
    return pl.pallas_call(
        functools.partial(project_kernel, part),
        out_shape=(
            jax.ShapeDtypeStruct(shape, F32),
            jax.ShapeDtypeStruct(shape, BF),
            jax.ShapeDtypeStruct((blocks, META, 2 * HD), BF),
            jax.ShapeDtypeStruct((2, width // depth, depth, columns), BF),
        ),
        in_specs=[pl.BlockSpec(memory_space=pltpu.SMEM)]
        + [pl.BlockSpec(memory_space=pltpu.HBM)] * (1 + len(pieces)),
        out_specs=(whole, whole, whole, whole),
        scratch_shapes=[
            pltpu.VMEM((blocks * rows, width), BF),
            pltpu.SemaphoreType.DMA((2, blocks)),
            pltpu.SemaphoreType.DMA((PIECES,)),
        ],
        compiler_params=pltpu.CompilerParams(vmem_limit_bytes=56 * MIB),
    )(place, gathered, *pieces)


def back_kernel(place_ref, *refs):
    grad_refs, weight_refs = refs[:4], refs[4:6]
    own_ref, near_ref, far_ref, last_ref = refs[6:]
    at_encoder = place_ref[0] == 0
    rows = own_ref.shape[0]
    grads = []
    for part in range(2):
        for columns in range(2):
            stay, back = grad_refs[2 * columns][part], grad_refs[2 * columns + 1][part]
            low = jnp.where(at_encoder, stay, back)
            high = jnp.where(at_encoder, back, stay)
            grads.append((part, columns, jnp.concatenate([low, high], 1)))
    z_size, depth = weight_refs[0].shape[1:3]
    for z in range(z_size):
        total = 0.0
        for part, columns, grad in grads:
            total += dot(grad, weight_refs[part][columns, z], ((1,), (1,)))
        pick = pl.ds(z * depth, depth)
        for at, ref in enumerate((own_ref, near_ref, far_ref, last_ref)):
            ref[:, pick] = total[at * rows : (at + 1) * rows].astype(ref.dtype)


def back_project(place, grads, weights, shape):
    whole = pl.BlockSpec(memory_space=pltpu.VMEM)
    return pl.pallas_call(
        back_kernel,
        out_shape=[jax.ShapeDtypeStruct(shape, kind) for kind in (F32, F32, BF, F32)],
        in_specs=[pl.BlockSpec(memory_space=pltpu.SMEM)] + [whole] * (len(grads) + len(weights)),
        out_specs=[whole] * 4,
        compiler_params=pltpu.CompilerParams(vmem_limit_bytes=16 * MIB),
    )(place, *grads, *weights)


def exchange_columns(weights):
    rows, parts, columns = weights.shape
    x_size = lax.axis_size("x")
    slices = weights.reshape(rows, parts, x_size, columns // x_size).transpose(2, 1, 0, 3)
    return lax.all_to_all(slices, "x", 0, 0, tiled=True)


def gather_weights(chunk, own_y, own_c):
    x_size, rows, columns = chunk.shape
    z_size = lax.axis_size("z")
    at_source = own_y == own_c
    near = lax.ppermute(chunk, ("y", "mp"), [(1, 0), (2, 3), (0, 2), (3, 1)])
    far = lax.ppermute(chunk, ("y", "mp"), [(1, 2), (2, 1)])
    merged = jnp.stack([jnp.where(at_source, chunk, near), jnp.where(at_source, near, far)], 0)
    up = down = merged.reshape(2, x_size * rows, columns)
    pieces = [up]
    for step in range(1, z_size // 2):
        up, down = shift(up, "z", 1), shift(down, "z", -1)
        pieces += [up, down]
    half = x_size * rows // 2
    return pieces + [shift(up[:, :half], "z", 1), shift(down[:, half:], "z", -1)]


def sum_over_x(own, near, far, last):
    half = own.shape[0] // 2
    up, down = shift(far[:half], "x", 1), shift(far[half:], "x", -1)
    below_rest = shift(near[half:].astype(BF), "x", 1)
    above_rest = shift(last[:half].astype(BF), "x", -1)
    below = shift((near[:half] + up.astype(F32)).astype(BF), "x", 1)
    above = shift((last[half:] + down.astype(F32)).astype(BF), "x", -1)
    return own, below, below_rest, above_rest, above


def on_device(section_rows, norm_gains, proj_weights, section_cotan, enc_lengths, dec_segments):
    side = lax.axis_index("section")
    own_y, own_z, own_c = (lax.axis_index(a) for a in ("y", "z", "mp"))
    at_encoder = side == 0
    rows, cotan, weights = section_rows[0], section_cotan[0], proj_weights[0]
    row_count, half_width = rows.shape
    width = 2 * half_width
    place = jnp.stack([side, own_z, lax.axis_index("x")])
    wide_rows = rows.astype(F32)

    square = jnp.sum(wide_rows * wide_rows, -1, keepdims=True)
    square = square + shift(square, "mp", 1)
    chunks = exchange_columns(weights)
    inverse, left = prepare(
        place, enc_lengths, dec_segments, rows, cotan, norm_gains, square, chunks
    )
    gathered = lax.all_gather(left, "x")
    pieces = [gather_weights(chunks[:, part], own_y, own_c) for part in range(2)]

    keep, recv, full = [], [], []
    for part in range(2):
        own, other, meta, assembled = project(part, place, gathered, pieces[part])
        full.append(assembled)
        other = shift(other, "mp", 1)

        def half(at):
            picked = [lax.dynamic_index_in_dim(whole, at, 0, False) for whole in (own, other)]
            return (picked[0] + picked[1].astype(F32)).astype(BF)

        recv.append(shift(half(1 - side), "section", 1))
        keep.append(half(side))
    stay, back = attention(place, meta, keep, recv)
    back = shift(back, "section", 1)
    grads = (stay, back, shift(stay, "mp", 1), shift(back, "mp", 1))
    parts = sum_over_x(*back_project(place, grads, full, rows.shape))
    gain_grad, row_dot = finish(place, rows, cotan, norm_gains, parts)
    row_dot = (row_dot + shift(row_dot, "mp", 1)) / width
    result = inverse * gain_grad - wide_rows * inverse**3 * row_dot
    return (result + jnp.where(at_encoder, 0.0, cotan.astype(F32)))[None]


def solution(mesh):
    names = ("section", "y", "x", "z", "mp")
    split = Mesh(mesh.devices.reshape(2, 2, 4, 8, 2), names)
    fsdp = ("y", "x", "z")
    return jax.shard_map(
        on_device,
        mesh=split,
        in_specs=(
            P("section", fsdp, "mp"),
            P("section", "mp"),
            P("section", fsdp, None, "mp"),
            P("section", fsdp, "mp"),
            P(fsdp, None),
            P(fsdp, None),
        ),
        out_specs=P("section", fsdp, "mp"),
        check_vma=False,
    )
```

time: 180 us -> 159 us (0.88)
  waiting for transfers between devices: 80.5 us -> 56 us
  Pallas kernels: 5.52 us -> 22 us
  between operations: 1.2 us -> 13.8 us
  matrix products: 12.2 us -> 0 us
  blocking collectives: 7.32 us -> 0 us
  starting transfers between devices: 59.3 us -> 53.6 us
    ppermute x30 -> x31, waiting for transfers between devices: 80.5 us -> 51.8 us  [shift(): lax.ppermute(block, axis, [(i, (i + distance) % size) for i in range(size)])]
    pallas_call x1 -> x6, Pallas kernels: 5.52 us -> 22 us  [the longest x2 10.2 us: project(): pl.pallas_call(functools.partial(project_kernel, part), out_shape=(jax.Sh...]
    ppermute x30 -> x31, starting transfers between devices: 51.6 us -> 39.4 us  [shift(): lax.ppermute(block, axis, [(i, (i + distance) % size) for i in range(size)])]
    dot_general x20 -> x0, matrix products: 12.2 us -> none  [dot(): lax.dot_general(left, right, (contract, ((), ())), preferred_element_type...]
    unnamed x1 -> x0, blocking collectives: 7.32 us -> none
    ppermute x4, starting transfers between devices: 2.85 us -> 9.32 us  [the longest x2 5.55 us: gather_weights(): far = lax.ppermute(chunk, ('y', 'mp'), [(1, 2), (2, 1)])]
    ppermute x4, waiting for transfers between devices: 0.01 us -> 2.91 us  [the longest x2 2.9 us: gather_weights(): far = lax.ppermute(chunk, ('y', 'mp'), [(1, 2), (2, 1)])]
  transfers between devices with their start and end apart: 35 -> 37, of which waited for: 16 -> 20; matrix products, arithmetic and copies ran while one was open for 12% -> 4% of each run, Pallas kernels for 3% -> 6%
where the time goes in v2:
time: 159 us; the launch traced here: 158 us
  waiting for transfers between devices  56 us (35%)
  starting transfers between devices  53.6 us (34%)
  Pallas kernels  22 us (14%)
  between operations  13.8 us (9%)
  local copies, waits for them, and re-layouts  7.16 us (5%)
  other arithmetic  5.54 us (3%)
    ppermute x31, waiting for transfers between devices, shift(): lax.ppermute(block, axis, [(i, (i + distance) % size) for i in range(size)])  51.8 us
    ppermute x31, starting transfers between devices, shift(): lax.ppermute(block, axis, [(i, (i + distance) % size) for i in range(size)])  39.4 us
    pallas_call x2, Pallas kernels, project(): pl.pallas_call(functools.partial(project_kernel, part), out_shape=(jax.Sh...  10.2 us
    ppermute x2, starting transfers between devices, gather_weights(): far = lax.ppermute(chunk, ('y', 'mp'), [(1, 2), (2, 1)])  5.55 us
    pallas_call x1, Pallas kernels, attention(): pl.pallas_call(attention_kernel, out_shape=(shape, shape), in_specs=[pl.B...  5.53 us
    all_to_all x1, starting transfers between devices, exchange_columns(): return lax.all_to_all(slices, 'x', 0, 0, tiled=True)  4.84 us
    ppermute x2, starting transfers between devices, gather_weights(): near = lax.ppermute(chunk, ('y', 'mp'), [(1, 0), (2, 3), (0, 2), (3, 1)])  3.77 us
    unnamed x54, local copies, waits for them, and re-layouts  3.56 us
  transfers between devices with their start and end apart: 37, of which 20 were waited for; matrix products, arithmetic and copies ran while one was open for 4% of the time, Pallas kernels for 6%

profile of v2, /device:TPU:1, one launch (start us, length us, event | category | flops | bytes accessed | tf_op | source)
XLA Modules:
  0.0 158.1 jit_solution(17798095195973393785)
XLA Ops:
  8.5 4.8 %all-to-all-start = ((bf16[4,2,64,256]{3,2,1,0:T(8,128)(2,1)}), bf16[4,2,64,256]{3,2,1,0:T(8,128)(2,1)S(1)}, u32[]{:S(2)}, u32[]{:S(2)}) async-start(bf16[4,2,64,256]{3,2,1,0:T(8,128)(2,1)} %bitcast.36), calls=%async_computation | async-start | bytes 524288 | tf_op jit(solution)/shard_map/all_to_all | solution.py:298
  18.9 2.2 %shard_map.64 = (f32[128,1]{1,0:T(8,128)S(1)}, bf16[272,2048]{1,0:T(8,128)(2,1)}) custom-call(s32[3]{0:T(128)S(1)} %pad_add_fusion.place_ref, s32[1,2]{1,0:T(1,128)S(1)} %copy-done.10, s32[1,128]{1,0:T(1,128)S(1)} %copy-done.11, bf16[128,2048]{1,0:T(8,128)(2,1)S(1)} %bitcast.37, bf16[128,2048]{1,0:T(8,128)(2,1)S(1)} %bitcast.39, ...), custom_call_target="tpu_custom_call" | custom-call | tf_op jit(solution)/shard_map/pallas_call | solution.py:137
  21.1 3.0 %collective-permute-start.1 = (bf16[4,64,256]{2,1,0:T(8,128)(2,1)S(1)}, bf16[4,64,256]{2,1,0:T(8,128)(2,1)S(1)}, u32[]{:S(2)}, u32[]{:S(2)}) collective-permute-start(bf16[4,64,256]{2,1,0:T(8,128)(2,1)S(1)} %get-tuple-element.50), channel_id=1, source_target_pairs={{1,0},{64,65},{0,64},{65,1},{3,2},{66,67},{2,66},{67,3},{5,4},{68,... | collective-permute-start | bytes 393224 | tf_op jit(solution)/shard_map/ppermute | solution.py:305
  26.8 3.6 %collective-permute-start.2 = (bf16[4,64,256]{2,1,0:T(8,128)(2,1)S(1)}, bf16[4,64,256]{2,1,0:T(8,128)(2,1)S(1)}, u32[]{:S(2)}, u32[]{:S(2)}) collective-permute-start(bf16[4,64,256]{2,1,0:T(8,128)(2,1)S(1)} %get-tuple-element.50), channel_id=1, source_target_pairs={{1,64},{64,1},{3,66},{66,3},{5,68},{68,5},{7,70},{70,7},{9,72},{72... | collective-permute-start | bytes 393224 | tf_op jit(solution)/shard_map/ppermute | solution.py:306
  31.2 2.2 %collective-permute-done.2 = bf16[4,64,256]{2,1,0:T(8,128)(2,1)S(1)} collective-permute-done((bf16[4,64,256]{2,1,0:T(8,128)(2,1)S(1)}, bf16[4,64,256]{2,1,0:T(8,128)(2,1)S(1)}, u32[]{:S(2)}, u32[]{:S(2)}) %collective-permute-start.2) | collective-permute-done | bytes 131104 | tf_op jit(solution)/shard_map/ppermute | solution.py:306
  33.5 5.4 %collective-permute-start.4 = (bf16[2,256,256]{2,1,0:T(8,128)(2,1)S(1)}, bf16[2,256,256]{2,1,0:T(8,128)(2,1)S(1)}, u32[]{:S(2)}, u32[]{:S(2)}) collective-permute-start(bf16[2,256,256]{2,1,0:T(8,128)(2,1)S(1)} %pad_maximum_fusion.refs_0_), channel_id=1, source_target_pairs={{0,14},{2,0},{4,2},{6,4},{8,6},{10,8},{12,10},{14,12},{1,15},{3,1}... | collective-permute-start | bytes 786440 | tf_op jit(solution)/shard_map/ppermute | solution.py:23
  39.0 2.7 %collective-permute-start.14 = (bf16[2,256,256]{2,1,0:T(8,128)(2,1)S(1)}, bf16[2,256,256]{2,1,0:T(8,128)(2,1)S(1)}, u32[]{:S(2)}, u32[]{:S(2)}) collective-permute-start(bf16[2,256,256]{2,1,0:T(8,128)(2,1)S(1)} %pad_maximum_fusion.1.refs_0_), channel_id=1, source_target_pairs={{0,14},{2,0},{4,2},{6,4},{8,6},{10,8},{12,10},{14,12},{1,15},{3,1}... | collective-permute-start | bytes 786440 | tf_op jit(solution)/shard_map/ppermute | solution.py:23
  41.7 2.7 %collective-permute-done.4.refs_2_ = bf16[2,256,256]{2,1,0:T(8,128)(2,1)S(1)} collective-permute-done((bf16[2,256,256]{2,1,0:T(8,128)(2,1)S(1)}, bf16[2,256,256]{2,1,0:T(8,128)(2,1)S(1)}, u32[]{:S(2)}, u32[]{:S(2)}) %collective-permute-start.4) | collective-permute-done | bytes 262176 | tf_op jit(solution)/shard_map/ppermute | solution.py:23
  44.4 3.5 %collective-permute-start.6 = (bf16[2,256,256]{2,1,0:T(8,128)(2,1)S(1)}, bf16[2,256,256]{2,1,0:T(8,128)(2,1)S(1)}, u32[]{:S(2)}, u32[]{:S(2)}) collective-permute-start(bf16[2,256,256]{2,1,0:T(8,128)(2,1)S(1)} %collective-permute-done.4.refs_2_), channel_id=1, source_target_pairs={{0,14},{2,0},{4,2},{6,4},{8,6},{10,8},{12,10},{14,12},{1,15},{3,1}... | collective-permute-start | bytes 786440 | tf_op jit(solution)/shard_map/ppermute | solution.py:23
  48.6 5.6 %collective-permute-done.13.refs_1_ = bf16[2,256,256]{2,1,0:T(8,128)(2,1)S(1)} collective-permute-done((bf16[2,256,256]{2,1,0:T(8,128)(2,1)S(1)}, bf16[2,256,256]{2,1,0:T(8,128)(2,1)S(1)}, u32[]{:S(2)}, u32[]{:S(2)}) %collective-permute-start.13) | collective-permute-done | bytes 262176 | tf_op jit(solution)/shard_map/ppermute | solution.py:23
  54.2 2.7 %collective-permute-start.16 = (bf16[2,256,256]{2,1,0:T(8,128)(2,1)S(1)}, bf16[2,256,256]{2,1,0:T(8,128)(2,1)S(1)}, u32[]{:S(2)}, u32[]{:S(2)}) collective-permute-start(bf16[2,256,256]{2,1,0:T(8,128)(2,1)S(1)} %collective-permute-done.14.refs_2_), channel_id=1, source_target_pairs={{0,14},{2,0},{4,2},{6,4},{8,6},{10,8},{12,10},{14,12},{1,15},{3,1}... | collective-permute-start | bytes 786440 | tf_op jit(solution)/shard_map/ppermute | solution.py:23
  57.1 2.7 %collective-permute-done.5.refs_3_ = bf16[2,256,256]{2,1,0:T(8,128)(2,1)S(1)} collective-permute-done((bf16[2,256,256]{2,1,0:T(8,128)(2,1)S(1)}, bf16[2,256,256]{2,1,0:T(8,128)(2,1)S(1)}, u32[]{:S(2)}, u32[]{:S(2)}) %collective-permute-start.5) | collective-permute-done | bytes 262176 | tf_op jit(solution)/shard_map/ppermute | solution.py:23
  59.8 5.6 %collective-permute-done.15.refs_3_ = bf16[2,256,256]{2,1,0:T(8,128)(2,1)S(1)} collective-permute-done((bf16[2,256,256]{2,1,0:T(8,128)(2,1)S(1)}, bf16[2,256,256]{2,1,0:T(8,128)(2,1)S(1)}, u32[]{:S(2)}, u32[]{:S(2)}) %collective-permute-start.15) | collective-permute-done | bytes 262176 | tf_op jit(solution)/shard_map/ppermute | solution.py:23
  65.5 2.7 %collective-permute-start.18 = (bf16[2,256,256]{2,1,0:T(8,128)(2,1)S(1)}, bf16[2,256,256]{2,1,0:T(8,128)(2,1)S(1)}, u32[]{:S(2)}, u32[]{:S(2)}) collective-permute-start(bf16[2,256,256]{2,1,0:T(8,128)(2,1)S(1)} %collective-permute-done.16.refs_4_), channel_id=1, source_target_pairs={{0,14},{2,0},{4,2},{6,4},{8,6},{10,8},{12,10},{14,12},{1,15},{3,1}... | collective-permute-start | bytes 786440 | tf_op jit(solution)/shard_map/ppermute | solution.py:23
  68.3 2.7 %collective-permute-done.7.refs_5_ = bf16[2,256,256]{2,1,0:T(8,128)(2,1)S(1)} collective-permute-done((bf16[2,256,256]{2,1,0:T(8,128)(2,1)S(1)}, bf16[2,256,256]{2,1,0:T(8,128)(2,1)S(1)}, u32[]{:S(2)}, u32[]{:S(2)}) %collective-permute-start.7) | collective-permute-done | bytes 262176 | tf_op jit(solution)/shard_map/ppermute | solution.py:23
  71.1 4.3 %collective-permute-done.17.refs_5_ = bf16[2,256,256]{2,1,0:T(8,128)(2,1)S(1)} collective-permute-done((bf16[2,256,256]{2,1,0:T(8,128)(2,1)S(1)}, bf16[2,256,256]{2,1,0:T(8,128)(2,1)S(1)}, u32[]{:S(2)}, u32[]{:S(2)}) %collective-permute-start.17) | collective-permute-done | bytes 262176 | tf_op jit(solution)/shard_map/ppermute | solution.py:23
  76.9 2.7 %collective-permute-start.20 = (bf16[2,128,256]{2,1,0:T(8,128)(2,1)}, bf16[2,128,256]{2,1,0:T(8,128)(2,1)}, u32[]{:S(2)}, u32[]{:S(2)}) collective-permute-start(bf16[2,128,256]{2,1,0:T(8,128)(2,1)} %slice.55), channel_id=1, source_target_pairs={{0,14},{2,0},{4,2},{6,4},{8,6},{10,8},{12,10},{14,12},{1,15},{3,1}... | collective-permute-start | bytes 393224 | tf_op jit(solution)/shard_map/ppermute | solution.py:23
  80.2 5.1 %shard_map.65 = (f32[2,512,128]{2,1,0:T(8,128)}, bf16[2,512,128]{2,1,0:T(8,128)(2,1)}, bf16[4,16,128]{2,1,0:T(8,128)(2,1)}, bf16[2,8,256,256]{3,2,1,0:T(8,128)(2,1)}) custom-call(s32[3]{0:T(128)} %copy-done.7, bf16[4,272,2048]{2,1,0:T(8,128)(2,1)} %bitcast.41, bf16[2,256,256]{2,1,0:T(8,128)(2,1)} %copy-done.13, bf16[2,256,256]{2,1,0:T(8,128)(2,1)} %copy-done.21, ...), custom_call_target="tpu_custom_call" | custom-call | tf_op jit(solution)/shard_map/pallas_call | solution.py:241
  85.5 5.1 %shard_map.66 = (f32[2,512,128]{2,1,0:T(8,128)}, bf16[2,512,128]{2,1,0:T(8,128)(2,1)}, bf16[4,16,128]{2,1,0:T(8,128)(2,1)}, bf16[2,8,256,256]{3,2,1,0:T(8,128)(2,1)}) custom-call(s32[3]{0:T(128)} %copy-done.7, bf16[4,272,2048]{2,1,0:T(8,128)(2,1)} %bitcast.42, bf16[2,256,256]{2,1,0:T(8,128)(2,1)} %copy-done.12, bf16[2,256,256]{2,1,0:T(8,128)(2,1)} %copy-done.18, ...), custom_call_target="tpu_custom_call" | custom-call | tf_op jit(solution)/shard_map/pallas_call | solution.py:241
  92.4 2.7 %collective-permute-start.24 = (bf16[512,128]{1,0:T(8,128)(2,1)S(1)}, bf16[512,128]{1,0:T(8,128)(2,1)S(1)}, u32[]{:S(2)}, u32[]{:S(2)}) collective-permute-start(bf16[512,128]{1,0:T(8,128)(2,1)S(1)} %get-tuple-element.41), channel_id=1, source_target_pairs={{0,128},{128,0},{1,129},{129,1},{2,130},{130,2},{3,131},{131,3},{4... | collective-permute-start | bytes 393224 | tf_op jit(solution)/shard_map/ppermute | solution.py:23
  96.8 2.3 %collective-permute-done.24.refs_3_ = bf16[512,128]{1,0:T(8,128)(2,1)S(1)} collective-permute-done((bf16[512,128]{1,0:T(8,128)(2,1)S(1)}, bf16[512,128]{1,0:T(8,128)(2,1)S(1)}, u32[]{:S(2)}, u32[]{:S(2)}) %collective-permute-start.24) | collective-permute-done | bytes 131104 | tf_op jit(solution)/shard_map/ppermute | solution.py:23
  99.1 3.6 %collective-permute-done.23.refs_2_ = bf16[512,128]{1,0:T(8,128)(2,1)S(1)} collective-permute-done((bf16[512,128]{1,0:T(8,128)(2,1)S(1)}, bf16[512,128]{1,0:T(8,128)(2,1)S(1)}, u32[]{:S(2)}, u32[]{:S(2)}) %collective-permute-start.23) | collective-permute-done | bytes 131104 | tf_op jit(solution)/shard_map/ppermute | solution.py:23
  102.6 5.5 %shard_map.67 = (bf16[2,512,128]{2,1,0:T(8,128)(2,1)S(1)}, bf16[2,512,128]{2,1,0:T(8,128)(2,1)S(1)}) custom-call(s32[3]{0:T(128)S(1)} %copy-done.8, bf16[4,16,128]{2,1,0:T(8,128)(2,1)S(1)} %copy-done.9, bf16[512,128]{1,0:T(8,128)(2,1)S(1)} %get-tuple-element.44.refs_0_, bf16[512,128]{1,0:T(8,128)(2,1)S(1)} %get-tuple-element.42.refs_1_, ...), custom_call_target="tpu_custom_call" | custom-call | tf_op jit(solution)/shard_map/pallas_call | solution.py:79
  108.2 2.0 %collective-permute-start.25 = (bf16[2,512,128]{2,1,0:T(8,128)(2,1)S(1)}, bf16[2,512,128]{2,1,0:T(8,128)(2,1)S(1)}, u32[]{:S(2)}, u32[]{:S(2)}) collective-permute-start(bf16[2,512,128]{2,1,0:T(8,128)(2,1)S(1)} %get-tuple-element.30), channel_id=1, source_target_pairs={{0,128},{128,0},{1,129},{129,1},{2,130},{130,2},{3,131},{131,3},{4... | collective-permute-start | bytes 786440 | tf_op jit(solution)/shard_map/ppermute | solution.py:23
  111.3 5.1 %collective-permute-done.25.refs_1_ = bf16[2,512,128]{2,1,0:T(8,128)(2,1)S(1)} collective-permute-done((bf16[2,512,128]{2,1,0:T(8,128)(2,1)S(1)}, bf16[2,512,128]{2,1,0:T(8,128)(2,1)S(1)}, u32[]{:S(2)}, u32[]{:S(2)}) %collective-permute-start.25) | collective-permute-done | bytes 262176 | tf_op jit(solution)/shard_map/ppermute | solution.py:23
  116.4 2.1 %collective-permute-start.27 = (bf16[2,512,128]{2,1,0:T(8,128)(2,1)S(1)}, bf16[2,512,128]{2,1,0:T(8,128)(2,1)S(1)}, u32[]{:S(2)}, u32[]{:S(2)}) collective-permute-start(bf16[2,512,128]{2,1,0:T(8,128)(2,1)S(1)} %collective-permute-done.25.refs_1_), channel_id=1, source_target_pairs={{0,1},{1,0},{2,3},{3,2},{4,5},{5,4},{6,7},{7,6},{8,9},{9,8},{10,11... | collective-permute-start | bytes 786440 | tf_op jit(solution)/shard_map/ppermute | solution.py:23
  121.2 2.9 %shard_map.68 = (f32[128,2048]{1,0:T(8,128)S(1)}, f32[128,2048]{1,0:T(8,128)S(1)}, bf16[128,2048]{1,0:T(8,128)(2,1)S(1)}, f32[128,2048]{1,0:T(8,128)S(1)}) custom-call(s32[3]{0:T(128)S(1)} %copy-done.8, bf16[2,512,128]{2,1,0:T(8,128)(2,1)S(1)} %get-tuple-element.29.refs_0_, bf16[2,512,128]{2,1,0:T(8,128)(2,1)S(1)} %collective-permute-done.25.refs_1_, ...), custom_call_target="tpu_custom_call" | custom-call | tf_op jit(solution)/shard_map/pallas_call | solution.py:285
  125.9 2.7 %collective-permute-start.31 = (bf16[64,2048]{1,0:T(8,128)(2,1)S(1)}, bf16[64,2048]{1,0:T(8,128)(2,1)S(1)}, u32[]{:S(2)}, u32[]{:S(2)}) collective-permute-start(bf16[64,2048]{1,0:T(8,128)(2,1)S(1)} %slice.68), channel_id=1, source_target_pairs={{0,48},{16,0},{32,16},{48,32},{1,49},{17,1},{33,17},{49,33},{2,50}... | collective-permute-start | bytes 786440 | tf_op jit(solution)/shard_map/ppermute | solution.py:23
  128.7 3.2 %collective-permute-done.32 = bf16[64,2048]{1,0:T(8,128)(2,1)S(1)} collective-permute-done((bf16[64,2048]{1,0:T(8,128)(2,1)S(1)}, bf16[64,2048]{1,0:T(8,128)(2,1)S(1)}, u32[]{:S(2)}, u32[]{:S(2)}) %collective-permute-start.32) | collective-permute-done | bytes 262176 | tf_op jit(solution)/shard_map/ppermute | solution.py:23
  131.9 2.2 %collective-permute-start.33 = (bf16[64,2048]{1,0:T(8,128)(2,1)S(1)}, bf16[64,2048]{1,0:T(8,128)(2,1)S(1)}, u32[]{:S(2)}, u32[]{:S(2)}) collective-permute-start(bf16[64,2048]{1,0:T(8,128)(2,1)S(1)} %add_convert_fusion), channel_id=1, source_target_pairs={{0,48},{16,0},{32,16},{48,32},{1,49},{17,1},{33,17},{49,33},{2,50}... | collective-permute-start | bytes 786440 | tf_op jit(solution)/shard_map/ppermute | solution.py:23
  134.2 5.0 %collective-permute-done.30.refs_2_ = bf16[64,2048]{1,0:T(8,128)(2,1)S(1)} collective-permute-done((bf16[64,2048]{1,0:T(8,128)(2,1)S(1)}, bf16[64,2048]{1,0:T(8,128)(2,1)S(1)}, u32[]{:S(2)}, u32[]{:S(2)}) %collective-permute-start.30) | collective-permute-done | bytes 262176 | tf_op jit(solution)/shard_map/ppermute | solution.py:23
  139.2 3.8 %collective-permute-done.33.refs_4_ = bf16[64,2048]{1,0:T(8,128)(2,1)S(1)} collective-permute-done((bf16[64,2048]{1,0:T(8,128)(2,1)S(1)}, bf16[64,2048]{1,0:T(8,128)(2,1)S(1)}, u32[]{:S(2)}, u32[]{:S(2)}) %collective-permute-start.33) | collective-permute-done | bytes 262176 | tf_op jit(solution)/shard_map/ppermute | solution.py:23
  (127 shorter events, 31.8 us)
Async XLA Ops:
  8.5 10.4 %all-to-all-start = ((bf16[4,2,64,256]{3,2,1,0:T(8,128)(2,1)}), bf16[4,2,64,256]{3,2,1,0:T(8,128)(2,1)S(1)}, u32[]{:S(2)}, u32[]{:S(2)}) async-start(bf16[4,2,64,256]{3,2,1,0:T(8,128)(2,1)} %bitcast.36), calls=%async_computation | async-start | bytes 524288 | tf_op jit(solution)/shard_map/all_to_all | solution.py:298
  13.4 66.9 %all-gather.3.cloned.1.call-start = ((), (), s32[]{:S(2)}) async-start(), calls=%async_computation.1 | async-start | bytes 5570560 | tf_op jit(solution)/shard_map/all_gather | solution.py:343
  21.1 9.3 %collective-permute-start.1 = (bf16[4,64,256]{2,1,0:T(8,128)(2,1)S(1)}, bf16[4,64,256]{2,1,0:T(8,128)(2,1)S(1)}, u32[]{:S(2)}, u32[]{:S(2)}) collective-permute-start(bf16[4,64,256]{2,1,0:T(8,128)(2,1)S(1)} %get-tuple-element.50), channel_id=1, source_target_pairs={{1,0},{64,65},{0,64},{65,1},{3,2},{66,67},{2,66},{67,3},{5,4},{68,... | collective-permute-start | bytes 393224 | tf_op jit(solution)/shard_map/ppermute | solution.py:305
  24.1 6.3 %collective-permute-start.11 = (bf16[4,64,256]{2,1,0:T(8,128)(2,1)S(1)}, bf16[4,64,256]{2,1,0:T(8,128)(2,1)S(1)}, u32[]{:S(2)}, u32[]{:S(2)}) collective-permute-start(bf16[4,64,256]{2,1,0:T(8,128)(2,1)S(1)} %get-tuple-element.49), channel_id=1, source_target_pairs={{1,0},{64,65},{0,64},{65,1},{3,2},{66,67},{2,66},{67,3},{5,4},{68,... | collective-permute-start | bytes 393224 | tf_op jit(solution)/shard_map/ppermute | solution.py:305
  24.9 6.3 %collective-permute-start.12 = (bf16[4,64,256]{2,1,0:T(8,128)(2,1)S(1)}, bf16[4,64,256]{2,1,0:T(8,128)(2,1)S(1)}, u32[]{:S(2)}, u32[]{:S(2)}) collective-permute-start(bf16[4,64,256]{2,1,0:T(8,128)(2,1)S(1)} %get-tuple-element.49), channel_id=1, source_target_pairs={{1,64},{64,1},{3,66},{66,3},{5,68},{68,5},{7,70},{70,7},{9,72},{72... | collective-permute-start | bytes 393224 | tf_op jit(solution)/shard_map/ppermute | solution.py:306
  26.8 6.6 %collective-permute-start.2 = (bf16[4,64,256]{2,1,0:T(8,128)(2,1)S(1)}, bf16[4,64,256]{2,1,0:T(8,128)(2,1)S(1)}, u32[]{:S(2)}, u32[]{:S(2)}) collective-permute-start(bf16[4,64,256]{2,1,0:T(8,128)(2,1)S(1)} %get-tuple-element.50), channel_id=1, source_target_pairs={{1,64},{64,1},{3,66},{66,3},{5,68},{68,5},{7,70},{70,7},{9,72},{72... | collective-permute-start | bytes 393224 | tf_op jit(solution)/shard_map/ppermute | solution.py:306
  33.5 10.9 %collective-permute-start.4 = (bf16[2,256,256]{2,1,0:T(8,128)(2,1)S(1)}, bf16[2,256,256]{2,1,0:T(8,128)(2,1)S(1)}, u32[]{:S(2)}, u32[]{:S(2)}) collective-permute-start(bf16[2,256,256]{2,1,0:T(8,128)(2,1)S(1)} %pad_maximum_fusion.refs_0_), channel_id=1, source_target_pairs={{0,14},{2,0},{4,2},{6,4},{8,6},{10,8},{12,10},{14,12},{1,15},{3,1}... | collective-permute-start | bytes 786440 | tf_op jit(solution)/shard_map/ppermute | solution.py:23
  38.9 9.7 %collective-permute-start.3 = (bf16[2,256,256]{2,1,0:T(8,128)(2,1)S(1)}, bf16[2,256,256]{2,1,0:T(8,128)(2,1)S(1)}, u32[]{:S(2)}, u32[]{:S(2)}) collective-permute-start(bf16[2,256,256]{2,1,0:T(8,128)(2,1)S(1)} %pad_maximum_fusion.refs_0_), channel_id=1, source_target_pairs={{0,2},{2,4},{4,6},{6,8},{8,10},{10,12},{12,14},{14,0},{1,3},{3,5},... | collective-permute-start | bytes 786440 | tf_op jit(solution)/shard_map/ppermute | solution.py:23
  38.9 15.3 %collective-permute-start.13 = (bf16[2,256,256]{2,1,0:T(8,128)(2,1)S(1)}, bf16[2,256,256]{2,1,0:T(8,128)(2,1)S(1)}, u32[]{:S(2)}, u32[]{:S(2)}) collective-permute-start(bf16[2,256,256]{2,1,0:T(8,128)(2,1)S(1)} %pad_maximum_fusion.1.refs_0_), channel_id=1, source_target_pairs={{0,2},{2,4},{4,6},{6,8},{8,10},{10,12},{12,14},{14,0},{1,3},{3,5},... | collective-permute-start | bytes 786440 | tf_op jit(solution)/shard_map/ppermute | solution.py:23
  39.0 15.2 %collective-permute-start.14 = (bf16[2,256,256]{2,1,0:T(8,128)(2,1)S(1)}, bf16[2,256,256]{2,1,0:T(8,128)(2,1)S(1)}, u32[]{:S(2)}, u32[]{:S(2)}) collective-permute-start(bf16[2,256,256]{2,1,0:T(8,128)(2,1)S(1)} %pad_maximum_fusion.1.refs_0_), channel_id=1, source_target_pairs={{0,14},{2,0},{4,2},{6,4},{8,6},{10,8},{12,10},{14,12},{1,15},{3,1}... | collective-permute-start | bytes 786440 | tf_op jit(solution)/shard_map/ppermute | solution.py:23
  44.4 12.5 %collective-permute-start.6 = (bf16[2,256,256]{2,1,0:T(8,128)(2,1)S(1)}, bf16[2,256,256]{2,1,0:T(8,128)(2,1)S(1)}, u32[]{:S(2)}, u32[]{:S(2)}) collective-permute-start(bf16[2,256,256]{2,1,0:T(8,128)(2,1)S(1)} %collective-permute-done.4.refs_2_), channel_id=1, source_target_pairs={{0,14},{2,0},{4,2},{6,4},{8,6},{10,8},{12,10},{14,12},{1,15},{3,1}... | collective-permute-start | bytes 786440 | tf_op jit(solution)/shard_map/ppermute | solution.py:23
  48.6 11.2 %collective-permute-start.5 = (bf16[2,256,256]{2,1,0:T(8,128)(2,1)S(1)}, bf16[2,256,256]{2,1,0:T(8,128)(2,1)S(1)}, u32[]{:S(2)}, u32[]{:S(2)}) collective-permute-start(bf16[2,256,256]{2,1,0:T(8,128)(2,1)S(1)} %collective-permute-done.3.refs_1_), channel_id=1, source_target_pairs={{0,2},{2,4},{4,6},{6,8},{8,10},{10,12},{12,14},{14,0},{1,3},{3,5},... | collective-permute-start | bytes 786440 | tf_op jit(solution)/shard_map/ppermute | solution.py:23
  54.2 11.2 %collective-permute-start.15 = (bf16[2,256,256]{2,1,0:T(8,128)(2,1)S(1)}, bf16[2,256,256]{2,1,0:T(8,128)(2,1)S(1)}, u32[]{:S(2)}, u32[]{:S(2)}) collective-permute-start(bf16[2,256,256]{2,1,0:T(8,128)(2,1)S(1)} %collective-permute-done.13.refs_1_), channel_id=1, source_target_pairs={{0,2},{2,4},{4,6},{6,8},{8,10},{10,12},{12,14},{14,0},{1,3},{3,5},... | collective-permute-start | bytes 786440 | tf_op jit(solution)/shard_map/ppermute | solution.py:23
  54.2 11.2 %collective-permute-start.16 = (bf16[2,256,256]{2,1,0:T(8,128)(2,1)S(1)}, bf16[2,256,256]{2,1,0:T(8,128)(2,1)S(1)}, u32[]{:S(2)}, u32[]{:S(2)}) collective-permute-start(bf16[2,256,256]{2,1,0:T(8,128)(2,1)S(1)} %collective-permute-done.14.refs_2_), channel_id=1, source_target_pairs={{0,14},{2,0},{4,2},{6,4},{8,6},{10,8},{12,10},{14,12},{1,15},{3,1}... | collective-permute-start | bytes 786440 | tf_op jit(solution)/shard_map/ppermute | solution.py:23
  56.9 11.3 %collective-permute-start.8 = (bf16[2,256,256]{2,1,0:T(8,128)(2,1)S(1)}, bf16[2,256,256]{2,1,0:T(8,128)(2,1)S(1)}, u32[]{:S(2)}, u32[]{:S(2)}) collective-permute-start(bf16[2,256,256]{2,1,0:T(8,128)(2,1)S(1)} %collective-permute-done.6.refs_4_), channel_id=1, source_target_pairs={{0,14},{2,0},{4,2},{6,4},{8,6},{10,8},{12,10},{14,12},{1,15},{3,1}... | collective-permute-start | bytes 786440 | tf_op jit(solution)/shard_map/ppermute | solution.py:23
  59.8 11.2 %collective-permute-start.7 = (bf16[2,256,256]{2,1,0:T(8,128)(2,1)S(1)}, bf16[2,256,256]{2,1,0:T(8,128)(2,1)S(1)}, u32[]{:S(2)}, u32[]{:S(2)}) collective-permute-start(bf16[2,256,256]{2,1,0:T(8,128)(2,1)S(1)} %collective-permute-done.5.refs_3_), channel_id=1, source_target_pairs={{0,2},{2,4},{4,6},{6,8},{8,10},{10,12},{12,14},{14,0},{1,3},{3,5},... | collective-permute-start | bytes 786440 | tf_op jit(solution)/shard_map/ppermute | solution.py:23
  65.4 10.0 %collective-permute-start.17 = (bf16[2,256,256]{2,1,0:T(8,128)(2,1)S(1)}, bf16[2,256,256]{2,1,0:T(8,128)(2,1)S(1)}, u32[]{:S(2)}, u32[]{:S(2)}) collective-permute-start(bf16[2,256,256]{2,1,0:T(8,128)(2,1)S(1)} %collective-permute-done.15.refs_3_), channel_id=1, source_target_pairs={{0,2},{2,4},{4,6},{6,8},{8,10},{10,12},{12,14},{14,0},{1,3},{3,5},... | collective-permute-start | bytes 786440 | tf_op jit(solution)/shard_map/ppermute | solution.py:23
  65.5 10.7 %collective-permute-start.18 = (bf16[2,256,256]{2,1,0:T(8,128)(2,1)S(1)}, bf16[2,256,256]{2,1,0:T(8,128)(2,1)S(1)}, u32[]{:S(2)}, u32[]{:S(2)}) collective-permute-start(bf16[2,256,256]{2,1,0:T(8,128)(2,1)S(1)} %collective-permute-done.16.refs_4_), channel_id=1, source_target_pairs={{0,14},{2,0},{4,2},{6,4},{8,6},{10,8},{12,10},{14,12},{1,15},{3,1}... | collective-permute-start | bytes 786440 | tf_op jit(solution)/shard_map/ppermute | solution.py:23
  68.2 11.4 %collective-permute-start.10 = (bf16[2,128,256]{2,1,0:T(8,128)(2,1)S(1)}, bf16[2,128,256]{2,1,0:T(8,128)(2,1)S(1)}, u32[]{:S(2)}, u32[]{:S(2)}) collective-permute-start(bf16[2,128,256]{2,1,0:T(8,128)(2,1)S(1)} %slice.52), channel_id=1, source_target_pairs={{0,14},{2,0},{4,2},{6,4},{8,6},{10,8},{12,10},{14,12},{1,15},{3,1}... | collective-permute-start | bytes 393224 | tf_op jit(solution)/shard_map/ppermute | solution.py:23
  71.1 9.2 %collective-permute-start.9 = (bf16[2,128,256]{2,1,0:T(8,128)(2,1)S(1)}, bf16[2,128,256]{2,1,0:T(8,128)(2,1)}, u32[]{:S(2)}, u32[]{:S(2)}) collective-permute-start(bf16[2,128,256]{2,1,0:T(8,128)(2,1)S(1)} %slice.51), channel_id=1, source_target_pairs={{0,2},{2,4},{4,6},{6,8},{8,10},{10,12},{12,14},{14,0},{1,3},{3,5},... | collective-permute-start | bytes 393224 | tf_op jit(solution)/shard_map/ppermute | solution.py:23
  76.2 9.3 %collective-permute-start.19 = (bf16[2,128,256]{2,1,0:T(8,128)(2,1)}, bf16[2,128,256]{2,1,0:T(8,128)(2,1)}, u32[]{:S(2)}, u32[]{:S(2)}) collective-permute-start(bf16[2,128,256]{2,1,0:T(8,128)(2,1)} %slice.54), channel_id=1, source_target_pairs={{0,2},{2,4},{4,6},{6,8},{8,10},{10,12},{12,14},{14,0},{1,3},{3,5},... | collective-permute-start | bytes 393224 | tf_op jit(solution)/shard_map/ppermute | solution.py:23
  76.9 8.6 %collective-permute-start.20 = (bf16[2,128,256]{2,1,0:T(8,128)(2,1)}, bf16[2,128,256]{2,1,0:T(8,128)(2,1)}, u32[]{:S(2)}, u32[]{:S(2)}) collective-permute-start(bf16[2,128,256]{2,1,0:T(8,128)(2,1)} %slice.55), channel_id=1, source_target_pairs={{0,14},{2,0},{4,2},{6,4},{8,6},{10,8},{12,10},{14,12},{1,15},{3,1}... | collective-permute-start | bytes 393224 | tf_op jit(solution)/shard_map/ppermute | solution.py:23
  92.4 6.7 %collective-permute-start.24 = (bf16[512,128]{1,0:T(8,128)(2,1)S(1)}, bf16[512,128]{1,0:T(8,128)(2,1)S(1)}, u32[]{:S(2)}, u32[]{:S(2)}) collective-permute-start(bf16[512,128]{1,0:T(8,128)(2,1)S(1)} %get-tuple-element.41), channel_id=1, source_target_pairs={{0,128},{128,0},{1,129},{129,1},{2,130},{130,2},{3,131},{131,3},{4... | collective-permute-start | bytes 393224 | tf_op jit(solution)/shard_map/ppermute | solution.py:23
  96.3 6.3 %collective-permute-start.23 = (bf16[512,128]{1,0:T(8,128)(2,1)S(1)}, bf16[512,128]{1,0:T(8,128)(2,1)S(1)}, u32[]{:S(2)}, u32[]{:S(2)}) collective-permute-start(bf16[512,128]{1,0:T(8,128)(2,1)S(1)} %get-tuple-element.43), channel_id=1, source_target_pairs={{0,128},{128,0},{1,129},{129,1},{2,130},{130,2},{3,131},{131,3},{4... | collective-permute-start | bytes 393224 | tf_op jit(solution)/shard_map/ppermute | solution.py:23
  108.2 8.2 %collective-permute-start.25 = (bf16[2,512,128]{2,1,0:T(8,128)(2,1)S(1)}, bf16[2,512,128]{2,1,0:T(8,128)(2,1)S(1)}, u32[]{:S(2)}, u32[]{:S(2)}) collective-permute-start(bf16[2,512,128]{2,1,0:T(8,128)(2,1)S(1)} %get-tuple-element.30), channel_id=1, source_target_pairs={{0,128},{128,0},{1,129},{129,1},{2,130},{130,2},{3,131},{131,3},{4... | collective-permute-start | bytes 786440 | tf_op jit(solution)/shard_map/ppermute | solution.py:23
  110.1 8.3 %collective-permute-start.26 = (bf16[2,512,128]{2,1,0:T(8,128)(2,1)S(1)}, bf16[2,512,128]{2,1,0:T(8,128)(2,1)S(1)}, u32[]{:S(2)}, u32[]{:S(2)}) collective-permute-start(bf16[2,512,128]{2,1,0:T(8,128)(2,1)S(1)} %get-tuple-element.29.refs_0_), channel_id=1, source_target_pairs={{0,1},{1,0},{2,3},{3,2},{4,5},{5,4},{6,7},{7,6},{8,9},{9,8},{10,11... | collective-permute-start | bytes 786440 | tf_op jit(solution)/shard_map/ppermute | solution.py:23
  124.2 7.6 %collective-permute-start.32 = (bf16[64,2048]{1,0:T(8,128)(2,1)S(1)}, bf16[64,2048]{1,0:T(8,128)(2,1)S(1)}, u32[]{:S(2)}, u32[]{:S(2)}) collective-permute-start(bf16[64,2048]{1,0:T(8,128)(2,1)S(1)} %get-tuple-element.45), channel_id=1, source_target_pairs={{0,48},{16,0},{32,16},{48,32},{1,49},{17,1},{33,17},{49,33},{2,50}... | collective-permute-start | bytes 786440 | tf_op jit(solution)/shard_map/ppermute | solution.py:23
  125.2 8.9 %collective-permute-start.28 = (bf16[64,2048]{1,0:T(8,128)(2,1)S(1)}, bf16[64,2048]{1,0:T(8,128)(2,1)S(1)}, u32[]{:S(2)}, u32[]{:S(2)}) collective-permute-start(bf16[64,2048]{1,0:T(8,128)(2,1)S(1)} %get-tuple-element.46), channel_id=1, source_target_pairs={{0,16},{16,32},{32,48},{48,0},{1,17},{17,33},{33,49},{49,1},{2,18}... | collective-permute-start | bytes 786440 | tf_op jit(solution)/shard_map/ppermute | solution.py:23
  125.8 13.4 %collective-permute-start.30 = (bf16[64,2048]{1,0:T(8,128)(2,1)S(1)}, bf16[64,2048]{1,0:T(8,128)(2,1)S(1)}, u32[]{:S(2)}, u32[]{:S(2)}) collective-permute-start(bf16[64,2048]{1,0:T(8,128)(2,1)S(1)} %slice.69), channel_id=1, source_target_pairs={{0,16},{16,32},{32,48},{48,0},{1,17},{17,33},{33,49},{49,1},{2,18}... | collective-permute-start | bytes 786440 | tf_op jit(solution)/shard_map/ppermute | solution.py:23
  125.9 13.3 %collective-permute-start.31 = (bf16[64,2048]{1,0:T(8,128)(2,1)S(1)}, bf16[64,2048]{1,0:T(8,128)(2,1)S(1)}, u32[]{:S(2)}, u32[]{:S(2)}) collective-permute-start(bf16[64,2048]{1,0:T(8,128)(2,1)S(1)} %slice.68), channel_id=1, source_target_pairs={{0,48},{16,0},{32,16},{48,32},{1,49},{17,1},{33,17},{49,33},{2,50}... | collective-permute-start | bytes 786440 | tf_op jit(solution)/shard_map/ppermute | solution.py:23
  131.9 11.2 %collective-permute-start.33 = (bf16[64,2048]{1,0:T(8,128)(2,1)S(1)}, bf16[64,2048]{1,0:T(8,128)(2,1)S(1)}, u32[]{:S(2)}, u32[]{:S(2)}) collective-permute-start(bf16[64,2048]{1,0:T(8,128)(2,1)S(1)} %add_convert_fusion), channel_id=1, source_target_pairs={{0,48},{16,0},{32,16},{48,32},{1,49},{17,1},{33,17},{49,33},{2,50}... | collective-permute-start | bytes 786440 | tf_op jit(solution)/shard_map/ppermute | solution.py:23
  134.1 10.7 %collective-permute-start.29 = (bf16[64,2048]{1,0:T(8,128)(2,1)S(1)}, bf16[64,2048]{1,0:T(8,128)(2,1)S(1)}, u32[]{:S(2)}, u32[]{:S(2)}) collective-permute-start(bf16[64,2048]{1,0:T(8,128)(2,1)S(1)} %add_convert_fusion.1), channel_id=1, source_target_pairs={{0,16},{16,32},{32,48},{48,0},{1,17},{17,33},{33,49},{49,1},{2,18}... | collective-permute-start | bytes 786440 | tf_op jit(solution)/shard_map/ppermute | solution.py:23
  (32 other events, 454.7 us)
Sparse Core Ops, SparseCore 0:
  21.2 55.5 all-gather.2

commit v3 on v2

--- a/solution.py
+++ b/solution.py
@@ -16,6 +16,8 @@
 MIB = 1024 * 1024
 META = 16
 PIECES = 9
+BLOCKS = 4
+PROJECT_LIMIT = 56
 
 
 def shift(block, axis, distance):
@@ -25,6 +27,11 @@
 
 def dot(left, right, contract):
     return lax.dot_general(left, right, (contract, ((), ())), preferred_element_type=F32)
+
+
+def side_by_side(heads):
+    half = heads.shape[0] // 2
+    return jnp.concatenate([heads[:half], heads[half:]], 1)
 
 
 def attention_kernel(place_ref, meta_ref, *refs):
@@ -46,26 +53,24 @@
         own_slot = (query_index >= meta[:1, 0:1]).astype(F32)
         key_end = jnp.where(key_slot > 0, meta[:1, 2:3] + ELEN, meta[:1, 1:2])
         allowed = (own_slot == key_slot) & (key_index < key_end)
-        sums = None
-        for head in range(2):
-            mine = lane // HD == head
-            query_head = jnp.where(mine, query, 0)
-            grad_head = jnp.where(mine, output_grad, 0)
-            scores = dot(query_head, keys, ((1,), (1,)))
-            scores = jnp.where(allowed, scores, -1e30)
-            exponent = jnp.exp(scores - jnp.max(scores, -1, keepdims=True))
-            softmax_rows = exponent / jnp.sum(exponent, -1, keepdims=True)
-            soft_low = softmax_rows.astype(BF)
-            attended = dot(soft_low, values, ((1,), (0,))).astype(BF)
-            row_delta = jnp.sum(grad_head.astype(F32) * attended.astype(F32), -1, keepdims=True)
-            prob_grad = dot(grad_head, values, ((1,), (1,)))
-            score_grad = (softmax_rows * (prob_grad - row_delta)).astype(BF)
-            query_grad = dot(score_grad, keys, ((1,), (0,)))
-            key_grad = dot(score_grad, query, ((0,), (0,)))
-            value_grad = dot(soft_low, output_grad, ((0,), (0,)))
-            grads = (query_grad, key_grad, value_grad)
-            sums = grads if head == 0 else [jnp.where(mine, g, s) for g, s in zip(grads, sums)]
-        query_grad, key_grad, value_grad = [g.astype(BF) for g in sums]
+        allowed = jnp.concatenate([allowed.astype(F32)] * 2, 0) > 0
+        query, output_grad, key_heads, value_heads = [
+            jnp.concatenate([jnp.where(lane // HD == head, part, 0) for head in range(2)], 0)
+            for part in (query, output_grad, keys, values)
+        ]
+        scores = dot(query, keys, ((1,), (1,)))
+        prob_grad = dot(output_grad, values, ((1,), (1,)))
+        scores = jnp.where(allowed, scores, -1e30)
+        exponent = jnp.exp(scores - jnp.max(scores, -1, keepdims=True))
+        softmax_rows = exponent / jnp.sum(exponent, -1, keepdims=True)
+        soft_low = softmax_rows.astype(BF)
+        attended = dot(side_by_side(soft_low), value_heads, ((1,), (0,))).astype(BF).astype(F32)
+        attended = jnp.concatenate([attended, attended], 0)
+        row_delta = jnp.sum(output_grad.astype(F32) * attended, -1, keepdims=True)
+        score_grad = (softmax_rows * (prob_grad - row_delta)).astype(BF)
+        query_grad = dot(side_by_side(score_grad), key_heads, ((1,), (0,))).astype(BF)
+        key_grad = dot(score_grad, query, ((0,), (0,))).astype(BF)
+        value_grad = dot(soft_low, output_grad, ((0,), (0,))).astype(BF)
         empty = jnp.zeros_like(query_grad)
         stay_ref[0, pick, :] = jnp.where(at_encoder, key_grad, query_grad)
         stay_ref[1, pick, :] = jnp.where(at_encoder, value_grad, empty)
@@ -183,7 +188,7 @@
         ),
         in_specs=[pl.BlockSpec(memory_space=pltpu.SMEM)] + [whole] * (3 + len(parts)),
         out_specs=(whole, whole),
-        compiler_params=pltpu.CompilerParams(vmem_limit_bytes=8 * MIB),
+        compiler_params=pltpu.CompilerParams(vmem_limit_bytes=30 * MIB),
     )(place, rows, cotan, gain, *parts)
 
 
@@ -207,7 +212,7 @@
 
 def project_kernel(part, place_ref, gathered_ref, *refs):
     piece_refs = refs[:PIECES]
-    own_ref, other_ref, meta_ref, weight_ref, left_ref, left_sems, sems = refs[PIECES:]
+    own_ref, other_ref, meta_ref, out_ref, left_ref, weight_ref, left_sems, sems = refs[PIECES:]
     blocks = gathered_ref.shape[0]
     rows = left_ref.shape[0] // blocks
     copies = []
@@ -223,13 +228,16 @@
         copy.start()
     for copy in copies:
         copy.wait()
+    assembled = pltpu.make_async_copy(weight_ref, out_ref, left_sems.at[2, 0])
+    assembled.start()
     half = own_ref.shape[2]
     z_size, depth, width = weight_ref.shape[1:]
-    for columns, out_ref in enumerate((own_ref, other_ref)):
+    for columns, ref in ((1, other_ref), (0, own_ref)):
         weights = weight_ref[columns].reshape(z_size * depth, width)
         product = dot(left_ref[...], weights, ((1,), (0,)))
         for at in range(2):
-            out_ref[at] = product[:, at * half : (at + 1) * half].astype(out_ref.dtype)
+            ref[at] = product[:, at * half : (at + 1) * half].astype(ref.dtype)
+    assembled.wait()
 
 
 def project(part, place, gathered, pieces):
@@ -237,6 +245,7 @@
     rows = (rows - META) // 2
     _, depth, columns = pieces[0].shape
     shape = (2, blocks * rows, columns // 2)
+    weights = (2, width // depth, depth, columns)
     whole = pl.BlockSpec(memory_space=pltpu.VMEM)
     return pl.pallas_call(
         functools.partial(project_kernel, part),
@@ -244,31 +253,34 @@
             jax.ShapeDtypeStruct(shape, F32),
             jax.ShapeDtypeStruct(shape, BF),
             jax.ShapeDtypeStruct((blocks, META, 2 * HD), BF),
-            jax.ShapeDtypeStruct((2, width // depth, depth, columns), BF),
+            jax.ShapeDtypeStruct(weights, BF),
         ),
         in_specs=[pl.BlockSpec(memory_space=pltpu.SMEM)]
         + [pl.BlockSpec(memory_space=pltpu.HBM)] * (1 + len(pieces)),
-        out_specs=(whole, whole, whole, whole),
+        out_specs=(whole, whole, whole, pl.BlockSpec(memory_space=pltpu.HBM)),
         scratch_shapes=[
             pltpu.VMEM((blocks * rows, width), BF),
-            pltpu.SemaphoreType.DMA((2, blocks)),
+            pltpu.VMEM(weights, BF),
+            pltpu.SemaphoreType.DMA((3, blocks)),
             pltpu.SemaphoreType.DMA((PIECES,)),
         ],
-        compiler_params=pltpu.CompilerParams(vmem_limit_bytes=56 * MIB),
+        compiler_params=pltpu.CompilerParams(vmem_limit_bytes=PROJECT_LIMIT * MIB),
     )(place, gathered, *pieces)
 
 
-def back_kernel(place_ref, *refs):
-    grad_refs, weight_refs = refs[:4], refs[4:6]
-    own_ref, near_ref, far_ref, last_ref = refs[6:]
+def back_kernel(blocks, place_ref, *refs):
+    grad_refs, weight_refs, out_refs = refs[:4], refs[4:6], refs[6:]
     at_encoder = place_ref[0] == 0
-    rows = own_ref.shape[0]
+    rows = grad_refs[0].shape[1] // BLOCKS
     grads = []
     for part in range(2):
         for columns in range(2):
-            stay, back = grad_refs[2 * columns][part], grad_refs[2 * columns + 1][part]
-            low = jnp.where(at_encoder, stay, back)
-            high = jnp.where(at_encoder, back, stay)
+            picked = []
+            for ref in grad_refs[2 * columns : 2 * columns + 2]:
+                pieces = [ref[part, pl.ds(block * rows, rows)] for block in blocks]
+                picked.append(jnp.concatenate(pieces, 0))
+            low = jnp.where(at_encoder, picked[0], picked[1])
+            high = jnp.where(at_encoder, picked[1], picked[0])
             grads.append((part, columns, jnp.concatenate([low, high], 1)))
     z_size, depth = weight_refs[0].shape[1:3]
     for z in range(z_size):
@@ -276,32 +288,33 @@
         for part, columns, grad in grads:
             total += dot(grad, weight_refs[part][columns, z], ((1,), (1,)))
         pick = pl.ds(z * depth, depth)
-        for at, ref in enumerate((own_ref, near_ref, far_ref, last_ref)):
-            ref[:, pick] = total[at * rows : (at + 1) * rows].astype(ref.dtype)
-
-
-def back_project(place, grads, weights, shape):
+        start = 0
+        for ref in out_refs:
+            stop = start + ref.shape[0]
+            ref[:, pick] = total[start:stop].astype(ref.dtype)
+            start = stop
+
+
+def back_project(blocks, outs, place, grads, weights):
     whole = pl.BlockSpec(memory_space=pltpu.VMEM)
     return pl.pallas_call(
-        back_kernel,
-        out_shape=[jax.ShapeDtypeStruct(shape, kind) for kind in (F32, F32, BF, F32)],
+        functools.partial(back_kernel, blocks),
+        out_shape=outs,
         in_specs=[pl.BlockSpec(memory_space=pltpu.SMEM)] + [whole] * (len(grads) + len(weights)),
-        out_specs=[whole] * 4,
+        out_specs=[whole] * len(outs),
         compiler_params=pltpu.CompilerParams(vmem_limit_bytes=16 * MIB),
     )(place, *grads, *weights)
 
 
-def exchange_columns(weights):
+def slice_columns(weights):
     rows, parts, columns = weights.shape
     x_size = lax.axis_size("x")
-    slices = weights.reshape(rows, parts, x_size, columns // x_size).transpose(2, 1, 0, 3)
-    return lax.all_to_all(slices, "x", 0, 0, tiled=True)
-
-
-def gather_weights(chunk, own_y, own_c):
+    return weights.reshape(rows, parts, x_size, columns // x_size).transpose(2, 1, 0, 3)
+
+
+def gather_weights(chunk, at_source):
     x_size, rows, columns = chunk.shape
     z_size = lax.axis_size("z")
-    at_source = own_y == own_c
     near = lax.ppermute(chunk, ("y", "mp"), [(1, 0), (2, 3), (0, 2), (3, 1)])
     far = lax.ppermute(chunk, ("y", "mp"), [(1, 2), (2, 1)])
     merged = jnp.stack([jnp.where(at_source, chunk, near), jnp.where(at_source, near, far)], 0)
@@ -314,34 +327,30 @@
     return pieces + [shift(up[:, :half], "z", 1), shift(down[:, half:], "z", -1)]
 
 
-def sum_over_x(own, near, far, last):
-    half = own.shape[0] // 2
-    up, down = shift(far[:half], "x", 1), shift(far[half:], "x", -1)
-    below_rest = shift(near[half:].astype(BF), "x", 1)
-    above_rest = shift(last[:half].astype(BF), "x", -1)
-    below = shift((near[:half] + up.astype(F32)).astype(BF), "x", 1)
-    above = shift((last[half:] + down.astype(F32)).astype(BF), "x", -1)
-    return own, below, below_rest, above_rest, above
+def sum_over_x(far_low, far_high, own, near_low, near_high, last_low, last_high):
+    up, down = shift(far_low, "x", 1), shift(far_high, "x", -1)
+    below_high, above_low = shift(near_high, "x", 1), shift(last_low, "x", -1)
+    below_low = shift((near_low + up.astype(F32)).astype(BF), "x", 1)
+    above_high = shift((last_high + down.astype(F32)).astype(BF), "x", -1)
+    return own, below_low, below_high, above_low, above_high
 
 
 def on_device(section_rows, norm_gains, proj_weights, section_cotan, enc_lengths, dec_segments):
     side = lax.axis_index("section")
     own_y, own_z, own_c = (lax.axis_index(a) for a in ("y", "z", "mp"))
-    at_encoder = side == 0
     rows, cotan, weights = section_rows[0], section_cotan[0], proj_weights[0]
-    row_count, half_width = rows.shape
-    width = 2 * half_width
     place = jnp.stack([side, own_z, lax.axis_index("x")])
     wide_rows = rows.astype(F32)
 
     square = jnp.sum(wide_rows * wide_rows, -1, keepdims=True)
     square = square + shift(square, "mp", 1)
-    chunks = exchange_columns(weights)
+    slices = slice_columns(weights)
+    chunks = lax.all_to_all(slices, "x", 0, 0, tiled=True)
     inverse, left = prepare(
         place, enc_lengths, dec_segments, rows, cotan, norm_gains, square, chunks
     )
     gathered = lax.all_gather(left, "x")
-    pieces = [gather_weights(chunks[:, part], own_y, own_c) for part in range(2)]
+    pieces = [gather_weights(chunks[:, part], own_y == own_c) for part in range(2)]
 
     keep, recv, full = [], [], []
     for part in range(2):
@@ -358,11 +367,19 @@
     stay, back = attention(place, meta, keep, recv)
     back = shift(back, "section", 1)
     grads = (stay, back, shift(stay, "mp", 1), shift(back, "mp", 1))
-    parts = sum_over_x(*back_project(place, grads, full, rows.shape))
+    row_count, half_width = rows.shape
+
+    def outs(*kinds):
+        return [jax.ShapeDtypeStruct((row_count // 2, half_width), kind) for kind in kinds]
+
+    far = back_project((2,), outs(BF, BF), place, grads, full)
+    whole = [jax.ShapeDtypeStruct(rows.shape, F32)]
+    near = back_project((0, 1, 3), whole + outs(F32, BF, BF, F32), place, grads, full)
+    parts = sum_over_x(*far, *near)
     gain_grad, row_dot = finish(place, rows, cotan, norm_gains, parts)
-    row_dot = (row_dot + shift(row_dot, "mp", 1)) / width
+    row_dot = (row_dot + shift(row_dot, "mp", 1)) / (2 * rows.shape[1])
     result = inverse * gain_grad - wide_rows * inverse**3 * row_dot
-    return (result + jnp.where(at_encoder, 0.0, cotan.astype(F32)))[None]
+    return (result + jnp.where(side == 0, 0.0, cotan.astype(F32)))[None]
 
 
 def solution(mesh):

time: 159 us -> 155 us (0.975)
  waiting for transfers between devices: 56 us -> 51.5 us
    ppermute x31, waiting for transfers between devices: 51.8 us -> 47.3 us  [shift(): lax.ppermute(block, axis, [(i, (i + distance) % size) for i in range(size)])]
    pallas_call x1, Pallas kernels: 5.53 us -> 3.21 us  [attention(): pl.pallas_call(attention_kernel, out_shape=(shape, shape), in_specs=[pl.B...]
    pallas_call x1 -> x2, Pallas kernels: 2.91 us -> 5.04 us  [back_project(): pl.pallas_call(functools.partial(back_kernel, blocks), out_shape=outs, in...]
  transfers between devices with their start and end apart: 37 -> 37, of which waited for: 20 -> 19; matrix products, arithmetic and copies ran while one was open for 4% -> 4% of each run, Pallas kernels for 6% -> 9%
where the time goes in v3:
time: 155 us; the launch traced here: 154 us
  starting transfers between devices  53 us (34%)
  waiting for transfers between devices  51.5 us (33%)
  Pallas kernels  22.1 us (14%)
  between operations  13.8 us (9%)
  other arithmetic  6.94 us (4%)
  local copies, waits for them, and re-layouts  6.81 us (4%)
    ppermute x31, waiting for transfers between devices, shift(): lax.ppermute(block, axis, [(i, (i + distance) % size) for i in range(size)])  47.3 us
    ppermute x31, starting transfers between devices, shift(): lax.ppermute(block, axis, [(i, (i + distance) % size) for i in range(size)])  38.8 us
    pallas_call x2, Pallas kernels, project(): pl.pallas_call(functools.partial(project_kernel, part), out_shape=(jax.Sh...  10.6 us
    ppermute x2, starting transfers between devices, gather_weights(): far = lax.ppermute(chunk, ('y', 'mp'), [(1, 2), (2, 1)])  5.55 us
    pallas_call x2, Pallas kernels, back_project(): pl.pallas_call(functools.partial(back_kernel, blocks), out_shape=outs, in...  5.04 us
    all_to_all x1, starting transfers between devices, on_device(): chunks = lax.all_to_all(slices, 'x', 0, 0, tiled=True)  4.84 us
    ppermute x2, starting transfers between devices, gather_weights(): near = lax.ppermute(chunk, ('y', 'mp'), [(1, 0), (2, 3), (0, 2), (3, 1)])  3.77 us
    unnamed x54, local copies, waits for them, and re-layouts  3.3 us
  transfers between devices with their start and end apart: 37, of which 19 were waited for; matrix products, arithmetic and copies ran while one was open for 4% of the time, Pallas kernels for 9%

profile of v3, /device:TPU:1, one launch (start us, length us, event | category | flops | bytes accessed | tf_op | source)
XLA Modules:
  0.0 154.2 jit_solution(6286142545682158714)
XLA Ops:
  8.5 4.8 %all-to-all-start = ((bf16[4,2,64,256]{3,2,1,0:T(8,128)(2,1)}), bf16[4,2,64,256]{3,2,1,0:T(8,128)(2,1)S(1)}, u32[]{:S(2)}, u32[]{:S(2)}) async-start(bf16[4,2,64,256]{3,2,1,0:T(8,128)(2,1)} %bitcast.36), calls=%async_computation | async-start | bytes 524288 | tf_op jit(solution)/shard_map/all_to_all | solution.py:348
  18.9 2.2 %shard_map.64 = (f32[128,1]{1,0:T(8,128)S(1)}, bf16[272,2048]{1,0:T(8,128)(2,1)}) custom-call(s32[3]{0:T(128)S(1)} %pad_add_fusion.place_ref, s32[1,2]{1,0:T(1,128)S(1)} %copy-done.10, s32[1,128]{1,0:T(1,128)S(1)} %copy-done.11, bf16[128,2048]{1,0:T(8,128)(2,1)S(1)} %bitcast.37, bf16[128,2048]{1,0:T(8,128)(2,1)S(1)} %bitcast.39, ...), custom_call_target="tpu_custom_call" | custom-call | tf_op jit(solution)/shard_map/pallas_call | solution.py:142
  21.1 3.0 %collective-permute-start.1 = (bf16[4,64,256]{2,1,0:T(8,128)(2,1)S(1)}, bf16[4,64,256]{2,1,0:T(8,128)(2,1)S(1)}, u32[]{:S(2)}, u32[]{:S(2)}) collective-permute-start(bf16[4,64,256]{2,1,0:T(8,128)(2,1)S(1)} %get-tuple-element.54), channel_id=1, source_target_pairs={{1,0},{64,65},{0,64},{65,1},{3,2},{66,67},{2,66},{67,3},{5,4},{68,... | collective-permute-start | bytes 393224 | tf_op jit(solution)/shard_map/ppermute | solution.py:318
  26.8 3.6 %collective-permute-start.2 = (bf16[4,64,256]{2,1,0:T(8,128)(2,1)S(1)}, bf16[4,64,256]{2,1,0:T(8,128)(2,1)S(1)}, u32[]{:S(2)}, u32[]{:S(2)}) collective-permute-start(bf16[4,64,256]{2,1,0:T(8,128)(2,1)S(1)} %get-tuple-element.54), channel_id=1, source_target_pairs={{1,64},{64,1},{3,66},{66,3},{5,68},{68,5},{7,70},{70,7},{9,72},{72... | collective-permute-start | bytes 393224 | tf_op jit(solution)/shard_map/ppermute | solution.py:319
  31.2 2.2 %collective-permute-done.2 = bf16[4,64,256]{2,1,0:T(8,128)(2,1)S(1)} collective-permute-done((bf16[4,64,256]{2,1,0:T(8,128)(2,1)S(1)}, bf16[4,64,256]{2,1,0:T(8,128)(2,1)S(1)}, u32[]{:S(2)}, u32[]{:S(2)}) %collective-permute-start.2) | collective-permute-done | bytes 131104 | tf_op jit(solution)/shard_map/ppermute | solution.py:319
  33.5 5.4 %collective-permute-start.4 = (bf16[2,256,256]{2,1,0:T(8,128)(2,1)S(1)}, bf16[2,256,256]{2,1,0:T(8,128)(2,1)S(1)}, u32[]{:S(2)}, u32[]{:S(2)}) collective-permute-start(bf16[2,256,256]{2,1,0:T(8,128)(2,1)S(1)} %pad_maximum_fusion.refs_0_), channel_id=1, source_target_pairs={{0,14},{2,0},{4,2},{6,4},{8,6},{10,8},{12,10},{14,12},{1,15},{3,1}... | collective-permute-start | bytes 786440 | tf_op jit(solution)/shard_map/ppermute | solution.py:25
  39.0 2.7 %collective-permute-start.14 = (bf16[2,256,256]{2,1,0:T(8,128)(2,1)S(1)}, bf16[2,256,256]{2,1,0:T(8,128)(2,1)S(1)}, u32[]{:S(2)}, u32[]{:S(2)}) collective-permute-start(bf16[2,256,256]{2,1,0:T(8,128)(2,1)S(1)} %pad_maximum_fusion.1.refs_0_), channel_id=1, source_target_pairs={{0,14},{2,0},{4,2},{6,4},{8,6},{10,8},{12,10},{14,12},{1,15},{3,1}... | collective-permute-start | bytes 786440 | tf_op jit(solution)/shard_map/ppermute | solution.py:25
  41.7 2.7 %collective-permute-done.4.refs_2_ = bf16[2,256,256]{2,1,0:T(8,128)(2,1)S(1)} collective-permute-done((bf16[2,256,256]{2,1,0:T(8,128)(2,1)S(1)}, bf16[2,256,256]{2,1,0:T(8,128)(2,1)S(1)}, u32[]{:S(2)}, u32[]{:S(2)}) %collective-permute-start.4) | collective-permute-done | bytes 262176 | tf_op jit(solution)/shard_map/ppermute | solution.py:25
  44.4 3.5 %collective-permute-start.6 = (bf16[2,256,256]{2,1,0:T(8,128)(2,1)S(1)}, bf16[2,256,256]{2,1,0:T(8,128)(2,1)S(1)}, u32[]{:S(2)}, u32[]{:S(2)}) collective-permute-start(bf16[2,256,256]{2,1,0:T(8,128)(2,1)S(1)} %collective-permute-done.4.refs_2_), channel_id=1, source_target_pairs={{0,14},{2,0},{4,2},{6,4},{8,6},{10,8},{12,10},{14,12},{1,15},{3,1}... | collective-permute-start | bytes 786440 | tf_op jit(solution)/shard_map/ppermute | solution.py:25
  48.6 5.6 %collective-permute-done.13.refs_1_ = bf16[2,256,256]{2,1,0:T(8,128)(2,1)S(1)} collective-permute-done((bf16[2,256,256]{2,1,0:T(8,128)(2,1)S(1)}, bf16[2,256,256]{2,1,0:T(8,128)(2,1)S(1)}, u32[]{:S(2)}, u32[]{:S(2)}) %collective-permute-start.13) | collective-permute-done | bytes 262176 | tf_op jit(solution)/shard_map/ppermute | solution.py:25
  54.2 2.7 %collective-permute-start.16 = (bf16[2,256,256]{2,1,0:T(8,128)(2,1)S(1)}, bf16[2,256,256]{2,1,0:T(8,128)(2,1)S(1)}, u32[]{:S(2)}, u32[]{:S(2)}) collective-permute-start(bf16[2,256,256]{2,1,0:T(8,128)(2,1)S(1)} %collective-permute-done.14.refs_2_), channel_id=1, source_target_pairs={{0,14},{2,0},{4,2},{6,4},{8,6},{10,8},{12,10},{14,12},{1,15},{3,1}... | collective-permute-start | bytes 786440 | tf_op jit(solution)/shard_map/ppermute | solution.py:25
  57.1 2.7 %collective-permute-done.5.refs_3_ = bf16[2,256,256]{2,1,0:T(8,128)(2,1)S(1)} collective-permute-done((bf16[2,256,256]{2,1,0:T(8,128)(2,1)S(1)}, bf16[2,256,256]{2,1,0:T(8,128)(2,1)S(1)}, u32[]{:S(2)}, u32[]{:S(2)}) %collective-permute-start.5) | collective-permute-done | bytes 262176 | tf_op jit(solution)/shard_map/ppermute | solution.py:25
  59.8 5.6 %collective-permute-done.15.refs_3_ = bf16[2,256,256]{2,1,0:T(8,128)(2,1)S(1)} collective-permute-done((bf16[2,256,256]{2,1,0:T(8,128)(2,1)S(1)}, bf16[2,256,256]{2,1,0:T(8,128)(2,1)S(1)}, u32[]{:S(2)}, u32[]{:S(2)}) %collective-permute-start.15) | collective-permute-done | bytes 262176 | tf_op jit(solution)/shard_map/ppermute | solution.py:25
  65.5 2.7 %collective-permute-start.18 = (bf16[2,256,256]{2,1,0:T(8,128)(2,1)S(1)}, bf16[2,256,256]{2,1,0:T(8,128)(2,1)S(1)}, u32[]{:S(2)}, u32[]{:S(2)}) collective-permute-start(bf16[2,256,256]{2,1,0:T(8,128)(2,1)S(1)} %collective-permute-done.16.refs_4_), channel_id=1, source_target_pairs={{0,14},{2,0},{4,2},{6,4},{8,6},{10,8},{12,10},{14,12},{1,15},{3,1}... | collective-permute-start | bytes 786440 | tf_op jit(solution)/shard_map/ppermute | solution.py:25
  68.3 2.7 %collective-permute-done.7.refs_5_ = bf16[2,256,256]{2,1,0:T(8,128)(2,1)S(1)} collective-permute-done((bf16[2,256,256]{2,1,0:T(8,128)(2,1)S(1)}, bf16[2,256,256]{2,1,0:T(8,128)(2,1)S(1)}, u32[]{:S(2)}, u32[]{:S(2)}) %collective-permute-start.7) | collective-permute-done | bytes 262176 | tf_op jit(solution)/shard_map/ppermute | solution.py:25
  71.1 4.3 %collective-permute-done.17.refs_5_ = bf16[2,256,256]{2,1,0:T(8,128)(2,1)S(1)} collective-permute-done((bf16[2,256,256]{2,1,0:T(8,128)(2,1)S(1)}, bf16[2,256,256]{2,1,0:T(8,128)(2,1)S(1)}, u32[]{:S(2)}, u32[]{:S(2)}) %collective-permute-start.17) | collective-permute-done | bytes 262176 | tf_op jit(solution)/shard_map/ppermute | solution.py:25
  76.9 2.7 %collective-permute-start.20 = (bf16[2,128,256]{2,1,0:T(8,128)(2,1)}, bf16[2,128,256]{2,1,0:T(8,128)(2,1)}, u32[]{:S(2)}, u32[]{:S(2)}) collective-permute-start(bf16[2,128,256]{2,1,0:T(8,128)(2,1)} %slice.29), channel_id=1, source_target_pairs={{0,14},{2,0},{4,2},{6,4},{8,6},{10,8},{12,10},{14,12},{1,15},{3,1}... | collective-permute-start | bytes 393224 | tf_op jit(solution)/shard_map/ppermute | solution.py:25
  80.2 5.3 %shard_map.65 = (f32[2,512,128]{2,1,0:T(8,128)}, bf16[2,512,128]{2,1,0:T(8,128)(2,1)}, bf16[4,16,128]{2,1,0:T(8,128)(2,1)}, bf16[2,8,256,256]{3,2,1,0:T(8,128)(2,1)}) custom-call(s32[3]{0:T(128)} %copy-done.7, bf16[4,272,2048]{2,1,0:T(8,128)(2,1)} %bitcast.41, bf16[2,256,256]{2,1,0:T(8,128)(2,1)} %copy-done.13, bf16[2,256,256]{2,1,0:T(8,128)(2,1)} %copy-done.21, ...), custom_call_target="tpu_custom_call" | custom-call | tf_op jit(solution)/shard_map/pallas_call | solution.py:250
  85.7 5.3 %shard_map.66 = (f32[2,512,128]{2,1,0:T(8,128)}, bf16[2,512,128]{2,1,0:T(8,128)(2,1)}, bf16[4,16,128]{2,1,0:T(8,128)(2,1)}, bf16[2,8,256,256]{3,2,1,0:T(8,128)(2,1)}) custom-call(s32[3]{0:T(128)} %copy-done.7, bf16[4,272,2048]{2,1,0:T(8,128)(2,1)} %bitcast.42, bf16[2,256,256]{2,1,0:T(8,128)(2,1)} %copy-done.12, bf16[2,256,256]{2,1,0:T(8,128)(2,1)} %copy-done.18, ...), custom_call_target="tpu_custom_call" | custom-call | tf_op jit(solution)/shard_map/pallas_call | solution.py:250
  92.8 2.7 %collective-permute-start.24 = (bf16[512,128]{1,0:T(8,128)(2,1)S(1)}, bf16[512,128]{1,0:T(8,128)(2,1)S(1)}, u32[]{:S(2)}, u32[]{:S(2)}) collective-permute-start(bf16[512,128]{1,0:T(8,128)(2,1)S(1)} %get-tuple-element.47), channel_id=1, source_target_pairs={{0,128},{128,0},{1,129},{129,1},{2,130},{130,2},{3,131},{131,3},{4... | collective-permute-start | bytes 393224 | tf_op jit(solution)/shard_map/ppermute | solution.py:25
  97.1 2.3 %collective-permute-done.24.refs_3_ = bf16[512,128]{1,0:T(8,128)(2,1)S(1)} collective-permute-done((bf16[512,128]{1,0:T(8,128)(2,1)S(1)}, bf16[512,128]{1,0:T(8,128)(2,1)S(1)}, u32[]{:S(2)}, u32[]{:S(2)}) %collective-permute-start.24) | collective-permute-done | bytes 131104 | tf_op jit(solution)/shard_map/ppermute | solution.py:25
  99.4 3.6 %collective-permute-done.23.refs_2_ = bf16[512,128]{1,0:T(8,128)(2,1)S(1)} collective-permute-done((bf16[512,128]{1,0:T(8,128)(2,1)S(1)}, bf16[512,128]{1,0:T(8,128)(2,1)S(1)}, u32[]{:S(2)}, u32[]{:S(2)}) %collective-permute-start.23) | collective-permute-done | bytes 131104 | tf_op jit(solution)/shard_map/ppermute | solution.py:25
  103.0 3.2 %shard_map.67 = (bf16[2,512,128]{2,1,0:T(8,128)(2,1)S(1)}, bf16[2,512,128]{2,1,0:T(8,128)(2,1)S(1)}) custom-call(s32[3]{0:T(128)S(1)} %copy-done.8, bf16[4,16,128]{2,1,0:T(8,128)(2,1)S(1)} %copy-done.9, bf16[512,128]{1,0:T(8,128)(2,1)S(1)} %get-tuple-element.50.refs_0_, bf16[512,128]{1,0:T(8,128)(2,1)S(1)} %get-tuple-element.48.refs_1_, ...), custom_call_target="tpu_custom_call" | custom-call | tf_op jit(solution)/shard_map/pallas_call | solution.py:84
  106.2 2.0 %collective-permute-start.25 = (bf16[2,512,128]{2,1,0:T(8,128)(2,1)S(1)}, bf16[2,512,128]{2,1,0:T(8,128)(2,1)S(1)}, u32[]{:S(2)}, u32[]{:S(2)}) collective-permute-start(bf16[2,512,128]{2,1,0:T(8,128)(2,1)S(1)} %get-tuple-element.33), channel_id=1, source_target_pairs={{0,128},{128,0},{1,129},{129,1},{2,130},{130,2},{3,131},{131,3},{4... | collective-permute-start | bytes 786440 | tf_op jit(solution)/shard_map/ppermute | solution.py:25
  109.3 5.1 %collective-permute-done.25.refs_1_ = bf16[2,512,128]{2,1,0:T(8,128)(2,1)S(1)} collective-permute-done((bf16[2,512,128]{2,1,0:T(8,128)(2,1)S(1)}, bf16[2,512,128]{2,1,0:T(8,128)(2,1)S(1)}, u32[]{:S(2)}, u32[]{:S(2)}) %collective-permute-start.25) | collective-permute-done | bytes 262176 | tf_op jit(solution)/shard_map/ppermute | solution.py:25
  114.4 2.1 %collective-permute-start.27 = (bf16[2,512,128]{2,1,0:T(8,128)(2,1)S(1)}, bf16[2,512,128]{2,1,0:T(8,128)(2,1)S(1)}, u32[]{:S(2)}, u32[]{:S(2)}) collective-permute-start(bf16[2,512,128]{2,1,0:T(8,128)(2,1)S(1)} %collective-permute-done.25.refs_1_), channel_id=1, source_target_pairs={{0,1},{1,0},{2,3},{3,2},{4,5},{5,4},{6,7},{7,6},{8,9},{9,8},{10,11... | collective-permute-start | bytes 786440 | tf_op jit(solution)/shard_map/ppermute | solution.py:25
  119.3 2.0 %shard_map.69 = (bf16[64,2048]{1,0:T(8,128)(2,1)S(1)}, bf16[64,2048]{1,0:T(8,128)(2,1)S(1)}) custom-call(s32[3]{0:T(128)S(1)} %copy-done.8, bf16[2,512,128]{2,1,0:T(8,128)(2,1)S(1)} %get-tuple-element.32.refs_0_, bf16[2,512,128]{2,1,0:T(8,128)(2,1)S(1)} %collective-permute-done.25.refs_1_, bf16[2,512,128]{2,1,0:T(8,128)(2,1)S(1)} %collective-permute-done.26.refs_2_, ...), custom_call_target="tpu_custom_call" | custom-call | tf_op jit(solution)/shard_map/pallas_call | solution.py:300
  123.0 3.0 %shard_map.68 = (f32[128,2048]{1,0:T(8,128)S(1)}, f32[64,2048]{1,0:T(8,128)S(1)}, bf16[64,2048]{1,0:T(8,128)(2,1)}, bf16[64,2048]{1,0:T(8,128)(2,1)S(1)}, f32[64,2048]{1,0:T(8,128)S(1)}) custom-call(s32[3]{0:T(128)S(1)} %copy-done.8, bf16[2,512,128]{2,1,0:T(8,128)(2,1)S(1)} %get-tuple-element.32.refs_0_, ...), custom_call_target="tpu_custom_call" | custom-call | tf_op jit(solution)/shard_map/pallas_call | solution.py:300
  127.1 2.7 %collective-permute-start.31 = (bf16[64,2048]{1,0:T(8,128)(2,1)S(1)}, bf16[64,2048]{1,0:T(8,128)(2,1)S(1)}, u32[]{:S(2)}, u32[]{:S(2)}) collective-permute-start(bf16[64,2048]{1,0:T(8,128)(2,1)S(1)} %get-tuple-element.40), channel_id=1, source_target_pairs={{0,48},{16,0},{32,16},{48,32},{1,49},{17,1},{33,17},{49,33},{2,50}... | collective-permute-start | bytes 786440 | tf_op jit(solution)/shard_map/ppermute | solution.py:25
  132.7 4.1 %collective-permute-done.30.refs_2_ = bf16[64,2048]{1,0:T(8,128)(2,1)S(1)} collective-permute-done((bf16[64,2048]{1,0:T(8,128)(2,1)}, bf16[64,2048]{1,0:T(8,128)(2,1)S(1)}, u32[]{:S(2)}, u32[]{:S(2)}) %collective-permute-start.30) | collective-permute-done | bytes 262176 | tf_op jit(solution)/shard_map/ppermute | solution.py:25
  136.9 3.0 %collective-permute-done.33.refs_4_ = bf16[64,2048]{1,0:T(8,128)(2,1)S(1)} collective-permute-done((bf16[64,2048]{1,0:T(8,128)(2,1)}, bf16[64,2048]{1,0:T(8,128)(2,1)S(1)}, u32[]{:S(2)}, u32[]{:S(2)}) %collective-permute-start.33) | collective-permute-done | bytes 262176 | tf_op jit(solution)/shard_map/ppermute | solution.py:25
  139.8 2.2 %collective-permute-done.29.refs_1_ = bf16[64,2048]{1,0:T(8,128)(2,1)S(1)} collective-permute-done((bf16[64,2048]{1,0:T(8,128)(2,1)}, bf16[64,2048]{1,0:T(8,128)(2,1)S(1)}, u32[]{:S(2)}, u32[]{:S(2)}) %collective-permute-start.29) | collective-permute-done | bytes 262176 | tf_op jit(solution)/shard_map/ppermute | solution.py:25
  (125 shorter events, 32.7 us)
Async XLA Ops:
  8.5 10.4 %all-to-all-start = ((bf16[4,2,64,256]{3,2,1,0:T(8,128)(2,1)}), bf16[4,2,64,256]{3,2,1,0:T(8,128)(2,1)S(1)}, u32[]{:S(2)}, u32[]{:S(2)}) async-start(bf16[4,2,64,256]{3,2,1,0:T(8,128)(2,1)} %bitcast.36), calls=%async_computation | async-start | bytes 524288 | tf_op jit(solution)/shard_map/all_to_all | solution.py:348
  13.4 66.9 %all-gather.3.cloned.1.call-start = ((), (), s32[]{:S(2)}) async-start(), calls=%async_computation.1 | async-start | bytes 5570560 | tf_op jit(solution)/shard_map/all_gather | solution.py:352
  21.1 9.3 %collective-permute-start.1 = (bf16[4,64,256]{2,1,0:T(8,128)(2,1)S(1)}, bf16[4,64,256]{2,1,0:T(8,128)(2,1)S(1)}, u32[]{:S(2)}, u32[]{:S(2)}) collective-permute-start(bf16[4,64,256]{2,1,0:T(8,128)(2,1)S(1)} %get-tuple-element.54), channel_id=1, source_target_pairs={{1,0},{64,65},{0,64},{65,1},{3,2},{66,67},{2,66},{67,3},{5,4},{68,... | collective-permute-start | bytes 393224 | tf_op jit(solution)/shard_map/ppermute | solution.py:318
  24.1 6.3 %collective-permute-start.11 = (bf16[4,64,256]{2,1,0:T(8,128)(2,1)S(1)}, bf16[4,64,256]{2,1,0:T(8,128)(2,1)S(1)}, u32[]{:S(2)}, u32[]{:S(2)}) collective-permute-start(bf16[4,64,256]{2,1,0:T(8,128)(2,1)S(1)} %get-tuple-element.53), channel_id=1, source_target_pairs={{1,0},{64,65},{0,64},{65,1},{3,2},{66,67},{2,66},{67,3},{5,4},{68,... | collective-permute-start | bytes 393224 | tf_op jit(solution)/shard_map/ppermute | solution.py:318
  24.9 6.3 %collective-permute-start.12 = (bf16[4,64,256]{2,1,0:T(8,128)(2,1)S(1)}, bf16[4,64,256]{2,1,0:T(8,128)(2,1)S(1)}, u32[]{:S(2)}, u32[]{:S(2)}) collective-permute-start(bf16[4,64,256]{2,1,0:T(8,128)(2,1)S(1)} %get-tuple-element.53), channel_id=1, source_target_pairs={{1,64},{64,1},{3,66},{66,3},{5,68},{68,5},{7,70},{70,7},{9,72},{72... | collective-permute-start | bytes 393224 | tf_op jit(solution)/shard_map/ppermute | solution.py:319
  26.8 6.6 %collective-permute-start.2 = (bf16[4,64,256]{2,1,0:T(8,128)(2,1)S(1)}, bf16[4,64,256]{2,1,0:T(8,128)(2,1)S(1)}, u32[]{:S(2)}, u32[]{:S(2)}) collective-permute-start(bf16[4,64,256]{2,1,0:T(8,128)(2,1)S(1)} %get-tuple-element.54), channel_id=1, source_target_pairs={{1,64},{64,1},{3,66},{66,3},{5,68},{68,5},{7,70},{70,7},{9,72},{72... | collective-permute-start | bytes 393224 | tf_op jit(solution)/shard_map/ppermute | solution.py:319
  33.5 10.9 %collective-permute-start.4 = (bf16[2,256,256]{2,1,0:T(8,128)(2,1)S(1)}, bf16[2,256,256]{2,1,0:T(8,128)(2,1)S(1)}, u32[]{:S(2)}, u32[]{:S(2)}) collective-permute-start(bf16[2,256,256]{2,1,0:T(8,128)(2,1)S(1)} %pad_maximum_fusion.refs_0_), channel_id=1, source_target_pairs={{0,14},{2,0},{4,2},{6,4},{8,6},{10,8},{12,10},{14,12},{1,15},{3,1}... | collective-permute-start | bytes 786440 | tf_op jit(solution)/shard_map/ppermute | solution.py:25
  38.9 9.7 %collective-permute-start.3 = (bf16[2,256,256]{2,1,0:T(8,128)(2,1)S(1)}, bf16[2,256,256]{2,1,0:T(8,128)(2,1)S(1)}, u32[]{:S(2)}, u32[]{:S(2)}) collective-permute-start(bf16[2,256,256]{2,1,0:T(8,128)(2,1)S(1)} %pad_maximum_fusion.refs_0_), channel_id=1, source_target_pairs={{0,2},{2,4},{4,6},{6,8},{8,10},{10,12},{12,14},{14,0},{1,3},{3,5},... | collective-permute-start | bytes 786440 | tf_op jit(solution)/shard_map/ppermute | solution.py:25
  38.9 15.3 %collective-permute-start.13 = (bf16[2,256,256]{2,1,0:T(8,128)(2,1)S(1)}, bf16[2,256,256]{2,1,0:T(8,128)(2,1)S(1)}, u32[]{:S(2)}, u32[]{:S(2)}) collective-permute-start(bf16[2,256,256]{2,1,0:T(8,128)(2,1)S(1)} %pad_maximum_fusion.1.refs_0_), channel_id=1, source_target_pairs={{0,2},{2,4},{4,6},{6,8},{8,10},{10,12},{12,14},{14,0},{1,3},{3,5},... | collective-permute-start | bytes 786440 | tf_op jit(solution)/shard_map/ppermute | solution.py:25
  39.0 15.2 %collective-permute-start.14 = (bf16[2,256,256]{2,1,0:T(8,128)(2,1)S(1)}, bf16[2,256,256]{2,1,0:T(8,128)(2,1)S(1)}, u32[]{:S(2)}, u32[]{:S(2)}) collective-permute-start(bf16[2,256,256]{2,1,0:T(8,128)(2,1)S(1)} %pad_maximum_fusion.1.refs_0_), channel_id=1, source_target_pairs={{0,14},{2,0},{4,2},{6,4},{8,6},{10,8},{12,10},{14,12},{1,15},{3,1}... | collective-permute-start | bytes 786440 | tf_op jit(solution)/shard_map/ppermute | solution.py:25
  44.4 12.5 %collective-permute-start.6 = (bf16[2,256,256]{2,1,0:T(8,128)(2,1)S(1)}, bf16[2,256,256]{2,1,0:T(8,128)(2,1)S(1)}, u32[]{:S(2)}, u32[]{:S(2)}) collective-permute-start(bf16[2,256,256]{2,1,0:T(8,128)(2,1)S(1)} %collective-permute-done.4.refs_2_), channel_id=1, source_target_pairs={{0,14},{2,0},{4,2},{6,4},{8,6},{10,8},{12,10},{14,12},{1,15},{3,1}... | collective-permute-start | bytes 786440 | tf_op jit(solution)/shard_map/ppermute | solution.py:25
  48.6 11.2 %collective-permute-start.5 = (bf16[2,256,256]{2,1,0:T(8,128)(2,1)S(1)}, bf16[2,256,256]{2,1,0:T(8,128)(2,1)S(1)}, u32[]{:S(2)}, u32[]{:S(2)}) collective-permute-start(bf16[2,256,256]{2,1,0:T(8,128)(2,1)S(1)} %collective-permute-done.3.refs_1_), channel_id=1, source_target_pairs={{0,2},{2,4},{4,6},{6,8},{8,10},{10,12},{12,14},{14,0},{1,3},{3,5},... | collective-permute-start | bytes 786440 | tf_op jit(solution)/shard_map/ppermute | solution.py:25
  54.2 11.2 %collective-permute-start.15 = (bf16[2,256,256]{2,1,0:T(8,128)(2,1)S(1)}, bf16[2,256,256]{2,1,0:T(8,128)(2,1)S(1)}, u32[]{:S(2)}, u32[]{:S(2)}) collective-permute-start(bf16[2,256,256]{2,1,0:T(8,128)(2,1)S(1)} %collective-permute-done.13.refs_1_), channel_id=1, source_target_pairs={{0,2},{2,4},{4,6},{6,8},{8,10},{10,12},{12,14},{14,0},{1,3},{3,5},... | collective-permute-start | bytes 786440 | tf_op jit(solution)/shard_map/ppermute | solution.py:25
  54.2 11.2 %collective-permute-start.16 = (bf16[2,256,256]{2,1,0:T(8,128)(2,1)S(1)}, bf16[2,256,256]{2,1,0:T(8,128)(2,1)S(1)}, u32[]{:S(2)}, u32[]{:S(2)}) collective-permute-start(bf16[2,256,256]{2,1,0:T(8,128)(2,1)S(1)} %collective-permute-done.14.refs_2_), channel_id=1, source_target_pairs={{0,14},{2,0},{4,2},{6,4},{8,6},{10,8},{12,10},{14,12},{1,15},{3,1}... | collective-permute-start | bytes 786440 | tf_op jit(solution)/shard_map/ppermute | solution.py:25
  56.9 11.3 %collective-permute-start.8 = (bf16[2,256,256]{2,1,0:T(8,128)(2,1)S(1)}, bf16[2,256,256]{2,1,0:T(8,128)(2,1)S(1)}, u32[]{:S(2)}, u32[]{:S(2)}) collective-permute-start(bf16[2,256,256]{2,1,0:T(8,128)(2,1)S(1)} %collective-permute-done.6.refs_4_), channel_id=1, source_target_pairs={{0,14},{2,0},{4,2},{6,4},{8,6},{10,8},{12,10},{14,12},{1,15},{3,1}... | collective-permute-start | bytes 786440 | tf_op jit(solution)/shard_map/ppermute | solution.py:25
  59.8 11.2 %collective-permute-start.7 = (bf16[2,256,256]{2,1,0:T(8,128)(2,1)S(1)}, bf16[2,256,256]{2,1,0:T(8,128)(2,1)S(1)}, u32[]{:S(2)}, u32[]{:S(2)}) collective-permute-start(bf16[2,256,256]{2,1,0:T(8,128)(2,1)S(1)} %collective-permute-done.5.refs_3_), channel_id=1, source_target_pairs={{0,2},{2,4},{4,6},{6,8},{8,10},{10,12},{12,14},{14,0},{1,3},{3,5},... | collective-permute-start | bytes 786440 | tf_op jit(solution)/shard_map/ppermute | solution.py:25
  65.4 10.0 %collective-permute-start.17 = (bf16[2,256,256]{2,1,0:T(8,128)(2,1)S(1)}, bf16[2,256,256]{2,1,0:T(8,128)(2,1)S(1)}, u32[]{:S(2)}, u32[]{:S(2)}) collective-permute-start(bf16[2,256,256]{2,1,0:T(8,128)(2,1)S(1)} %collective-permute-done.15.refs_3_), channel_id=1, source_target_pairs={{0,2},{2,4},{4,6},{6,8},{8,10},{10,12},{12,14},{14,0},{1,3},{3,5},... | collective-permute-start | bytes 786440 | tf_op jit(solution)/shard_map/ppermute | solution.py:25
  65.5 10.7 %collective-permute-start.18 = (bf16[2,256,256]{2,1,0:T(8,128)(2,1)S(1)}, bf16[2,256,256]{2,1,0:T(8,128)(2,1)S(1)}, u32[]{:S(2)}, u32[]{:S(2)}) collective-permute-start(bf16[2,256,256]{2,1,0:T(8,128)(2,1)S(1)} %collective-permute-done.16.refs_4_), channel_id=1, source_target_pairs={{0,14},{2,0},{4,2},{6,4},{8,6},{10,8},{12,10},{14,12},{1,15},{3,1}... | collective-permute-start | bytes 786440 | tf_op jit(solution)/shard_map/ppermute | solution.py:25
  68.2 11.4 %collective-permute-start.10 = (bf16[2,128,256]{2,1,0:T(8,128)(2,1)S(1)}, bf16[2,128,256]{2,1,0:T(8,128)(2,1)S(1)}, u32[]{:S(2)}, u32[]{:S(2)}) collective-permute-start(bf16[2,128,256]{2,1,0:T(8,128)(2,1)S(1)} %slice.26), channel_id=1, source_target_pairs={{0,14},{2,0},{4,2},{6,4},{8,6},{10,8},{12,10},{14,12},{1,15},{3,1}... | collective-permute-start | bytes 393224 | tf_op jit(solution)/shard_map/ppermute | solution.py:25
  71.1 9.2 %collective-permute-start.9 = (bf16[2,128,256]{2,1,0:T(8,128)(2,1)S(1)}, bf16[2,128,256]{2,1,0:T(8,128)(2,1)}, u32[]{:S(2)}, u32[]{:S(2)}) collective-permute-start(bf16[2,128,256]{2,1,0:T(8,128)(2,1)S(1)} %slice.25), channel_id=1, source_target_pairs={{0,2},{2,4},{4,6},{6,8},{8,10},{10,12},{12,14},{14,0},{1,3},{3,5},... | collective-permute-start | bytes 393224 | tf_op jit(solution)/shard_map/ppermute | solution.py:25
  76.2 9.5 %collective-permute-start.19 = (bf16[2,128,256]{2,1,0:T(8,128)(2,1)}, bf16[2,128,256]{2,1,0:T(8,128)(2,1)}, u32[]{:S(2)}, u32[]{:S(2)}) collective-permute-start(bf16[2,128,256]{2,1,0:T(8,128)(2,1)} %slice.28), channel_id=1, source_target_pairs={{0,2},{2,4},{4,6},{6,8},{8,10},{10,12},{12,14},{14,0},{1,3},{3,5},... | collective-permute-start | bytes 393224 | tf_op jit(solution)/shard_map/ppermute | solution.py:25
  76.9 8.8 %collective-permute-start.20 = (bf16[2,128,256]{2,1,0:T(8,128)(2,1)}, bf16[2,128,256]{2,1,0:T(8,128)(2,1)}, u32[]{:S(2)}, u32[]{:S(2)}) collective-permute-start(bf16[2,128,256]{2,1,0:T(8,128)(2,1)} %slice.29), channel_id=1, source_target_pairs={{0,14},{2,0},{4,2},{6,4},{8,6},{10,8},{12,10},{14,12},{1,15},{3,1}... | collective-permute-start | bytes 393224 | tf_op jit(solution)/shard_map/ppermute | solution.py:25
  92.8 6.7 %collective-permute-start.24 = (bf16[512,128]{1,0:T(8,128)(2,1)S(1)}, bf16[512,128]{1,0:T(8,128)(2,1)S(1)}, u32[]{:S(2)}, u32[]{:S(2)}) collective-permute-start(bf16[512,128]{1,0:T(8,128)(2,1)S(1)} %get-tuple-element.47), channel_id=1, source_target_pairs={{0,128},{128,0},{1,129},{129,1},{2,130},{130,2},{3,131},{131,3},{4... | collective-permute-start | bytes 393224 | tf_op jit(solution)/shard_map/ppermute | solution.py:25
  96.7 6.3 %collective-permute-start.23 = (bf16[512,128]{1,0:T(8,128)(2,1)S(1)}, bf16[512,128]{1,0:T(8,128)(2,1)S(1)}, u32[]{:S(2)}, u32[]{:S(2)}) collective-permute-start(bf16[512,128]{1,0:T(8,128)(2,1)S(1)} %get-tuple-element.49), channel_id=1, source_target_pairs={{0,128},{128,0},{1,129},{129,1},{2,130},{130,2},{3,131},{131,3},{4... | collective-permute-start | bytes 393224 | tf_op jit(solution)/shard_map/ppermute | solution.py:25
  106.2 8.2 %collective-permute-start.25 = (bf16[2,512,128]{2,1,0:T(8,128)(2,1)S(1)}, bf16[2,512,128]{2,1,0:T(8,128)(2,1)S(1)}, u32[]{:S(2)}, u32[]{:S(2)}) collective-permute-start(bf16[2,512,128]{2,1,0:T(8,128)(2,1)S(1)} %get-tuple-element.33), channel_id=1, source_target_pairs={{0,128},{128,0},{1,129},{129,1},{2,130},{130,2},{3,131},{131,3},{4... | collective-permute-start | bytes 786440 | tf_op jit(solution)/shard_map/ppermute | solution.py:25
  108.2 8.3 %collective-permute-start.26 = (bf16[2,512,128]{2,1,0:T(8,128)(2,1)S(1)}, bf16[2,512,128]{2,1,0:T(8,128)(2,1)S(1)}, u32[]{:S(2)}, u32[]{:S(2)}) collective-permute-start(bf16[2,512,128]{2,1,0:T(8,128)(2,1)S(1)} %get-tuple-element.32.refs_0_), channel_id=1, source_target_pairs={{0,1},{1,0},{2,3},{3,2},{4,5},{5,4},{6,7},{7,6},{8,9},{9,8},{10,11... | collective-permute-start | bytes 786440 | tf_op jit(solution)/shard_map/ppermute | solution.py:25
  121.3 8.5 %collective-permute-start.32 = (bf16[64,2048]{1,0:T(8,128)(2,1)S(1)}, bf16[64,2048]{1,0:T(8,128)(2,1)S(1)}, u32[]{:S(2)}, u32[]{:S(2)}) collective-permute-start(bf16[64,2048]{1,0:T(8,128)(2,1)S(1)} %get-tuple-element.42), channel_id=1, source_target_pairs={{0,48},{16,0},{32,16},{48,32},{1,49},{17,1},{33,17},{49,33},{2,50}... | collective-permute-start | bytes 786440 | tf_op jit(solution)/shard_map/ppermute | solution.py:25
  122.5 9.5 %collective-permute-start.28 = (bf16[64,2048]{1,0:T(8,128)(2,1)S(1)}, bf16[64,2048]{1,0:T(8,128)(2,1)S(1)}, u32[]{:S(2)}, u32[]{:S(2)}) collective-permute-start(bf16[64,2048]{1,0:T(8,128)(2,1)S(1)} %get-tuple-element.38), channel_id=1, source_target_pairs={{0,16},{16,32},{32,48},{48,0},{1,17},{17,33},{33,49},{49,1},{2,18}... | collective-permute-start | bytes 786440 | tf_op jit(solution)/shard_map/ppermute | solution.py:25
  127.0 9.8 %collective-permute-start.30 = (bf16[64,2048]{1,0:T(8,128)(2,1)}, bf16[64,2048]{1,0:T(8,128)(2,1)S(1)}, u32[]{:S(2)}, u32[]{:S(2)}) collective-permute-start(bf16[64,2048]{1,0:T(8,128)(2,1)} %get-tuple-element.39), channel_id=1, source_target_pairs={{0,16},{16,32},{32,48},{48,0},{1,17},{17,33},{33,49},{49,1},{2,18}... | collective-permute-start | bytes 786440 | tf_op jit(solution)/shard_map/ppermute | solution.py:25
  127.1 9.8 %collective-permute-start.31 = (bf16[64,2048]{1,0:T(8,128)(2,1)S(1)}, bf16[64,2048]{1,0:T(8,128)(2,1)S(1)}, u32[]{:S(2)}, u32[]{:S(2)}) collective-permute-start(bf16[64,2048]{1,0:T(8,128)(2,1)S(1)} %get-tuple-element.40), channel_id=1, source_target_pairs={{0,48},{16,0},{32,16},{48,32},{1,49},{17,1},{33,17},{49,33},{2,50}... | collective-permute-start | bytes 786440 | tf_op jit(solution)/shard_map/ppermute | solution.py:25
  130.5 9.3 %collective-permute-start.33 = (bf16[64,2048]{1,0:T(8,128)(2,1)}, bf16[64,2048]{1,0:T(8,128)(2,1)S(1)}, u32[]{:S(2)}, u32[]{:S(2)}) collective-permute-start(bf16[64,2048]{1,0:T(8,128)(2,1)} %add_convert_fusion), channel_id=1, source_target_pairs={{0,48},{16,0},{32,16},{48,32},{1,49},{17,1},{33,17},{49,33},{2,50}... | collective-permute-start | bytes 786440 | tf_op jit(solution)/shard_map/ppermute | solution.py:25
  132.7 9.3 %collective-permute-start.29 = (bf16[64,2048]{1,0:T(8,128)(2,1)}, bf16[64,2048]{1,0:T(8,128)(2,1)S(1)}, u32[]{:S(2)}, u32[]{:S(2)}) collective-permute-start(bf16[64,2048]{1,0:T(8,128)(2,1)} %add_convert_fusion.1), channel_id=1, source_target_pairs={{0,16},{16,32},{32,48},{48,0},{1,17},{17,33},{33,49},{49,1},{2,18}... | collective-permute-start | bytes 786440 | tf_op jit(solution)/shard_map/ppermute | solution.py:25
  (32 other events, 458.2 us)
Sparse Core Ops, SparseCore 0:
  21.2 55.5 all-gather.2

commit v4 on v3

--- a/solution.py
+++ b/solution.py
@@ -15,7 +15,7 @@
 F32 = jnp.float32
 MIB = 1024 * 1024
 META = 16
-PIECES = 9
+PIECES = 8
 BLOCKS = 4
 PROJECT_LIMIT = 56
 
@@ -106,13 +106,14 @@
     cotan_ref,
     gain_ref,
     square_ref,
+    other_ref,
     earlier_ref,
     inverse_ref,
     out_ref,
 ):
     at_encoder = place_ref[0] == 0
     row_count, half_width = rows_ref.shape
-    inverse = lax.rsqrt(square_ref[...] / (2 * half_width) + EPS)
+    inverse = lax.rsqrt((square_ref[...] + other_ref[...]) / (2 * half_width) + EPS)
     inverse_ref[...] = inverse
     first_count = row_count - jnp.sum(segments_ref[...].astype(F32), -1, keepdims=True)
     at = lax.broadcasted_iota(jnp.int32, (META, half_width), 1)
@@ -136,7 +137,7 @@
                     out_ref[pl.ds(part * row_count, row_count), pl.ds(start, tile)] = moved.astype(BF)
 
 
-def prepare(place, lengths, segments, rows, cotan, gain, square, earlier):
+def prepare(place, lengths, segments, rows, cotan, gain, square, other, earlier):
     whole = pl.BlockSpec(memory_space=pltpu.VMEM)
     scalars = pl.BlockSpec(memory_space=pltpu.SMEM)
     return pl.pallas_call(
@@ -145,10 +146,10 @@
             jax.ShapeDtypeStruct(square.shape, F32),
             jax.ShapeDtypeStruct((2 * rows.shape[0] + META, rows.shape[1]), BF),
         ),
-        in_specs=[scalars, scalars] + [whole] * 5 + [pl.BlockSpec(memory_space=pl.ANY)],
+        in_specs=[scalars, scalars] + [whole] * 6 + [pl.BlockSpec(memory_space=pl.ANY)],
         out_specs=(whole, whole),
         compiler_params=pltpu.CompilerParams(vmem_limit_bytes=5 * MIB),
-    )(place, lengths, segments, rows, cotan, gain, square, earlier)
+    )(place, lengths, segments, rows, cotan, gain, square, other, earlier)
 
 
 def join(refs, pick):
@@ -197,14 +198,11 @@
     distances = [0]
     for step in range(1, z_size // 2):
         distances += [-step, step]
+    distances.append(z_size // 2)
     pairs = [
         (ref, weight_ref.at[:, lax.rem(own_z + distance + z_size, z_size)])
         for ref, distance in zip(piece_refs, distances)
     ]
-    far = lax.rem(own_z + z_size // 2, z_size)
-    half = piece_refs[-1].shape[1]
-    for at in range(2):
-        pairs.append((piece_refs[at - 2], weight_ref.at[:, far, pl.ds(at * half, half)]))
     return [
         pltpu.make_async_copy(source, there, sems.at[at]) for at, (source, there) in enumerate(pairs)
     ]
@@ -212,7 +210,8 @@
 
 def project_kernel(part, place_ref, gathered_ref, *refs):
     piece_refs = refs[:PIECES]
-    own_ref, other_ref, meta_ref, out_ref, left_ref, weight_ref, left_sems, sems = refs[PIECES:]
+    own_ref, other_ref, meta_ref, *out_refs = refs[PIECES : PIECES + 5]
+    left_ref, weight_ref, left_sems, sems = refs[PIECES + 5 :]
     blocks = gathered_ref.shape[0]
     rows = left_ref.shape[0] // blocks
     copies = []
@@ -228,8 +227,12 @@
         copy.start()
     for copy in copies:
         copy.wait()
-    assembled = pltpu.make_async_copy(weight_ref, out_ref, left_sems.at[2, 0])
-    assembled.start()
+    assembled = [
+        pltpu.make_async_copy(weight_ref.at[at], ref, left_sems.at[2, at])
+        for at, ref in enumerate(out_refs)
+    ]
+    for copy in assembled:
+        copy.start()
     half = own_ref.shape[2]
     z_size, depth, width = weight_ref.shape[1:]
     for columns, ref in ((1, other_ref), (0, own_ref)):
@@ -237,7 +240,8 @@
         product = dot(left_ref[...], weights, ((1,), (0,)))
         for at in range(2):
             ref[at] = product[:, at * half : (at + 1) * half].astype(ref.dtype)
-    assembled.wait()
+    for copy in assembled:
+        copy.wait()
 
 
 def project(part, place, gathered, pieces):
@@ -253,11 +257,11 @@
             jax.ShapeDtypeStruct(shape, F32),
             jax.ShapeDtypeStruct(shape, BF),
             jax.ShapeDtypeStruct((blocks, META, 2 * HD), BF),
-            jax.ShapeDtypeStruct(weights, BF),
-        ),
+        )
+        + (jax.ShapeDtypeStruct(weights[1:], BF),) * 2,
         in_specs=[pl.BlockSpec(memory_space=pltpu.SMEM)]
         + [pl.BlockSpec(memory_space=pltpu.HBM)] * (1 + len(pieces)),
-        out_specs=(whole, whole, whole, pl.BlockSpec(memory_space=pltpu.HBM)),
+        out_specs=(whole,) * 3 + (pl.BlockSpec(memory_space=pltpu.HBM),) * 2,
         scratch_shapes=[
             pltpu.VMEM((blocks * rows, width), BF),
             pltpu.VMEM(weights, BF),
@@ -269,7 +273,7 @@
 
 
 def back_kernel(blocks, place_ref, *refs):
-    grad_refs, weight_refs, out_refs = refs[:4], refs[4:6], refs[6:]
+    grad_refs, weight_refs, out_refs = refs[:4], refs[4:8], refs[8:]
     at_encoder = place_ref[0] == 0
     rows = grad_refs[0].shape[1] // BLOCKS
     grads = []
@@ -282,11 +286,11 @@
             low = jnp.where(at_encoder, picked[0], picked[1])
             high = jnp.where(at_encoder, picked[1], picked[0])
             grads.append((part, columns, jnp.concatenate([low, high], 1)))
-    z_size, depth = weight_refs[0].shape[1:3]
+    z_size, depth = weight_refs[0].shape[:2]
     for z in range(z_size):
         total = 0.0
         for part, columns, grad in grads:
-            total += dot(grad, weight_refs[part][columns, z], ((1,), (1,)))
+            total += dot(grad, weight_refs[2 * part + columns][z], ((1,), (1,)))
         pick = pl.ds(z * depth, depth)
         start = 0
         for ref in out_refs:
@@ -312,7 +316,7 @@
     return weights.reshape(rows, parts, x_size, columns // x_size).transpose(2, 1, 0, 3)
 
 
-def gather_weights(chunk, at_source):
+def gather_weights(part, chunk, at_source):
     x_size, rows, columns = chunk.shape
     z_size = lax.axis_size("z")
     near = lax.ppermute(chunk, ("y", "mp"), [(1, 0), (2, 3), (0, 2), (3, 1)])
@@ -323,8 +327,7 @@
     for step in range(1, z_size // 2):
         up, down = shift(up, "z", 1), shift(down, "z", -1)
         pieces += [up, down]
-    half = x_size * rows // 2
-    return pieces + [shift(up[:, :half], "z", 1), shift(down[:, half:], "z", -1)]
+    return pieces + [shift(down, "z", -1) if part else shift(up, "z", 1)]
 
 
 def sum_over_x(far_low, far_high, own, near_low, near_high, last_low, last_high):
@@ -343,19 +346,19 @@
     wide_rows = rows.astype(F32)
 
     square = jnp.sum(wide_rows * wide_rows, -1, keepdims=True)
-    square = square + shift(square, "mp", 1)
+    other = shift(square, "mp", 1)
     slices = slice_columns(weights)
     chunks = lax.all_to_all(slices, "x", 0, 0, tiled=True)
     inverse, left = prepare(
-        place, enc_lengths, dec_segments, rows, cotan, norm_gains, square, chunks
+        place, enc_lengths, dec_segments, rows, cotan, norm_gains, square, other, chunks
     )
     gathered = lax.all_gather(left, "x")
-    pieces = [gather_weights(chunks[:, part], own_y == own_c) for part in range(2)]
+    pieces = [gather_weights(part, chunks[:, part], own_y == own_c) for part in range(2)]
 
     keep, recv, full = [], [], []
     for part in range(2):
-        own, other, meta, assembled = project(part, place, gathered, pieces[part])
-        full.append(assembled)
+        own, other, meta, *assembled = project(part, place, gathered, pieces[part])
+        full += assembled
         other = shift(other, "mp", 1)
 
         def half(at):

time: 155 us -> 156 us (level)
  local copies, waits for them, and re-layouts: 6.81 us -> 10.8 us
  starting transfers between devices: 53 us -> 55.9 us
  waiting for transfers between devices: 51.5 us -> 48.7 us
  other arithmetic: 6.94 us -> 4.33 us
    unnamed x54 -> x60, local copies, waits for them, and re-layouts: 3.3 us -> 8.82 us
    ppermute x31 -> x29, waiting for transfers between devices: 47.3 us -> 42.6 us  [shift(): lax.ppermute(block, axis, [(i, (i + distance) % size) for i in range(size)])]
    ppermute x31 -> x29, starting transfers between devices: 38.8 us -> 41.7 us  [shift(): lax.ppermute(block, axis, [(i, (i + distance) % size) for i in range(size)])]
    all_gather x1, waiting for transfers between devices: 0.01 us -> 1.82 us  [on_device(): gathered = lax.all_gather(left, 'x')]
  transfers between devices with their start and end apart: 37 -> 35, of which waited for: 19 -> 20; matrix products, arithmetic and copies ran while one was open for 4% -> 2% of each run, Pallas kernels for 9% -> 9%
where the time goes in v4:
time: 156 us
  starting transfers between devices  55.9 us (36%)
  waiting for transfers between devices  48.7 us (31%)
  Pallas kernels  22.2 us (14%)
  between operations  13.8 us (9%)
  local copies, waits for them, and re-layouts  10.8 us (7%)
  other arithmetic  4.33 us (3%)
    ppermute x29, waiting for transfers between devices, shift(): lax.ppermute(block, axis, [(i, (i + distance) % size) for i in range(size)])  42.6 us
    ppermute x29, starting transfers between devices, shift(): lax.ppermute(block, axis, [(i, (i + distance) % size) for i in range(size)])  41.7 us
    pallas_call x2, Pallas kernels, project(): pl.pallas_call(functools.partial(project_kernel, part), out_shape=(jax.Sh...  10.6 us
    unnamed x60, local copies, waits for them, and re-layouts  8.82 us
    ppermute x2, starting transfers between devices, gather_weights(): far = lax.ppermute(chunk, ('y', 'mp'), [(1, 2), (2, 1)])  5.55 us
    pallas_call x2, Pallas kernels, back_project(): pl.pallas_call(functools.partial(back_kernel, blocks), out_shape=outs, in...  5.04 us
    all_to_all x1, starting transfers between devices, on_device(): chunks = lax.all_to_all(slices, 'x', 0, 0, tiled=True)  4.84 us
    ppermute x2, starting transfers between devices, gather_weights(): near = lax.ppermute(chunk, ('y', 'mp'), [(1, 0), (2, 3), (0, 2), (3, 1)])  3.77 us
  transfers between devices with their start and end apart: 35, of which 20 were waited for; matrix products, arithmetic and copies ran while one was open for 2% of the time, Pallas kernels for 9%

profile of v4, /device:TPU:1, one launch (start us, length us, event | category | flops | bytes accessed | tf_op | source)
XLA Modules:
  0.0 155.7 jit_solution(7874158953088764248)
XLA Ops:
  8.4 4.8 %all-to-all-start = ((bf16[4,2,64,256]{3,2,1,0:T(8,128)(2,1)}), bf16[4,2,64,256]{3,2,1,0:T(8,128)(2,1)S(1)}, u32[]{:S(2)}, u32[]{:S(2)}) async-start(bf16[4,2,64,256]{3,2,1,0:T(8,128)(2,1)} %bitcast.36), calls=%async_computation | async-start | bytes 524288 | tf_op jit(solution)/shard_map/all_to_all | solution.py:351
  14.6 1.9 %collective-permute-start = (f32[128,1]{1,0:T(8,128)S(1)}, f32[128,1]{1,0:T(8,128)S(1)}, u32[]{:S(2)}, u32[]{:S(2)}) collective-permute-start(f32[128,1]{1,0:T(8,128)S(1)} %copy.13.square_ref), channel_id=1, source_target_pairs={{0,1},{1,0},{2,3},{3,2},{4,5},{5,4},{6,7},{7,6},{8,9},{9,8},{10,11... | collective-permute-start | bytes 1544 | tf_op jit(solution)/shard_map/ppermute | solution.py:25
  22.9 2.2 %shard_map.64 = (f32[128,1]{1,0:T(8,128)S(1)}, bf16[272,2048]{1,0:T(8,128)(2,1)}) custom-call(s32[3]{0:T(128)S(1)} %pad_add_fusion.place_ref, s32[1,2]{1,0:T(1,128)S(1)} %copy-done.15, s32[1,128]{1,0:T(1,128)S(1)} %copy-done.16, bf16[128,2048]{1,0:T(8,128)(2,1)S(1)} %bitcast.37, bf16[128,2048]{1,0:T(8,128)(2,1)S(1)} %bitcast.39, ...), custom_call_target="tpu_custom_call" | custom-call | tf_op jit(solution)/shard_map/pallas_call | solution.py:143
  25.1 3.0 %collective-permute-start.1 = (bf16[4,64,256]{2,1,0:T(8,128)(2,1)S(1)}, bf16[4,64,256]{2,1,0:T(8,128)(2,1)S(1)}, u32[]{:S(2)}, u32[]{:S(2)}) collective-permute-start(bf16[4,64,256]{2,1,0:T(8,128)(2,1)S(1)} %get-tuple-element.58), channel_id=1, source_target_pairs={{1,0},{64,65},{0,64},{65,1},{3,2},{66,67},{2,66},{67,3},{5,4},{68,... | collective-permute-start | bytes 393224 | tf_op jit(solution)/shard_map/ppermute | solution.py:322
  28.9 1.9 %collective-permute-start.11 = (bf16[4,64,256]{2,1,0:T(8,128)(2,1)S(1)}, bf16[4,64,256]{2,1,0:T(8,128)(2,1)S(1)}, u32[]{:S(2)}, u32[]{:S(2)}) collective-permute-start(bf16[4,64,256]{2,1,0:T(8,128)(2,1)S(1)} %get-tuple-element.57), channel_id=1, source_target_pairs={{1,64},{64,1},{3,66},{66,3},{5,68},{68,5},{7,70},{70,7},{9,72},{72... | collective-permute-start | bytes 393224 | tf_op jit(solution)/shard_map/ppermute | solution.py:323
  30.8 3.6 %collective-permute-start.2 = (bf16[4,64,256]{2,1,0:T(8,128)(2,1)S(1)}, bf16[4,64,256]{2,1,0:T(8,128)(2,1)S(1)}, u32[]{:S(2)}, u32[]{:S(2)}) collective-permute-start(bf16[4,64,256]{2,1,0:T(8,128)(2,1)S(1)} %get-tuple-element.58), channel_id=1, source_target_pairs={{1,64},{64,1},{3,66},{66,3},{5,68},{68,5},{7,70},{70,7},{9,72},{72... | collective-permute-start | bytes 393224 | tf_op jit(solution)/shard_map/ppermute | solution.py:323
  35.1 2.2 %collective-permute-done.2 = bf16[4,64,256]{2,1,0:T(8,128)(2,1)S(1)} collective-permute-done((bf16[4,64,256]{2,1,0:T(8,128)(2,1)S(1)}, bf16[4,64,256]{2,1,0:T(8,128)(2,1)S(1)}, u32[]{:S(2)}, u32[]{:S(2)}) %collective-permute-start.2) | collective-permute-done | bytes 131104 | tf_op jit(solution)/shard_map/ppermute | solution.py:323
  37.4 5.4 %collective-permute-start.4 = (bf16[2,256,256]{2,1,0:T(8,128)(2,1)S(1)}, bf16[2,256,256]{2,1,0:T(8,128)(2,1)S(1)}, u32[]{:S(2)}, u32[]{:S(2)}) collective-permute-start(bf16[2,256,256]{2,1,0:T(8,128)(2,1)S(1)} %pad_maximum_fusion.refs_0_), channel_id=1, source_target_pairs={{0,14},{2,0},{4,2},{6,4},{8,6},{10,8},{12,10},{14,12},{1,15},{3,1}... | collective-permute-start | bytes 786440 | tf_op jit(solution)/shard_map/ppermute | solution.py:25
  43.0 3.1 %collective-permute-done.4.refs_2_ = bf16[2,256,256]{2,1,0:T(8,128)(2,1)S(1)} collective-permute-done((bf16[2,256,256]{2,1,0:T(8,128)(2,1)S(1)}, bf16[2,256,256]{2,1,0:T(8,128)(2,1)S(1)}, u32[]{:S(2)}, u32[]{:S(2)}) %collective-permute-start.4) | collective-permute-done | bytes 262176 | tf_op jit(solution)/shard_map/ppermute | solution.py:25
  46.1 3.5 %collective-permute-start.6 = (bf16[2,256,256]{2,1,0:T(8,128)(2,1)S(1)}, bf16[2,256,256]{2,1,0:T(8,128)(2,1)S(1)}, u32[]{:S(2)}, u32[]{:S(2)}) collective-permute-start(bf16[2,256,256]{2,1,0:T(8,128)(2,1)S(1)} %collective-permute-done.4.refs_2_), channel_id=1, source_target_pairs={{0,14},{2,0},{4,2},{6,4},{8,6},{10,8},{12,10},{14,12},{1,15},{3,1}... | collective-permute-start | bytes 786440 | tf_op jit(solution)/shard_map/ppermute | solution.py:25
  49.7 3.0 %collective-permute-done.12.refs_1_ = bf16[2,256,256]{2,1,0:T(8,128)(2,1)S(1)} collective-permute-done((bf16[2,256,256]{2,1,0:T(8,128)(2,1)S(1)}, bf16[2,256,256]{2,1,0:T(8,128)(2,1)S(1)}, u32[]{:S(2)}, u32[]{:S(2)}) %collective-permute-start.12) | collective-permute-done | bytes 262176 | tf_op jit(solution)/shard_map/ppermute | solution.py:25
  52.6 5.6 %collective-permute-done.3.refs_1_ = bf16[2,256,256]{2,1,0:T(8,128)(2,1)S(1)} collective-permute-done((bf16[2,256,256]{2,1,0:T(8,128)(2,1)S(1)}, bf16[2,256,256]{2,1,0:T(8,128)(2,1)S(1)}, u32[]{:S(2)}, u32[]{:S(2)}) %collective-permute-start.3) | collective-permute-done | bytes 262176 | tf_op jit(solution)/shard_map/ppermute | solution.py:25
  58.3 2.7 %collective-permute-start.8 = (bf16[2,256,256]{2,1,0:T(8,128)(2,1)S(1)}, bf16[2,256,256]{2,1,0:T(8,128)(2,1)S(1)}, u32[]{:S(2)}, u32[]{:S(2)}) collective-permute-start(bf16[2,256,256]{2,1,0:T(8,128)(2,1)S(1)} %collective-permute-done.6.refs_4_), channel_id=1, source_target_pairs={{0,14},{2,0},{4,2},{6,4},{8,6},{10,8},{12,10},{14,12},{1,15},{3,1}... | collective-permute-start | bytes 786440 | tf_op jit(solution)/shard_map/ppermute | solution.py:25
  61.3 3.5 %collective-permute-start.15 = (bf16[2,256,256]{2,1,0:T(8,128)(2,1)S(1)}, bf16[2,256,256]{2,1,0:T(8,128)(2,1)}, u32[]{:S(2)}, u32[]{:S(2)}) collective-permute-start(bf16[2,256,256]{2,1,0:T(8,128)(2,1)S(1)} %collective-permute-done.13.refs_2_), channel_id=1, source_target_pairs={{0,14},{2,0},{4,2},{6,4},{8,6},{10,8},{12,10},{14,12},{1,15},{3,1}... | collective-permute-start | bytes 786440 | tf_op jit(solution)/shard_map/ppermute | solution.py:25
  64.8 3.1 %collective-permute-done.5.refs_3_ = bf16[2,256,256]{2,1,0:T(8,128)(2,1)S(1)} collective-permute-done((bf16[2,256,256]{2,1,0:T(8,128)(2,1)S(1)}, bf16[2,256,256]{2,1,0:T(8,128)(2,1)S(1)}, u32[]{:S(2)}, u32[]{:S(2)}) %collective-permute-start.5) | collective-permute-done | bytes 262176 | tf_op jit(solution)/shard_map/ppermute | solution.py:25
  68.0 2.7 %collective-permute-start.9 = (bf16[2,256,256]{2,1,0:T(8,128)(2,1)S(1)}, bf16[2,256,256]{2,1,0:T(8,128)(2,1)S(1)}, u32[]{:S(2)}, u32[]{:S(2)}) collective-permute-start(bf16[2,256,256]{2,1,0:T(8,128)(2,1)S(1)} %collective-permute-done.8.refs_6_), channel_id=1, source_target_pairs={{0,14},{2,0},{4,2},{6,4},{8,6},{10,8},{12,10},{14,12},{1,15},{3,1}... | collective-permute-start | bytes 786440 | tf_op jit(solution)/shard_map/ppermute | solution.py:25
  72.5 3.5 %collective-permute-start.17 = (bf16[2,256,256]{2,1,0:T(8,128)(2,1)}, bf16[2,256,256]{2,1,0:T(8,128)(2,1)}, u32[]{:S(2)}, u32[]{:S(2)}) collective-permute-start(bf16[2,256,256]{2,1,0:T(8,128)(2,1)} %collective-permute-done.15.refs_4_), channel_id=1, source_target_pairs={{0,14},{2,0},{4,2},{6,4},{8,6},{10,8},{12,10},{14,12},{1,15},{3,1}... | collective-permute-start | bytes 786440 | tf_op jit(solution)/shard_map/ppermute | solution.py:25
  76.1 2.9 %collective-permute-done.7.refs_5_ = bf16[2,256,256]{2,1,0:T(8,128)(2,1)S(1)} collective-permute-done((bf16[2,256,256]{2,1,0:T(8,128)(2,1)S(1)}, bf16[2,256,256]{2,1,0:T(8,128)(2,1)S(1)}, u32[]{:S(2)}, u32[]{:S(2)}) %collective-permute-start.7) | collective-permute-done | bytes 262176 | tf_op jit(solution)/shard_map/ppermute | solution.py:25
  80.8 5.3 %shard_map.65 = (f32[2,512,128]{2,1,0:T(8,128)}, bf16[2,512,128]{2,1,0:T(8,128)(2,1)}, bf16[4,16,128]{2,1,0:T(8,128)(2,1)}, bf16[8,256,256]{2,1,0:T(8,128)(2,1)}, bf16[8,256,256]{2,1,0:T(8,128)(2,1)}) custom-call(s32[3]{0:T(128)} %copy-done.12, bf16[4,272,2048]{2,1,0:T(8,128)(2,1)} %bitcast.41, bf16[2,256,256]{2,1,0:T(8,128)(2,1)} %copy-done.18, ...), custom_call_target="tpu_custom_call" | custom-call | tf_op jit(solution)/shard_map/pallas_call | solution.py:254
  87.0 5.3 %shard_map.66 = (f32[2,512,128]{2,1,0:T(8,128)}, bf16[2,512,128]{2,1,0:T(8,128)(2,1)}, bf16[4,16,128]{2,1,0:T(8,128)(2,1)}, bf16[8,256,256]{2,1,0:T(8,128)(2,1)}, bf16[8,256,256]{2,1,0:T(8,128)(2,1)}) custom-call(s32[3]{0:T(128)} %copy-done.12, bf16[4,272,2048]{2,1,0:T(8,128)(2,1)} %bitcast.42, bf16[2,256,256]{2,1,0:T(8,128)(2,1)} %copy-done.17, ...), custom_call_target="tpu_custom_call" | custom-call | tf_op jit(solution)/shard_map/pallas_call | solution.py:254
  92.6 2.8 %collective-permute-start.22 = (bf16[512,128]{1,0:T(8,128)(2,1)S(1)}, bf16[512,128]{1,0:T(8,128)(2,1)S(1)}, u32[]{:S(2)}, u32[]{:S(2)}) collective-permute-start(bf16[512,128]{1,0:T(8,128)(2,1)S(1)} %get-tuple-element.51), channel_id=1, source_target_pairs={{0,128},{128,0},{1,129},{129,1},{2,130},{130,2},{3,131},{131,3},{4... | collective-permute-start | bytes 393224 | tf_op jit(solution)/shard_map/ppermute | solution.py:25
  98.9 3.6 %collective-permute-done.21.refs_2_ = bf16[512,128]{1,0:T(8,128)(2,1)S(1)} collective-permute-done((bf16[512,128]{1,0:T(8,128)(2,1)S(1)}, bf16[512,128]{1,0:T(8,128)(2,1)S(1)}, u32[]{:S(2)}, u32[]{:S(2)}) %collective-permute-start.21) | collective-permute-done | bytes 131104 | tf_op jit(solution)/shard_map/ppermute | solution.py:25
  102.5 3.2 %shard_map.67 = (bf16[2,512,128]{2,1,0:T(8,128)(2,1)S(1)}, bf16[2,512,128]{2,1,0:T(8,128)(2,1)S(1)}) custom-call(s32[3]{0:T(128)S(1)} %copy-done.13, bf16[4,16,128]{2,1,0:T(8,128)(2,1)S(1)} %copy-done.14, bf16[512,128]{1,0:T(8,128)(2,1)S(1)} %get-tuple-element.54.refs_0_, bf16[512,128]{1,0:T(8,128)(2,1)S(1)} %get-tuple-element.52.refs_1_, ...), custom_call_target="tpu_custom_call" | custom-call | tf_op jit(solution)/shard_map/pallas_call | solution.py:84
  105.8 2.4 %collective-permute-start.23 = (bf16[2,512,128]{2,1,0:T(8,128)(2,1)S(1)}, bf16[2,512,128]{2,1,0:T(8,128)(2,1)S(1)}, u32[]{:S(2)}, u32[]{:S(2)}) collective-permute-start(bf16[2,512,128]{2,1,0:T(8,128)(2,1)S(1)} %get-tuple-element.35), channel_id=1, source_target_pairs={{0,128},{128,0},{1,129},{129,1},{2,130},{130,2},{3,131},{131,3},{4... | collective-permute-start | bytes 786440 | tf_op jit(solution)/shard_map/ppermute | solution.py:25
  109.2 4.4 %collective-permute-done.23.refs_1_ = bf16[2,512,128]{2,1,0:T(8,128)(2,1)S(1)} collective-permute-done((bf16[2,512,128]{2,1,0:T(8,128)(2,1)S(1)}, bf16[2,512,128]{2,1,0:T(8,128)(2,1)S(1)}, u32[]{:S(2)}, u32[]{:S(2)}) %collective-permute-start.23) | collective-permute-done | bytes 262176 | tf_op jit(solution)/shard_map/ppermute | solution.py:25
  113.7 2.4 %collective-permute-start.25 = (bf16[2,512,128]{2,1,0:T(8,128)(2,1)S(1)}, bf16[2,512,128]{2,1,0:T(8,128)(2,1)S(1)}, u32[]{:S(2)}, u32[]{:S(2)}) collective-permute-start(bf16[2,512,128]{2,1,0:T(8,128)(2,1)S(1)} %collective-permute-done.23.refs_1_), channel_id=1, source_target_pairs={{0,1},{1,0},{2,3},{3,2},{4,5},{5,4},{6,7},{7,6},{8,9},{9,8},{10,11... | collective-permute-start | bytes 786440 | tf_op jit(solution)/shard_map/ppermute | solution.py:25
  119.7 2.0 %shard_map.69 = (bf16[64,2048]{1,0:T(8,128)(2,1)S(1)}, bf16[64,2048]{1,0:T(8,128)(2,1)S(1)}) custom-call(s32[3]{0:T(128)S(1)} %copy-done.13, bf16[2,512,128]{2,1,0:T(8,128)(2,1)S(1)} %get-tuple-element.34.refs_0_, bf16[2,512,128]{2,1,0:T(8,128)(2,1)S(1)} %collective-permute-done.23.refs_1_, bf16[2,512,128]{2,1,0:T(8,128)(2,1)S(1)} %collective-permute-done.24.refs_2_, ...), custom_call_target="tpu_custom_call" | custom-call | tf_op jit(solution)/shard_map/pallas_call | solution.py:304
  123.3 3.0 %shard_map.68 = (f32[128,2048]{1,0:T(8,128)S(1)}, f32[64,2048]{1,0:T(8,128)S(1)}, bf16[64,2048]{1,0:T(8,128)(2,1)}, bf16[64,2048]{1,0:T(8,128)(2,1)S(1)}, f32[64,2048]{1,0:T(8,128)S(1)}) custom-call(s32[3]{0:T(128)S(1)} %copy-done.13, bf16[2,512,128]{2,1,0:T(8,128)(2,1)S(1)} %get-tuple-element.34.refs_0_, ...), custom_call_target="tpu_custom_call" | custom-call | tf_op jit(solution)/shard_map/pallas_call | solution.py:304
  127.9 2.1 %collective-permute-start.29 = (bf16[64,2048]{1,0:T(8,128)(2,1)S(1)}, bf16[64,2048]{1,0:T(8,128)(2,1)S(1)}, u32[]{:S(2)}, u32[]{:S(2)}) collective-permute-start(bf16[64,2048]{1,0:T(8,128)(2,1)S(1)} %get-tuple-element.44), channel_id=1, source_target_pairs={{0,48},{16,0},{32,16},{48,32},{1,49},{17,1},{33,17},{49,33},{2,50}... | collective-permute-start | bytes 786440 | tf_op jit(solution)/shard_map/ppermute | solution.py:25
  131.7 5.4 %collective-permute-done.28.refs_2_ = bf16[64,2048]{1,0:T(8,128)(2,1)S(1)} collective-permute-done((bf16[64,2048]{1,0:T(8,128)(2,1)}, bf16[64,2048]{1,0:T(8,128)(2,1)S(1)}, u32[]{:S(2)}, u32[]{:S(2)}) %collective-permute-start.28) | collective-permute-done | bytes 262176 | tf_op jit(solution)/shard_map/ppermute | solution.py:25
  137.1 3.0 %collective-permute-done.31.refs_4_ = bf16[64,2048]{1,0:T(8,128)(2,1)S(1)} collective-permute-done((bf16[64,2048]{1,0:T(8,128)(2,1)S(1)}, bf16[64,2048]{1,0:T(8,128)(2,1)S(1)}, u32[]{:S(2)}, u32[]{:S(2)}) %collective-permute-start.31) | collective-permute-done | bytes 262176 | tf_op jit(solution)/shard_map/ppermute | solution.py:25
  140.1 2.6 %collective-permute-done.27.refs_1_ = bf16[64,2048]{1,0:T(8,128)(2,1)S(1)} collective-permute-done((bf16[64,2048]{1,0:T(8,128)(2,1)S(1)}, bf16[64,2048]{1,0:T(8,128)(2,1)S(1)}, u32[]{:S(2)}, u32[]{:S(2)}) %collective-permute-start.27) | collective-permute-done | bytes 262176 | tf_op jit(solution)/shard_map/ppermute | solution.py:25
  (122 shorter events, 35.7 us)
Async XLA Ops:
  8.4 10.4 %all-to-all-start = ((bf16[4,2,64,256]{3,2,1,0:T(8,128)(2,1)}), bf16[4,2,64,256]{3,2,1,0:T(8,128)(2,1)S(1)}, u32[]{:S(2)}, u32[]{:S(2)}) async-start(bf16[4,2,64,256]{3,2,1,0:T(8,128)(2,1)} %bitcast.36), calls=%async_computation | async-start | bytes 524288 | tf_op jit(solution)/shard_map/all_to_all | solution.py:351
  13.2 67.5 %all-gather.3.cloned.1.call-start = ((), (), s32[]{:S(2)}) async-start(), calls=%async_computation.1 | async-start | bytes 5570560 | tf_op jit(solution)/shard_map/all_gather | solution.py:355
  25.1 9.3 %collective-permute-start.1 = (bf16[4,64,256]{2,1,0:T(8,128)(2,1)S(1)}, bf16[4,64,256]{2,1,0:T(8,128)(2,1)S(1)}, u32[]{:S(2)}, u32[]{:S(2)}) collective-permute-start(bf16[4,64,256]{2,1,0:T(8,128)(2,1)S(1)} %get-tuple-element.58), channel_id=1, source_target_pairs={{1,0},{64,65},{0,64},{65,1},{3,2},{66,67},{2,66},{67,3},{5,4},{68,... | collective-permute-start | bytes 393224 | tf_op jit(solution)/shard_map/ppermute | solution.py:322
  28.1 6.3 %collective-permute-start.10 = (bf16[4,64,256]{2,1,0:T(8,128)(2,1)S(1)}, bf16[4,64,256]{2,1,0:T(8,128)(2,1)S(1)}, u32[]{:S(2)}, u32[]{:S(2)}) collective-permute-start(bf16[4,64,256]{2,1,0:T(8,128)(2,1)S(1)} %get-tuple-element.57), channel_id=1, source_target_pairs={{1,0},{64,65},{0,64},{65,1},{3,2},{66,67},{2,66},{67,3},{5,4},{68,... | collective-permute-start | bytes 393224 | tf_op jit(solution)/shard_map/ppermute | solution.py:322
  28.9 6.3 %collective-permute-start.11 = (bf16[4,64,256]{2,1,0:T(8,128)(2,1)S(1)}, bf16[4,64,256]{2,1,0:T(8,128)(2,1)S(1)}, u32[]{:S(2)}, u32[]{:S(2)}) collective-permute-start(bf16[4,64,256]{2,1,0:T(8,128)(2,1)S(1)} %get-tuple-element.57), channel_id=1, source_target_pairs={{1,64},{64,1},{3,66},{66,3},{5,68},{68,5},{7,70},{70,7},{9,72},{72... | collective-permute-start | bytes 393224 | tf_op jit(solution)/shard_map/ppermute | solution.py:323
  30.8 6.6 %collective-permute-start.2 = (bf16[4,64,256]{2,1,0:T(8,128)(2,1)S(1)}, bf16[4,64,256]{2,1,0:T(8,128)(2,1)S(1)}, u32[]{:S(2)}, u32[]{:S(2)}) collective-permute-start(bf16[4,64,256]{2,1,0:T(8,128)(2,1)S(1)} %get-tuple-element.58), channel_id=1, source_target_pairs={{1,64},{64,1},{3,66},{66,3},{5,68},{68,5},{7,70},{70,7},{9,72},{72... | collective-permute-start | bytes 393224 | tf_op jit(solution)/shard_map/ppermute | solution.py:323
  37.4 8.7 %collective-permute-start.4 = (bf16[2,256,256]{2,1,0:T(8,128)(2,1)S(1)}, bf16[2,256,256]{2,1,0:T(8,128)(2,1)S(1)}, u32[]{:S(2)}, u32[]{:S(2)}) collective-permute-start(bf16[2,256,256]{2,1,0:T(8,128)(2,1)S(1)} %pad_maximum_fusion.refs_0_), channel_id=1, source_target_pairs={{0,14},{2,0},{4,2},{6,4},{8,6},{10,8},{12,10},{14,12},{1,15},{3,1}... | collective-permute-start | bytes 786440 | tf_op jit(solution)/shard_map/ppermute | solution.py:25
  42.8 9.8 %collective-permute-start.12 = (bf16[2,256,256]{2,1,0:T(8,128)(2,1)S(1)}, bf16[2,256,256]{2,1,0:T(8,128)(2,1)S(1)}, u32[]{:S(2)}, u32[]{:S(2)}) collective-permute-start(bf16[2,256,256]{2,1,0:T(8,128)(2,1)S(1)} %pad_maximum_fusion.1.refs_0_), channel_id=1, source_target_pairs={{0,2},{2,4},{4,6},{6,8},{8,10},{10,12},{12,14},{14,0},{1,3},{3,5},... | collective-permute-start | bytes 786440 | tf_op jit(solution)/shard_map/ppermute | solution.py:25
  42.9 15.3 %collective-permute-start.3 = (bf16[2,256,256]{2,1,0:T(8,128)(2,1)S(1)}, bf16[2,256,256]{2,1,0:T(8,128)(2,1)S(1)}, u32[]{:S(2)}, u32[]{:S(2)}) collective-permute-start(bf16[2,256,256]{2,1,0:T(8,128)(2,1)S(1)} %pad_maximum_fusion.refs_0_), channel_id=1, source_target_pairs={{0,2},{2,4},{4,6},{6,8},{8,10},{10,12},{12,14},{14,0},{1,3},{3,5},... | collective-permute-start | bytes 786440 | tf_op jit(solution)/shard_map/ppermute | solution.py:25
  46.1 12.1 %collective-permute-start.6 = (bf16[2,256,256]{2,1,0:T(8,128)(2,1)S(1)}, bf16[2,256,256]{2,1,0:T(8,128)(2,1)S(1)}, u32[]{:S(2)}, u32[]{:S(2)}) collective-permute-start(bf16[2,256,256]{2,1,0:T(8,128)(2,1)S(1)} %collective-permute-done.4.refs_2_), channel_id=1, source_target_pairs={{0,14},{2,0},{4,2},{6,4},{8,6},{10,8},{12,10},{14,12},{1,15},{3,1}... | collective-permute-start | bytes 786440 | tf_op jit(solution)/shard_map/ppermute | solution.py:25
  49.6 11.7 %collective-permute-start.13 = (bf16[2,256,256]{2,1,0:T(8,128)(2,1)S(1)}, bf16[2,256,256]{2,1,0:T(8,128)(2,1)S(1)}, u32[]{:S(2)}, u32[]{:S(2)}) collective-permute-start(bf16[2,256,256]{2,1,0:T(8,128)(2,1)S(1)} %pad_maximum_fusion.1.refs_0_), channel_id=1, source_target_pairs={{0,14},{2,0},{4,2},{6,4},{8,6},{10,8},{12,10},{14,12},{1,15},{3,1}... | collective-permute-start | bytes 786440 | tf_op jit(solution)/shard_map/ppermute | solution.py:25
  52.6 12.2 %collective-permute-start.14 = (bf16[2,256,256]{2,1,0:T(8,128)(2,1)S(1)}, bf16[2,256,256]{2,1,0:T(8,128)(2,1)S(1)}, u32[]{:S(2)}, u32[]{:S(2)}) collective-permute-start(bf16[2,256,256]{2,1,0:T(8,128)(2,1)S(1)} %collective-permute-done.12.refs_1_), channel_id=1, source_target_pairs={{0,2},{2,4},{4,6},{6,8},{8,10},{10,12},{12,14},{14,0},{1,3},{3,5},... | collective-permute-start | bytes 786440 | tf_op jit(solution)/shard_map/ppermute | solution.py:25
  58.2 9.7 %collective-permute-start.5 = (bf16[2,256,256]{2,1,0:T(8,128)(2,1)S(1)}, bf16[2,256,256]{2,1,0:T(8,128)(2,1)S(1)}, u32[]{:S(2)}, u32[]{:S(2)}) collective-permute-start(bf16[2,256,256]{2,1,0:T(8,128)(2,1)S(1)} %collective-permute-done.3.refs_1_), channel_id=1, source_target_pairs={{0,2},{2,4},{4,6},{6,8},{8,10},{10,12},{12,14},{14,0},{1,3},{3,5},... | collective-permute-start | bytes 786440 | tf_op jit(solution)/shard_map/ppermute | solution.py:25
  58.3 9.7 %collective-permute-start.8 = (bf16[2,256,256]{2,1,0:T(8,128)(2,1)S(1)}, bf16[2,256,256]{2,1,0:T(8,128)(2,1)S(1)}, u32[]{:S(2)}, u32[]{:S(2)}) collective-permute-start(bf16[2,256,256]{2,1,0:T(8,128)(2,1)S(1)} %collective-permute-done.6.refs_4_), channel_id=1, source_target_pairs={{0,14},{2,0},{4,2},{6,4},{8,6},{10,8},{12,10},{14,12},{1,15},{3,1}... | collective-permute-start | bytes 786440 | tf_op jit(solution)/shard_map/ppermute | solution.py:25
  61.3 11.2 %collective-permute-start.15 = (bf16[2,256,256]{2,1,0:T(8,128)(2,1)S(1)}, bf16[2,256,256]{2,1,0:T(8,128)(2,1)}, u32[]{:S(2)}, u32[]{:S(2)}) collective-permute-start(bf16[2,256,256]{2,1,0:T(8,128)(2,1)S(1)} %collective-permute-done.13.refs_2_), channel_id=1, source_target_pairs={{0,14},{2,0},{4,2},{6,4},{8,6},{10,8},{12,10},{14,12},{1,15},{3,1}... | collective-permute-start | bytes 786440 | tf_op jit(solution)/shard_map/ppermute | solution.py:25
  64.8 11.2 %collective-permute-start.16 = (bf16[2,256,256]{2,1,0:T(8,128)(2,1)S(1)}, bf16[2,256,256]{2,1,0:T(8,128)(2,1)}, u32[]{:S(2)}, u32[]{:S(2)}) collective-permute-start(bf16[2,256,256]{2,1,0:T(8,128)(2,1)S(1)} %collective-permute-done.14.refs_3_), channel_id=1, source_target_pairs={{0,2},{2,4},{4,6},{6,8},{8,10},{10,12},{12,14},{14,0},{1,3},{3,5},... | collective-permute-start | bytes 786440 | tf_op jit(solution)/shard_map/ppermute | solution.py:25
  67.9 11.0 %collective-permute-start.7 = (bf16[2,256,256]{2,1,0:T(8,128)(2,1)S(1)}, bf16[2,256,256]{2,1,0:T(8,128)(2,1)S(1)}, u32[]{:S(2)}, u32[]{:S(2)}) collective-permute-start(bf16[2,256,256]{2,1,0:T(8,128)(2,1)S(1)} %collective-permute-done.5.refs_3_), channel_id=1, source_target_pairs={{0,2},{2,4},{4,6},{6,8},{8,10},{10,12},{12,14},{14,0},{1,3},{3,5},... | collective-permute-start | bytes 786440 | tf_op jit(solution)/shard_map/ppermute | solution.py:25
  68.0 11.0 %collective-permute-start.9 = (bf16[2,256,256]{2,1,0:T(8,128)(2,1)S(1)}, bf16[2,256,256]{2,1,0:T(8,128)(2,1)S(1)}, u32[]{:S(2)}, u32[]{:S(2)}) collective-permute-start(bf16[2,256,256]{2,1,0:T(8,128)(2,1)S(1)} %collective-permute-done.8.refs_6_), channel_id=1, source_target_pairs={{0,14},{2,0},{4,2},{6,4},{8,6},{10,8},{12,10},{14,12},{1,15},{3,1}... | collective-permute-start | bytes 786440 | tf_op jit(solution)/shard_map/ppermute | solution.py:25
  72.5 14.4 %collective-permute-start.17 = (bf16[2,256,256]{2,1,0:T(8,128)(2,1)}, bf16[2,256,256]{2,1,0:T(8,128)(2,1)}, u32[]{:S(2)}, u32[]{:S(2)}) collective-permute-start(bf16[2,256,256]{2,1,0:T(8,128)(2,1)} %collective-permute-done.15.refs_4_), channel_id=1, source_target_pairs={{0,14},{2,0},{4,2},{6,4},{8,6},{10,8},{12,10},{14,12},{1,15},{3,1}... | collective-permute-start | bytes 786440 | tf_op jit(solution)/shard_map/ppermute | solution.py:25
  76.1 10.9 %collective-permute-start.18 = (bf16[2,256,256]{2,1,0:T(8,128)(2,1)}, bf16[2,256,256]{2,1,0:T(8,128)(2,1)}, u32[]{:S(2)}, u32[]{:S(2)}) collective-permute-start(bf16[2,256,256]{2,1,0:T(8,128)(2,1)} %collective-permute-done.16.refs_5_), channel_id=1, source_target_pairs={{0,2},{2,4},{4,6},{6,8},{8,10},{10,12},{12,14},{14,0},{1,3},{3,5},... | collective-permute-start | bytes 786440 | tf_op jit(solution)/shard_map/ppermute | solution.py:25
  86.2 6.3 %collective-permute-start.20 = (bf16[2,512,128]{2,1,0:T(8,128)(2,1)}, bf16[2,512,128]{2,1,0:T(8,128)(2,1)S(1)}, u32[]{:S(2)}, u32[]{:S(2)}) collective-permute-start(bf16[2,512,128]{2,1,0:T(8,128)(2,1)} %get-tuple-element.33), channel_id=1, source_target_pairs={{0,1},{1,0},{2,3},{3,2},{4,5},{5,4},{6,7},{7,6},{8,9},{9,8},{10,11... | collective-permute-start | bytes 786440 | tf_op jit(solution)/shard_map/ppermute | solution.py:25
  92.6 6.3 %collective-permute-start.22 = (bf16[512,128]{1,0:T(8,128)(2,1)S(1)}, bf16[512,128]{1,0:T(8,128)(2,1)S(1)}, u32[]{:S(2)}, u32[]{:S(2)}) collective-permute-start(bf16[512,128]{1,0:T(8,128)(2,1)S(1)} %get-tuple-element.51), channel_id=1, source_target_pairs={{0,128},{128,0},{1,129},{129,1},{2,130},{130,2},{3,131},{131,3},{4... | collective-permute-start | bytes 393224 | tf_op jit(solution)/shard_map/ppermute | solution.py:25
  96.5 6.0 %collective-permute-start.21 = (bf16[512,128]{1,0:T(8,128)(2,1)S(1)}, bf16[512,128]{1,0:T(8,128)(2,1)S(1)}, u32[]{:S(2)}, u32[]{:S(2)}) collective-permute-start(bf16[512,128]{1,0:T(8,128)(2,1)S(1)} %get-tuple-element.53), channel_id=1, source_target_pairs={{0,128},{128,0},{1,129},{129,1},{2,130},{130,2},{3,131},{131,3},{4... | collective-permute-start | bytes 393224 | tf_op jit(solution)/shard_map/ppermute | solution.py:25
  105.8 7.9 %collective-permute-start.23 = (bf16[2,512,128]{2,1,0:T(8,128)(2,1)S(1)}, bf16[2,512,128]{2,1,0:T(8,128)(2,1)S(1)}, u32[]{:S(2)}, u32[]{:S(2)}) collective-permute-start(bf16[2,512,128]{2,1,0:T(8,128)(2,1)S(1)} %get-tuple-element.35), channel_id=1, source_target_pairs={{0,128},{128,0},{1,129},{129,1},{2,130},{130,2},{3,131},{131,3},{4... | collective-permute-start | bytes 786440 | tf_op jit(solution)/shard_map/ppermute | solution.py:25
  108.2 7.9 %collective-permute-start.24 = (bf16[2,512,128]{2,1,0:T(8,128)(2,1)S(1)}, bf16[2,512,128]{2,1,0:T(8,128)(2,1)S(1)}, u32[]{:S(2)}, u32[]{:S(2)}) collective-permute-start(bf16[2,512,128]{2,1,0:T(8,128)(2,1)S(1)} %get-tuple-element.34.refs_0_), channel_id=1, source_target_pairs={{0,1},{1,0},{2,3},{3,2},{4,5},{5,4},{6,7},{7,6},{8,9},{9,8},{10,11... | collective-permute-start | bytes 786440 | tf_op jit(solution)/shard_map/ppermute | solution.py:25
  113.7 3.6 %collective-permute-start.25 = (bf16[2,512,128]{2,1,0:T(8,128)(2,1)S(1)}, bf16[2,512,128]{2,1,0:T(8,128)(2,1)S(1)}, u32[]{:S(2)}, u32[]{:S(2)}) collective-permute-start(bf16[2,512,128]{2,1,0:T(8,128)(2,1)S(1)} %collective-permute-done.23.refs_1_), channel_id=1, source_target_pairs={{0,1},{1,0},{2,3},{3,2},{4,5},{5,4},{6,7},{7,6},{8,9},{9,8},{10,11... | collective-permute-start | bytes 786440 | tf_op jit(solution)/shard_map/ppermute | solution.py:25
  121.7 8.2 %collective-permute-start.30 = (bf16[64,2048]{1,0:T(8,128)(2,1)S(1)}, bf16[64,2048]{1,0:T(8,128)(2,1)S(1)}, u32[]{:S(2)}, u32[]{:S(2)}) collective-permute-start(bf16[64,2048]{1,0:T(8,128)(2,1)S(1)} %get-tuple-element.46), channel_id=1, source_target_pairs={{0,48},{16,0},{32,16},{48,32},{1,49},{17,1},{33,17},{49,33},{2,50}... | collective-permute-start | bytes 786440 | tf_op jit(solution)/shard_map/ppermute | solution.py:25
  122.7 8.8 %collective-permute-start.26 = (bf16[64,2048]{1,0:T(8,128)(2,1)S(1)}, bf16[64,2048]{1,0:T(8,128)(2,1)S(1)}, u32[]{:S(2)}, u32[]{:S(2)}) collective-permute-start(bf16[64,2048]{1,0:T(8,128)(2,1)S(1)} %get-tuple-element.42), channel_id=1, source_target_pairs={{0,16},{16,32},{32,48},{48,0},{1,17},{17,33},{33,49},{49,1},{2,18}... | collective-permute-start | bytes 786440 | tf_op jit(solution)/shard_map/ppermute | solution.py:25
  127.3 9.8 %collective-permute-start.28 = (bf16[64,2048]{1,0:T(8,128)(2,1)}, bf16[64,2048]{1,0:T(8,128)(2,1)S(1)}, u32[]{:S(2)}, u32[]{:S(2)}) collective-permute-start(bf16[64,2048]{1,0:T(8,128)(2,1)} %get-tuple-element.43), channel_id=1, source_target_pairs={{0,16},{16,32},{32,48},{48,0},{1,17},{17,33},{33,49},{49,1},{2,18}... | collective-permute-start | bytes 786440 | tf_op jit(solution)/shard_map/ppermute | solution.py:25
  127.9 9.2 %collective-permute-start.29 = (bf16[64,2048]{1,0:T(8,128)(2,1)S(1)}, bf16[64,2048]{1,0:T(8,128)(2,1)S(1)}, u32[]{:S(2)}, u32[]{:S(2)}) collective-permute-start(bf16[64,2048]{1,0:T(8,128)(2,1)S(1)} %get-tuple-element.44), channel_id=1, source_target_pairs={{0,48},{16,0},{32,16},{48,32},{1,49},{17,1},{33,17},{49,33},{2,50}... | collective-permute-start | bytes 786440 | tf_op jit(solution)/shard_map/ppermute | solution.py:25
  130.0 10.1 %collective-permute-start.31 = (bf16[64,2048]{1,0:T(8,128)(2,1)S(1)}, bf16[64,2048]{1,0:T(8,128)(2,1)S(1)}, u32[]{:S(2)}, u32[]{:S(2)}) collective-permute-start(bf16[64,2048]{1,0:T(8,128)(2,1)S(1)} %add_convert_fusion), channel_id=1, source_target_pairs={{0,48},{16,0},{32,16},{48,32},{1,49},{17,1},{33,17},{49,33},{2,50}... | collective-permute-start | bytes 786440 | tf_op jit(solution)/shard_map/ppermute | solution.py:25
  131.6 11.1 %collective-permute-start.27 = (bf16[64,2048]{1,0:T(8,128)(2,1)S(1)}, bf16[64,2048]{1,0:T(8,128)(2,1)S(1)}, u32[]{:S(2)}, u32[]{:S(2)}) collective-permute-start(bf16[64,2048]{1,0:T(8,128)(2,1)S(1)} %add_convert_fusion.1), channel_id=1, source_target_pairs={{0,16},{16,32},{32,48},{48,0},{1,17},{17,33},{33,49},{49,1},{2,18}... | collective-permute-start | bytes 786440 | tf_op jit(solution)/shard_map/ppermute | solution.py:25
  (33 other events, 511.6 us)
Sparse Core Ops, SparseCore 0:
  25.2 55.5 all-gather.2
